TPU v7x, 512 devices: a whole 4x4x16 slice. The times are simulated.
512 devices in a mesh: row: 4 (over x), col: 16 (over z), depth: 8 (over y, core).
Axes of the slice: x: 4, y: 4, z: 16, core: 2. Of those that a mesh axis runs over, the one named last changes fastest.
Arguments:
- inputs: bfloat16 [4096, 2560], P('depth', ('row', 'col')), may hold values from -6 to 6
- w_in: bfloat16 [2560, 10240], P('row', 'col'), may hold values from -0.15625 to 0.15625
- w_out: bfloat16 [10240, 2560], P('col', 'row'), may hold values from -0.078125 to 0.078125
- y_cot: bfloat16 [4096, 2560], P('depth', ('row', 'col')), may hold values from -0.75 to 0.75
Outputs:
- y_out: bfloat16 [4096, 2560], P('depth', ('row', 'col'))
- x_grad: bfloat16 [4096, 2560], P('depth', ('row', 'col'))
- w_in_grad: bfloat16 [2560, 10240], P('row', 'col')
- w_out_grad: bfloat16 [10240, 2560], P('col', 'row')
All inputs are finite; a program needn't handle non-finite values.
Results may differ from a plain program's by a relative error of at most 0.029.
Values may be sent and summed in bfloat16 or wider, within the bound.
No kernel may reach another device: no remote copies, remote signals or barrier semaphores. Data moves between devices by JAX's collectives and lax.ppermute only.
A program may use at most 64 MiB of HBM per device.

v0:
```python
import jax
import jax.numpy as jnp
from jax import lax
from jax.sharding import PartitionSpec as P

gelu_c = 0.7978845608
gelu_a = 0.044715


def gelu_value(h):
    t = jnp.tanh(gelu_c * (h + gelu_a * h * h * h))
    return 0.5 * h * (1.0 + t)


def gelu_slope(h):
    t = jnp.tanh(gelu_c * (h + gelu_a * h * h * h))
    return 0.5 * (1.0 + t) + 0.5 * h * (1.0 - t * t) * gelu_c * (1.0 + 3.0 * gelu_a * h * h)


def per_device(inputs, w_in, w_out, y_cot):
    x_rows = lax.all_gather(inputs, "col", axis=1, tiled=True)
    cot_rows = lax.all_gather(y_cot, "col", axis=1, tiled=True)
    block = x_rows
    hidden = lax.psum_scatter(
        jnp.dot(block, w_in, preferred_element_type=jnp.float32).astype(jnp.bfloat16),
        "row",
        scatter_dimension=0,
        tiled=True,
    ).astype(jnp.float32)
    act_share = gelu_value(hidden).astype(jnp.bfloat16)
    act_rows = lax.all_gather(act_share, "row", axis=0, tiled=True)
    out_terms = jnp.dot(act_rows, w_out, preferred_element_type=jnp.float32)
    y_out = lax.psum_scatter(out_terms.astype(jnp.bfloat16), "col", scatter_dimension=1, tiled=True)
    block = cot_rows
    act_grad = lax.psum_scatter(
        jnp.einsum("td,fd->tf", block, w_out, preferred_element_type=jnp.float32).astype(
            jnp.bfloat16
        ),
        "row",
        scatter_dimension=0,
        tiled=True,
    ).astype(jnp.float32)
    grad_share = (act_grad * gelu_slope(hidden)).astype(jnp.bfloat16)
    grad_rows = lax.all_gather(grad_share, "row", axis=0, tiled=True)
    input_terms = jnp.einsum("tf,df->td", grad_rows, w_in, preferred_element_type=jnp.float32)
    x_grad = lax.psum_scatter(
        input_terms.astype(jnp.bfloat16), "col", scatter_dimension=1, tiled=True
    )
    w_in_term = jnp.einsum("td,tf->df", x_rows, grad_rows, preferred_element_type=jnp.float32)
    w_out_term = jnp.einsum("tf,td->fd", act_rows, cot_rows, preferred_element_type=jnp.float32)
    w_in_sum, w_out_sum = (
        lax.psum(w_in_term.astype(jnp.bfloat16), "depth").astype(jnp.float32),
        lax.psum(w_out_term.astype(jnp.bfloat16), "depth").astype(jnp.float32),
    )
    return (y_out, x_grad, w_in_sum.astype(jnp.bfloat16), w_out_sum.astype(jnp.bfloat16))


def solution(mesh):
    in_specs = (
        P("depth", ("row", "col")),
        P("row", "col"),
        P("col", "row"),
        P("depth", ("row", "col")),
    )
    out_specs = (
        P("depth", ("row", "col")),
        P("depth", ("row", "col")),
        P("row", "col"),
        P("col", "row"),
    )
    return jax.shard_map(
        per_device, mesh=mesh, in_specs=in_specs, out_specs=out_specs, check_vma=False
    )
```

profile of v0, /device:TPU:24, one launch (start us, length us, event | category | flops | bytes accessed | tf_op | source)
XLA Modules:
  0.0 369.3 jit_solution(15094468329962635623)
XLA Ops:
  7.2 0.0 reduce-scatter.9.cloned.1.call-start
  7.2 40.0 %all_gather.14 = bf16[512,640]{0,1:T(8,128)(2,1)S(1)} all-gather(bf16[512,40]{0,1:T(8,128)(2,1)} %param.7), channel_id=1, replica_groups=mesh['row'=4,'col'=16,'depth'=8] {'col'}, dimensions={1}, use_global_device_ids=true | all-gather | bytes 696320 | tf_op jit(solution)/shard_map/all_gather | solution.py:22
  47.2 2.8 convolution_convert_fusion.3
  50.0 0.0 reduce-scatter.9.cloned.1.call-update
  50.1 0.0 reduce-scatter.5.cloned.1.call-start
  50.1 30.2 %all_gather.12 = bf16[512,640]{0,1:T(8,128)(2,1)S(1)} all-gather(bf16[512,40]{0,1:T(8,128)(2,1)S(1)} %copy-done.2), channel_id=1, replica_groups=mesh['row'=4,'col'=16,'depth'=8] {'col'}, dimensions={1}, use_global_device_ids=true | all-gather | bytes 696320 | tf_op jit(solution)/shard_map/all_gather | solution.py:21
  80.3 1.6 convolution_convert_fusion.5
  82.0 0.0 all-reduce.3.cloned.1.call-start
  82.0 0.0 reduce-scatter.9.cloned.1.call-done
  82.0 25.6 %reduce-scatter.5.cloned.1.call-done = bf16[128,640]{1,0:T(8,128)(2,1)} async-done(((bf16[512,640]{1,0:T(8,128)(2,1)}), bf16[128,640]{1,0:T(8,128)(2,1)}) %reduce-scatter.5.cloned.1.call-update) | async-done | bytes 163856 | tf_op jit(solution)/shard_map/reduce_scatter | solution.py:24
  107.6 1.2 fusion.8
  108.9 13.3 %all_gather.15 = bf16[512,640]{1,0:T(8,128)(2,1)S(1)} all-gather(bf16[128,640]{1,0:T(8,128)(2,1)S(1)} %get-tuple-element.10), channel_id=1, replica_groups=mesh['row'=4,'col'=16,'depth'=8] {'row'}, dimensions={0}, use_global_device_ids=true | all-gather | bytes 819200 | tf_op jit(solution)/shard_map/all_gather | solution.py:44
  122.2 1.6 fusion
  123.8 13.8 %all_gather.13 = bf16[512,640]{1,0:T(8,128)(2,1)S(1)} all-gather(bf16[128,640]{1,0:T(8,128)(2,1)S(1)} %get-tuple-element.11), channel_id=1, replica_groups=mesh['row'=4,'col'=16,'depth'=8] {'row'}, dimensions={0}, use_global_device_ids=true | all-gather | bytes 819200 | tf_op jit(solution)/shard_map/all_gather | solution.py:31
  137.6 1.6 convolution_convert_fusion
  139.2 0.0 reduce-scatter.11.cloned.1.call-start
  139.3 1.5 convolution_convert_fusion.2
  140.8 0.0 reduce-scatter.7.cloned.1.call-start
  140.9 2.7 convolution_convert_fusion.4
  143.6 72.7 %all-reduce.3.cloned.1.call-done = (bf16[640,640]{0,1:T(8,128)(2,1)}, bf16[640,640]{1,0:T(8,128)(2,1)}) async-done(((bf16[640,640]{0,1:T(8,128)(2,1)}, bf16[640,640]{1,0:T(8,128)(2,1)}), (bf16[640,640]{0,1:T(8,128)(2,1)}, bf16[640,640]{1,0:T(8,128)(2,1)})) %all-reduce.3.cloned.1.call-update) | async-done | bytes 1638416 | tf_op jit(solution)/shard_map/psum | solution.py:52
  216.4 2.3 copy.8
  218.6 72.4 %reduce-scatter.11.cloned.1.call-done = bf16[512,40]{0,1:T(8,128)(2,1)} async-done(((bf16[512,640]{0,1:T(8,128)(2,1)}), bf16[512,40]{0,1:T(8,128)(2,1)}) %reduce-scatter.11.cloned.1.call-update) | async-done | bytes 40976 | tf_op jit(solution)/shard_map/reduce_scatter | solution.py:46
  291.0 70.8 %reduce-scatter.7.cloned.1.call-done = bf16[512,40]{0,1:T(8,128)(2,1)} async-done(((bf16[512,640]{0,1:T(8,128)(2,1)}), bf16[512,40]{0,1:T(8,128)(2,1)}) %reduce-scatter.7.cloned.1.call-update) | async-done | bytes 40976 | tf_op jit(solution)/shard_map/reduce_scatter | solution.py:33
  361.9 0.9 copy.11
  (10 shorter events, 0.1 us)
Async XLA Ops:
  7.2 73.2 %copy-start = (bf16[640,640]{1,0:T(8,128)(2,1)S(1)}, bf16[640,640]{1,0:T(8,128)(2,1)}, u32[]{:S(2)}) copy-start(bf16[640,640]{1,0:T(8,128)(2,1)} %param.5) | copy-start | bytes 2457604
  7.2 74.9 %reduce-scatter.9.cloned.1.call-start = ((), (), s32[]{:S(2)}) async-start(), calls=%async_computation.6 | async-start | bytes 819200 | tf_op jit(solution)/shard_map/reduce_scatter | solution.py:35
  47.2 2.9 copy-start.2
  50.1 57.6 %reduce-scatter.5.cloned.1.call-start = ((), (), s32[]{:S(2)}) async-start(), calls=%async_computation.4 | async-start | bytes 819200 | tf_op jit(solution)/shard_map/reduce_scatter | solution.py:24
  82.0 134.4 %all-reduce.3.cloned.1.call-start = ((), (), s32[]{:S(2)}) async-start(), calls=%async_computation.8 | async-start | bytes 3276800 | tf_op jit(solution)/shard_map/psum | solution.py:52
  139.2 151.8 %reduce-scatter.11.cloned.1.call-start = ((), (), s32[]{:S(2)}) async-start(), calls=%async_computation.7 | async-start | bytes 696320 | tf_op jit(solution)/shard_map/reduce_scatter | solution.py:46
  140.8 221.0 %reduce-scatter.7.cloned.1.call-start = ((), (), s32[]{:S(2)}) async-start(), calls=%async_computation.5 | async-start | bytes 696320 | tf_op jit(solution)/shard_map/reduce_scatter | solution.py:33
  216.4 145.5 %copy-start.1 = (bf16[640,640]{1,0:T(8,128)(2,1)S(1)}, bf16[640,640]{1,0:T(8,128)(2,1)}, u32[]{:S(2)}) copy-start(bf16[640,640]{1,0:T(8,128)(2,1)} %get-tuple-element.15) | copy-start | bytes 2457604
Sparse Core Ops, SparseCore 0:
  50.2 24.7 reduce-scatter.8
  82.1 25.4 reduce-scatter.4
  139.3 76.9 all-reduce.2
  219.6 71.3 reduce-scatter.10
  294.5 67.3 reduce-scatter.6
where the time goes:
time: 370 us; the launch traced here: 369 us
  waiting for transfers between devices  242 us (65%)
  blocking collectives  97.3 us (26%)
  between operations  13.8 us (4%)
  matrix products  11.9 us (3%)
    psum x1, waiting for transfers between devices, per_device(): lax.psum(w_in_term.astype(jnp.bfloat16), 'depth').astype(jnp.float32)  72.7 us
    reduce_scatter x1, waiting for transfers between devices, per_device(): lax.psum_scatter(input_terms.astype(jnp.bfloat16), 'col', scatter_dimensi...  72.4 us
    reduce_scatter x1, waiting for transfers between devices, per_device(): lax.psum_scatter(out_terms.astype(jnp.bfloat16), 'col', scatter_dimension...  70.8 us
    all_gather x1, blocking collectives, per_device(): cot_rows = lax.all_gather(y_cot, 'col', axis=1, tiled=True)  40 us
    all_gather x1, blocking collectives, per_device(): x_rows = lax.all_gather(inputs, 'col', axis=1, tiled=True)  30.2 us
    reduce_scatter x1, waiting for transfers between devices, per_device(): lax.psum_scatter(jnp.dot(block, w_in, preferred_element_type=jnp.float32)...  25.6 us
    all_gather x1, blocking collectives, per_device(): act_rows = lax.all_gather(act_share, 'row', axis=0, tiled=True)  13.8 us
    all_gather x1, blocking collectives, per_device(): grad_rows = lax.all_gather(grad_share, 'row', axis=0, tiled=True)  13.3 us
  transfers between devices with their start and end apart: 5, of which 4 were waited for; matrix products, arithmetic and copies ran while one was open for 2% of the time, Pallas kernels for 0%

commit v1 on v0

v1 whole, which is shorter than its diff:
```python
import jax
import jax.numpy as jnp
from jax import lax
from jax.sharding import PartitionSpec as P

gelu_c = 0.7978845608
gelu_a = 0.044715


def gelu_pair(h):
    t = jnp.tanh(gelu_c * (h + gelu_a * h * h * h))
    value = 0.5 * h * (1.0 + t)
    slope = 0.5 * (1.0 + t) + 0.5 * h * (1.0 - t * t) * gelu_c * (1.0 + 3.0 * gelu_a * h * h)
    return value, slope


def scatter_sum(terms, axis, count):
    blocks = terms.astype(jnp.bfloat16).reshape((count, -1) + terms.shape[1:])
    got = lax.all_to_all(blocks, axis, 0, 0, tiled=True)
    return jnp.sum(got.astype(jnp.float32), axis=0)


def dot(a, b, spec):
    return jnp.einsum(spec, a, b, preferred_element_type=jnp.float32)


def per_device(inputs, w_in, w_out, y_cot):
    n_row, n_col = 4, 16
    x_t = lax.all_gather(inputs.T, "col", axis=0, tiled=True)
    cot_t = lax.all_gather(y_cot.T, "col", axis=0, tiled=True)
    hidden = scatter_sum(dot(x_t, w_in, "dt,df->tf"), "row", n_row)
    value, slope = gelu_pair(hidden)
    act_rows = lax.all_gather(value.astype(jnp.bfloat16), "row", axis=0, tiled=True)
    y_out = scatter_sum(dot(w_out, act_rows, "fd,tf->dt"), "col", n_col)
    act_grad = scatter_sum(dot(cot_t, w_out, "dt,fd->tf"), "row", n_row)
    grad_rows = lax.all_gather((act_grad * slope).astype(jnp.bfloat16), "row", axis=0, tiled=True)
    x_grad = scatter_sum(dot(w_in, grad_rows, "df,tf->dt"), "col", n_col)
    w_in_sum, w_out_sum = lax.psum(
        (
            dot(x_t, grad_rows, "dt,tf->df").astype(jnp.bfloat16),
            dot(act_rows, cot_t, "tf,dt->fd").astype(jnp.bfloat16),
        ),
        "depth",
    )
    return (y_out.astype(jnp.bfloat16).T, x_grad.astype(jnp.bfloat16).T, w_in_sum, w_out_sum)


def solution(mesh):
    in_specs = (
        P("depth", ("row", "col")),
        P("row", "col"),
        P("col", "row"),
        P("depth", ("row", "col")),
    )
    out_specs = (
        P("depth", ("row", "col")),
        P("depth", ("row", "col")),
        P("row", "col"),
        P("col", "row"),
    )
    return jax.shard_map(
        per_device, mesh=mesh, in_specs=in_specs, out_specs=out_specs, check_vma=False
    )
```

time: 370 us -> 258 us (0.70)
  waiting for transfers between devices: 242 us -> 93.9 us
  starting transfers between devices: 0.21 us -> 30.2 us
    reduce_scatter x4 -> x0, waiting for transfers between devices: 169 us -> none  [the longest x1 72.4 us: per_device(): lax.psum_scatter(input_terms.astype(jnp.bfloat16), 'col', scatter_dimensi...]
    all_to_all x0 -> x4, starting transfers between devices: none -> 30.2 us  [scatter_sum(): got = lax.all_to_all(blocks, axis, 0, 0, tiled=True)]
    all_to_all x0 -> x4, waiting for transfers between devices: none -> 17.8 us  [scatter_sum(): got = lax.all_to_all(blocks, axis, 0, 0, tiled=True)]
  transfers between devices with their start and end apart: 5 -> 5, of which waited for: 4 -> 3; matrix products, arithmetic and copies ran while one was open for 2% -> 5% of each run, Pallas kernels for 0% -> 0%
where the time goes in v1:
time: 258 us; the launch traced here: 255 us
  blocking collectives  97 us (38%)
  waiting for transfers between devices  93.9 us (36%)
  starting transfers between devices  30.2 us (12%)
  between operations  14.1 us (5%)
  matrix products  11.3 us (4%)
  local copies, waits for them, and re-layouts  6.38 us (2%)
    psum x1, waiting for transfers between devices, per_device(): lax.psum((dot(x_t, grad_rows, 'dt,tf->df').astype(jnp.bfloat16), dot(act_...  76.1 us
    all_gather x1, blocking collectives, per_device(): cot_t = lax.all_gather(y_cot.T, 'col', axis=0, tiled=True)  40 us
    all_to_all x4, starting transfers between devices, scatter_sum(): got = lax.all_to_all(blocks, axis, 0, 0, tiled=True)  30.2 us
    all_gather x1, blocking collectives, per_device(): x_t = lax.all_gather(inputs.T, 'col', axis=0, tiled=True)  29.8 us
    all_to_all x4, waiting for transfers between devices, scatter_sum(): got = lax.all_to_all(blocks, axis, 0, 0, tiled=True)  17.8 us
    all_gather x1, blocking collectives, per_device(): lax.all_gather((act_grad * slope).astype(jnp.bfloat16), 'row', axis=0, ti...  14 us
    all_gather x1, blocking collectives, per_device(): lax.all_gather(value.astype(jnp.bfloat16), 'row', axis=0, tiled=True)  13.2 us
    dot_general x6, matrix products, dot(): return jnp.einsum(spec, a, b, preferred_element_type=jnp.float32)  11.3 us
  transfers between devices with their start and end apart: 5, of which 3 were waited for; matrix products, arithmetic and copies ran while one was open for 5% of the time, Pallas kernels for 0%

profile of v1, /device:TPU:24, one launch (start us, length us, event | category | flops | bytes accessed | tf_op | source)
XLA Modules:
  0.0 254.7 jit_solution(15336404362137598576)
XLA Ops:
  7.2 40.0 %all_gather.14 = bf16[640,512]{1,0:T(8,128)(2,1)S(1)} all-gather(bf16[40,512]{1,0:T(8,128)(2,1)} %bitcast.29), channel_id=1, replica_groups=mesh['row'=4,'col'=16,'depth'=8] {'col'}, dimensions={0}, use_global_device_ids=true | all-gather | bytes 696320 | tf_op jit(solution)/shard_map/all_gather | solution.py:30
  47.2 2.8 %convolution_convert_fusion.3 = bf16[512,640]{1,0:T(8,128)(2,1)} fusion(bf16[640,512]{1,0:T(8,128)(2,1)S(1)} %all_gather.14, bf16[640,640]{1,0:T(8,128)(2,1)} %param.6), kind=kOutput, calls=%fused_computation.3 | convolution fusion | flops 419758080 | bytes 2129920 | tf_op jit(solution)/shard_map/dt,fd->tf/dot_general | solution.py:24
  50.0 4.4 %all-to-all-start.2 = ((bf16[4,128,640]{2,1,0:T(8,128)(2,1)}), bf16[4,128,640]{2,1,0:T(8,128)(2,1)S(1)}, u32[]{:S(2)}, u32[]{:S(2)}) async-start(bf16[4,128,640]{2,1,0:T(8,128)(2,1)} %bitcast.6), calls=%async_computation.2 | async-start | bytes 1310720 | tf_op jit(solution)/shard_map/all_to_all | solution.py:19
  54.4 29.8 %all_gather.12 = bf16[640,512]{1,0:T(8,128)(2,1)S(1)} all-gather(bf16[40,512]{1,0:T(8,128)(2,1)S(1)} %bitcast.30), channel_id=1, replica_groups=mesh['row'=4,'col'=16,'depth'=8] {'col'}, dimensions={0}, use_global_device_ids=true | all-gather | bytes 696320 | tf_op jit(solution)/shard_map/all_gather | solution.py:29
  84.2 1.6 convolution_convert_fusion.5
  85.8 5.0 %all-to-all-start = ((bf16[4,128,640]{2,1,0:T(8,128)(2,1)}), bf16[4,128,640]{2,1,0:T(8,128)(2,1)S(1)}, u32[]{:S(2)}, u32[]{:S(2)}) async-start(bf16[4,128,640]{2,1,0:T(8,128)(2,1)} %bitcast.26), calls=%async_computation | async-start | bytes 1310720 | tf_op jit(solution)/shard_map/all_to_all | solution.py:19
  90.9 8.7 %all-to-all-done = bf16[4,128,640]{2,1,0:T(8,128)(2,1)S(1)} async-done(((bf16[4,128,640]{2,1,0:T(8,128)(2,1)}), bf16[4,128,640]{2,1,0:T(8,128)(2,1)S(1)}, u32[]{:S(2)}, u32[]{:S(2)}) %all-to-all-start) | async-done | bytes 655392 | tf_op jit(solution)/shard_map/all_to_all | solution.py:19
  99.7 0.2 fusion.9
  99.9 14.0 %all_gather.15 = bf16[512,640]{1,0:T(8,128)(2,1)S(1)} all-gather(bf16[128,640]{1,0:T(8,128)(2,1)S(1)} %get-tuple-element.14), channel_id=1, replica_groups=mesh['row'=4,'col'=16,'depth'=8] {'row'}, dimensions={0}, use_global_device_ids=true | all-gather | bytes 819200 | tf_op jit(solution)/shard_map/all_gather | solution.py:36
  113.9 0.8 fusion.2
  114.7 1.1 copy.10
  115.8 6.9 %all-to-all-start.3 = ((bf16[16,40,512]{2,1,0:T(8,128)(2,1)}), bf16[16,40,512]{2,1,0:T(8,128)(2,1)S(1)}, u32[]{:S(2)}, u32[]{:S(2)}) async-start(bf16[16,40,512]{2,1,0:T(8,128)(2,1)} %bitcast.8), calls=%async_computation.3 | async-start | bytes 1310720 | tf_op jit(solution)/shard_map/all_to_all | solution.py:19
  122.7 13.2 %all_gather.13 = bf16[512,640]{1,0:T(8,128)(2,1)S(1)} all-gather(bf16[128,640]{1,0:T(8,128)(2,1)S(1)} %get-tuple-element.15), channel_id=1, replica_groups=mesh['row'=4,'col'=16,'depth'=8] {'row'}, dimensions={0}, use_global_device_ids=true | all-gather | bytes 819200 | tf_op jit(solution)/shard_map/all_gather | solution.py:33
  135.9 1.6 fusion.1
  137.5 2.2 copy.9
  139.7 9.1 %all-to-all-done.3 = bf16[16,40,512]{2,1,0:T(8,128)(2,1)S(1)} async-done(((bf16[16,40,512]{2,1,0:T(8,128)(2,1)}), bf16[16,40,512]{2,1,0:T(8,128)(2,1)S(1)}, u32[]{:S(2)}, u32[]{:S(2)}) %all-to-all-start.3) | async-done | bytes 655392 | tf_op jit(solution)/shard_map/all_to_all | solution.py:19
  148.8 13.9 %all-to-all-start.1 = ((bf16[16,40,512]{2,1,0:T(8,128)(2,1)}), bf16[16,40,512]{2,1,0:T(8,128)(2,1)S(1)}, u32[]{:S(2)}, u32[]{:S(2)}) async-start(bf16[16,40,512]{2,1,0:T(8,128)(2,1)} %bitcast.3), calls=%async_computation.1 | async-start | bytes 1310720 | tf_op jit(solution)/shard_map/all_to_all | solution.py:19
  162.7 3.0 %fusion = bf16[640,640]{0,1:T(8,128)(2,1)} fusion(bf16[512,640]{1,0:T(8,128)(2,1)} %copy-done.3, bf16[640,512]{1,0:T(8,128)(2,1)} %copy-done.2), kind=kOutput, calls=%fused_computation.8 | convolution fusion | flops 419840000 | bytes 2129920 | tf_op jit(solution)/shard_map/dt,tf->df/dot_general | solution.py:24
  165.7 1.6 convolution_convert_fusion
  167.3 76.1 %all-reduce.3.cloned.1.call-done = (bf16[640,640]{0,1:T(8,128)(2,1)}, bf16[640,640]{1,0:T(8,128)(2,1)}) async-done(((bf16[640,640]{0,1:T(8,128)(2,1)}, bf16[640,640]{1,0:T(8,128)(2,1)}), (bf16[640,640]{0,1:T(8,128)(2,1)}, bf16[640,640]{1,0:T(8,128)(2,1)})) %all-reduce.3.cloned.1.call-update) | async-done | bytes 1638416 | tf_op jit(solution)/shard_map/psum | solution.py:38
  243.4 2.2 copy.11
  245.6 0.7 reduce_sum.45
  246.3 0.7 reduce_sum.43
  247.0 0.9 copy.14
  (22 shorter events, 0.3 us)
Async XLA Ops:
  7.2 77.0 %copy-start = (bf16[640,640]{1,0:T(8,128)(2,1)S(1)}, bf16[640,640]{1,0:T(8,128)(2,1)}, u32[]{:S(2)}) copy-start(bf16[640,640]{1,0:T(8,128)(2,1)} %param.5) | copy-start | bytes 2457604
  50.0 4.4 %copy-start.6 = (bf16[512,40]{0,1:T(8,128)(2,1)S(1)}, bf16[512,40]{0,1:T(8,128)(2,1)}, u32[]{:S(2)}) copy-start(bf16[512,40]{0,1:T(8,128)(2,1)} %param.4) | copy-start | bytes 122884
  50.0 35.8 %all-to-all-start.2 = ((bf16[4,128,640]{2,1,0:T(8,128)(2,1)}), bf16[4,128,640]{2,1,0:T(8,128)(2,1)S(1)}, u32[]{:S(2)}, u32[]{:S(2)}) async-start(bf16[4,128,640]{2,1,0:T(8,128)(2,1)} %bitcast.6), calls=%async_computation.2 | async-start | bytes 1310720 | tf_op jit(solution)/shard_map/all_to_all | solution.py:19
  84.2 1.6 copy-start.2
  85.8 13.8 %all-to-all-start = ((bf16[4,128,640]{2,1,0:T(8,128)(2,1)}), bf16[4,128,640]{2,1,0:T(8,128)(2,1)S(1)}, u32[]{:S(2)}, u32[]{:S(2)}) async-start(bf16[4,128,640]{2,1,0:T(8,128)(2,1)} %bitcast.26), calls=%async_computation | async-start | bytes 1310720 | tf_op jit(solution)/shard_map/all_to_all | solution.py:19
  113.9 1.9 copy-start.3
  115.8 33.0 %all-to-all-start.3 = ((bf16[16,40,512]{2,1,0:T(8,128)(2,1)}), bf16[16,40,512]{2,1,0:T(8,128)(2,1)S(1)}, u32[]{:S(2)}, u32[]{:S(2)}) async-start(bf16[16,40,512]{2,1,0:T(8,128)(2,1)} %bitcast.8), calls=%async_computation.3 | async-start | bytes 1310720 | tf_op jit(solution)/shard_map/all_to_all | solution.py:19
  122.7 13.2 %copy-start.7 = (bf16[640,640]{1,0:T(8,128)(2,1)S(1)}, bf16[640,640]{1,0:T(8,128)(2,1)}, u32[]{:S(2)}) copy-start(bf16[640,640]{1,0:T(8,128)(2,1)} %param.6) | copy-start | bytes 2457604
  135.9 1.6 copy-start.4
  148.8 97.5 %all-to-all-start.1 = ((bf16[16,40,512]{2,1,0:T(8,128)(2,1)}), bf16[16,40,512]{2,1,0:T(8,128)(2,1)S(1)}, u32[]{:S(2)}, u32[]{:S(2)}) async-start(bf16[16,40,512]{2,1,0:T(8,128)(2,1)} %bitcast.3), calls=%async_computation.1 | async-start | bytes 1310720 | tf_op jit(solution)/shard_map/all_to_all | solution.py:19
  162.7 80.7 %all-reduce.3.cloned.1.call-start = ((), (), s32[]{:S(2)}) async-start(), calls=%async_computation.4 | async-start | bytes 3276800 | tf_op jit(solution)/shard_map/psum | solution.py:38
  162.7 3.0 %copy-start.5 = (bf16[512,640]{1,0:T(8,128)(2,1)S(1)}, bf16[512,640]{1,0:T(8,128)(2,1)}, u32[]{:S(2)}) copy-start(bf16[512,640]{1,0:T(8,128)(2,1)} %copy-done.4) | copy-start | bytes 1966084
  245.6 1.4 copy-start.1
Sparse Core Ops, SparseCore 0:
  167.4 75.8 all-reduce.2

commit v2 on v1

v2 whole, which is shorter than its diff:
```python
import jax
import jax.numpy as jnp
from jax import lax
from jax.sharding import PartitionSpec as P

gelu_c = 0.7978845608
gelu_a = 0.044715
bf16 = jnp.bfloat16
f32 = jnp.float32
n_row, n_col, n_chip = 4, 16, 4


def gelu_pair(h):
    t = jnp.tanh(gelu_c * (h + gelu_a * h * h * h))
    value = 0.5 * h * (1.0 + t)
    slope = 0.5 * (1.0 + t) + 0.5 * h * (1.0 - t * t) * gelu_c * (1.0 + 3.0 * gelu_a * h * h)
    return value, slope


def dot(a, b, spec):
    return jnp.einsum(spec, a, b, preferred_element_type=f32).astype(bf16)


def gather(block, axis):
    return lax.all_gather(block, axis, axis=0, tiled=True)


def scatter_sum(terms, axis, count):
    blocks = terms.reshape((count, -1) + terms.shape[1:])
    got = lax.all_to_all(blocks, axis, 0, 0, tiled=True)
    return jnp.sum(got.astype(f32), axis=0)


def scatter_sum_steps(terms, axis, count):
    blocks = terms.reshape((count, -1) + terms.shape[1:])
    me = lax.axis_index(axis)
    total = lax.dynamic_index_in_dim(blocks, me, 0, keepdims=False).astype(f32)
    for step in (2, 1, 3):
        block = lax.dynamic_index_in_dim(blocks, lax.rem(me + step, count), 0, keepdims=False)
        pairs = [(i, (i + step) % count) for i in range(count)]
        total = total + lax.ppermute(block, axis, pairs).astype(f32)
    return total


def core_half_sum(terms):
    me = lax.axis_index("core")
    halves = terms.reshape((2, -1) + terms.shape[1:])
    mine = lax.dynamic_index_in_dim(halves, me, 0, keepdims=False)
    other = lax.dynamic_index_in_dim(halves, 1 - me, 0, keepdims=False)
    got = lax.ppermute(other, "core", [(0, 1), (1, 0)])
    return (mine.astype(f32) + got.astype(f32)).astype(bf16)


def per_device(inputs, w_in, w_out, y_cot):
    cot_pad = jnp.pad(y_cot.T, ((0, 24), (0, 0)))
    cot_t = lax.all_gather(cot_pad, "col", axis=0)[:, :40].reshape(640, 512)
    x_t = gather(inputs.T, "col")
    hidden = scatter_sum(dot(x_t, w_in, "dt,df->tf"), "row", n_row)
    value, slope = gelu_pair(hidden)
    act_rows = gather(value.astype(bf16), "row")
    y_out = scatter_sum(dot(w_out, act_rows, "fd,tf->dt"), "col", n_col)
    cot_t, _ = lax.optimization_barrier((cot_t, act_rows))
    act_grad = scatter_sum_steps(dot(cot_t, w_out, "dt,fd->tf"), "row", n_row)
    grad_rows = gather((act_grad * slope).astype(bf16), "row")
    x_grad = scatter_sum(dot(w_in, grad_rows, "df,tf->dt"), "col", n_col)
    w_terms = jnp.concatenate(
        [dot(x_t, grad_rows, "dt,tf->df"), dot(act_rows, cot_t, "tf,dt->fd")], 0
    )
    w_terms = w_terms.reshape(2, 2, 320, 640).swapaxes(0, 1).reshape(1280, 640)
    half = core_half_sum(w_terms)
    quarter = scatter_sum_steps(half, "chip", n_chip).astype(bf16)
    half = gather(quarter, "chip")
    w_in_sum = gather(half[:320], "core")
    w_out_sum = gather(half[320:], "core")
    return (y_out.astype(bf16).T, x_grad.astype(bf16).T, w_in_sum, w_out_sum)


def solution(mesh):
    shape = mesh.devices.shape
    fine = jax.sharding.Mesh(
        mesh.devices.reshape(shape[0], shape[1], shape[2] // 2, 2), ("row", "col", "chip", "core")
    )
    depth = ("chip", "core")
    acts = P(depth, ("row", "col"))
    return jax.shard_map(
        per_device,
        mesh=fine,
        in_specs=(acts, P("row", "col"), P("col", "row"), acts),
        out_specs=(acts, acts, P("row", "col"), P("col", "row")),
        check_vma=False,
    )
```

time: 258 us -> 191 us (0.74)
  the two profiles are of different devices: /device:TPU:24 before, /device:TPU:1 now
where the time goes in v2:
time: 191 us; the launch traced here: 190 us
  blocking collectives  91.6 us (48%)
  starting transfers between devices  52.5 us (27%)
  between operations  14.3 us (7%)
  local copies, waits for them, and re-layouts  10.6 us (6%)
  waiting for transfers between devices  9.5 us (5%)
  matrix products  6.74 us (4%)
  other arithmetic  4.62 us (2%)
    all_gather x6, blocking collectives, gather(): return lax.all_gather(block, axis, axis=0, tiled=True)  78.6 us
    ppermute x1, starting transfers between devices, core_half_sum(): got = lax.ppermute(other, 'core', [(0, 1), (1, 0)])  22.2 us
    ppermute x6, starting transfers between devices, scatter_sum_steps(): total = total + lax.ppermute(block, axis, pairs).astype(f32)  19.8 us
    all_to_all x1, blocking collectives, scatter_sum(): got = lax.all_to_all(blocks, axis, 0, 0, tiled=True)  12.9 us
    all_to_all x2, starting transfers between devices, scatter_sum(): got = lax.all_to_all(blocks, axis, 0, 0, tiled=True)  10.5 us
    ppermute x6, waiting for transfers between devices, scatter_sum_steps(): total = total + lax.ppermute(block, axis, pairs).astype(f32)  9.46 us
    dot_general x6, matrix products, dot(): return jnp.einsum(spec, a, b, preferred_element_type=f32).astype(bf16)  6.74 us
  transfers between devices with their start and end apart: 10, of which 4 were waited for; matrix products, arithmetic and copies ran while one was open for 8% of the time, Pallas kernels for 0%

profile of v2, /device:TPU:1, one launch (start us, length us, event | category | flops | bytes accessed | tf_op | source)
XLA Modules:
  0.0 189.8 jit_solution(2186439814359269864)
XLA Ops:
  7.2 1.5 pad.4
  8.7 35.1 %all_gather.24 = bf16[640,512]{1,0:T(8,128)(2,1)S(1)} all-gather(bf16[40,512]{1,0:T(8,128)(2,1)} %bitcast.71), channel_id=1, replica_groups=mesh['row'=4,'col'=16,'chip'=4,'core'=2] {'col'}, dimensions={0}, use_global_device_ids=true | all-gather | bytes 696320 | tf_op jit(solution)/shard_map/all_gather | solution.py:25
  43.8 2.2 %convolution_convert_fusion.5 = bf16[512,640]{1,0:T(8,128)(2,1)S(1)} fusion(bf16[640,512]{1,0:T(8,128)(2,1)S(1)} %all_gather.24, bf16[640,640]{1,0:T(8,128)(2,1)} %param.5), kind=kOutput, calls=%fused_computation.8 | convolution fusion | flops 419758080 | bytes 2129920 | tf_op jit(solution)/shard_map/dt,df->tf/dot_general | solution.py:21
  46.0 12.9 %all_to_all.15 = bf16[4,128,640]{2,1,0:T(8,128)(2,1)S(1)} all-to-all(bf16[4,128,640]{2,1,0:T(8,128)(2,1)S(1)} %bitcast.64), channel_id=1, replica_groups=mesh['row'=4,'col'=16,'chip'=4,'core'=2] {'row'}, dimensions={0} | all-to-all | bytes 1310720 | tf_op jit(solution)/shard_map/all_to_all | solution.py:30
  59.2 11.1 %all_gather.25 = bf16[512,640]{1,0:T(8,128)(2,1)S(1)} all-gather(bf16[128,640]{1,0:T(8,128)(2,1)S(1)} %multiply_convert_fusion), channel_id=1, replica_groups=mesh['row'=4,'col'=16,'chip'=4,'core'=2] {'row'}, dimensions={0}, use_global_device_ids=true | all-gather | bytes 819200 | tf_op jit(solution)/shard_map/all_gather | solution.py:25
  72.9 4.4 %all-to-all-start.1 = ((bf16[16,40,512]{2,1,0:T(8,128)(2,1)}), bf16[16,40,512]{2,1,0:T(8,128)(2,1)S(1)}, u32[]{:S(2)}, u32[]{:S(2)}) async-start(bf16[16,40,512]{2,1,0:T(8,128)(2,1)} %bitcast.3), calls=%async_computation.1 | async-start | bytes 1310720 | tf_op jit(solution)/shard_map/all_to_all | solution.py:30
  79.4 4.4 %collective-permute-start = (bf16[128,640]{1,0:T(8,128)(2,1)S(1)}, bf16[128,640]{1,0:T(8,128)(2,1)S(1)}, u32[]{:S(2)}, u32[]{:S(2)}) collective-permute-start(bf16[128,640]{1,0:T(8,128)(2,1)S(1)} %get-tuple-element.11), channel_id=1, source_target_pairs={{0,256},{128,384},{256,0},{384,128},{1,257},{129,385},{257,1},{385... | collective-permute-start | bytes 491528 | tf_op jit(solution)/shard_map/ppermute | solution.py:41
  83.9 2.5 %collective-permute-start.2 = (bf16[128,640]{1,0:T(8,128)(2,1)S(1)}, bf16[128,640]{1,0:T(8,128)(2,1)S(1)}, u32[]{:S(2)}, u32[]{:S(2)}) collective-permute-start(bf16[128,640]{1,0:T(8,128)(2,1)S(1)} %get-tuple-element.12), channel_id=1, source_target_pairs={{0,384},{128,0},{256,128},{384,256},{1,385},{129,1},{257,129},{385... | collective-permute-start | bytes 491528 | tf_op jit(solution)/shard_map/ppermute | solution.py:41
  86.4 2.9 %collective-permute-start.1 = (bf16[128,640]{1,0:T(8,128)(2,1)S(1)}, bf16[128,640]{1,0:T(8,128)(2,1)S(1)}, u32[]{:S(2)}, u32[]{:S(2)}) collective-permute-start(bf16[128,640]{1,0:T(8,128)(2,1)S(1)} %get-tuple-element.13), channel_id=1, source_target_pairs={{0,128},{128,256},{256,384},{384,0},{1,129},{129,257},{257,385},{3... | collective-permute-start | bytes 491528 | tf_op jit(solution)/shard_map/ppermute | solution.py:41
  90.3 3.5 %collective-permute-done.1 = bf16[128,640]{1,0:T(8,128)(2,1)S(1)} collective-permute-done((bf16[128,640]{1,0:T(8,128)(2,1)S(1)}, bf16[128,640]{1,0:T(8,128)(2,1)S(1)}, u32[]{:S(2)}, u32[]{:S(2)}) %collective-permute-start.1) | collective-permute-done | bytes 163872 | tf_op jit(solution)/shard_map/ppermute | solution.py:41
  94.1 12.2 %all_gather.28 = bf16[512,640]{1,0:T(8,128)(2,1)S(1)} all-gather(bf16[128,640]{1,0:T(8,128)(2,1)S(1)} %fusion.13), channel_id=1, replica_groups=mesh['row'=4,'col'=16,'chip'=4,'core'=2] {'row'}, dimensions={0}, use_global_device_ids=true | all-gather | bytes 819200 | tf_op jit(solution)/shard_map/all_gather | solution.py:25
  108.3 22.2 %collective-permute-start.3 = (bf16[640,640]{1,0:T(8,128)(2,1)}, bf16[640,640]{1,0:T(8,128)(2,1)}, u32[]{:S(2)}, u32[]{:S(2)}) collective-permute-start(bf16[640,640]{1,0:T(8,128)(2,1)} %dynamic-slice_bitcast_fusion), channel_id=1, source_target_pairs={{0,1},{1,0},{2,3},{3,2},{4,5},{5,4},{6,7},{7,6},{8,9},{9,8},{10,11... | collective-permute-start | bytes 2457608 | tf_op jit(solution)/shard_map/ppermute | solution.py:50
  130.5 1.6 fusion.3
  132.2 2.2 %copy.9 = bf16[640,512]{1,0:T(8,128)(2,1)} copy(bf16[640,512]{0,1:T(8,128)(2,1)} %fusion.3) | data formatting | bytes 1310720 | tf_op jit(solution)/shard_map/convert_element_type | solution.py:21
  134.4 6.0 %all-to-all-start.2 = ((bf16[16,40,512]{2,1,0:T(8,128)(2,1)}), bf16[16,40,512]{2,1,0:T(8,128)(2,1)}, u32[]{:S(2)}, u32[]{:S(2)}) async-start(bf16[16,40,512]{2,1,0:T(8,128)(2,1)} %bitcast.61), calls=%async_computation.2 | async-start | bytes 1310720 | tf_op jit(solution)/shard_map/all_to_all | solution.py:30
  142.6 4.7 %collective-permute-start.4 = (bf16[160,640]{1,0:T(8,128)(2,1)}, bf16[160,640]{1,0:T(8,128)(2,1)S(1)}, u32[]{:S(2)}, u32[]{:S(2)}) collective-permute-start(bf16[160,640]{1,0:T(8,128)(2,1)} %get-tuple-element.8), channel_id=1, source_target_pairs={{0,4},{2,6},{4,0},{6,2},{1,5},{3,7},{5,1},{7,3},{8,12},{10,14},{12... | collective-permute-start | bytes 614408 | tf_op jit(solution)/shard_map/ppermute | solution.py:41
  147.2 2.8 %collective-permute-start.6 = (bf16[160,640]{1,0:T(8,128)(2,1)S(1)}, bf16[160,640]{1,0:T(8,128)(2,1)S(1)}, u32[]{:S(2)}, u32[]{:S(2)}) collective-permute-start(bf16[160,640]{1,0:T(8,128)(2,1)S(1)} %get-tuple-element.9), channel_id=1, source_target_pairs={{0,6},{2,0},{4,2},{6,4},{1,7},{3,1},{5,3},{7,5},{8,14},{10,8},{12,... | collective-permute-start | bytes 614408 | tf_op jit(solution)/shard_map/ppermute | solution.py:41
  150.0 2.5 %collective-permute-start.5 = (bf16[160,640]{1,0:T(8,128)(2,1)S(1)}, bf16[160,640]{1,0:T(8,128)(2,1)S(1)}, u32[]{:S(2)}, u32[]{:S(2)}) collective-permute-start(bf16[160,640]{1,0:T(8,128)(2,1)S(1)} %get-tuple-element.10), channel_id=1, source_target_pairs={{0,2},{2,4},{4,6},{6,0},{1,3},{3,5},{5,7},{7,1},{8,10},{10,12},{12... | collective-permute-start | bytes 614408 | tf_op jit(solution)/shard_map/ppermute | solution.py:41
  153.3 3.8 %collective-permute-done.6 = bf16[160,640]{1,0:T(8,128)(2,1)S(1)} collective-permute-done((bf16[160,640]{1,0:T(8,128)(2,1)S(1)}, bf16[160,640]{1,0:T(8,128)(2,1)S(1)}, u32[]{:S(2)}, u32[]{:S(2)}) %collective-permute-start.6) | collective-permute-done | bytes 204832 | tf_op jit(solution)/shard_map/ppermute | solution.py:41
  157.0 1.9 %collective-permute-done.5 = bf16[160,640]{1,0:T(8,128)(2,1)S(1)} collective-permute-done((bf16[160,640]{1,0:T(8,128)(2,1)S(1)}, bf16[160,640]{1,0:T(8,128)(2,1)S(1)}, u32[]{:S(2)}, u32[]{:S(2)}) %collective-permute-start.5) | collective-permute-done | bytes 204832 | tf_op jit(solution)/shard_map/ppermute | solution.py:41
  159.1 11.7 %all_gather.29 = bf16[640,640]{1,0:T(8,128)(2,1)S(1)} all-gather(bf16[160,640]{1,0:T(8,128)(2,1)S(1)} %fusion.6), channel_id=1, replica_groups=mesh['row'=4,'col'=16,'chip'=4,'core'=2] {'chip'}, dimensions={0}, use_global_device_ids=true | all-gather | bytes 1024000 | tf_op jit(solution)/shard_map/all_gather | solution.py:25
  170.9 6.2 %all_gather.31 = bf16[640,640]{1,0:T(8,128)(2,1)S(1)} all-gather(bf16[320,640]{1,0:T(8,128)(2,1)S(1)} %get-tuple-element.6), channel_id=1, replica_groups=mesh['row'=4,'col'=16,'chip'=4,'core'=2] {'core'}, dimensions={0}, use_global_device_ids=true | all-gather | bytes 1228800 | tf_op jit(solution)/shard_map/all_gather | solution.py:25
  177.0 2.4 %all_gather.30 = bf16[640,640]{1,0:T(8,128)(2,1)S(1)} all-gather(bf16[320,640]{1,0:T(8,128)(2,1)S(1)} %get-tuple-element.7), channel_id=1, replica_groups=mesh['row'=4,'col'=16,'chip'=4,'core'=2] {'core'}, dimensions={0}, use_global_device_ids=true | all-gather | bytes 1228800 | tf_op jit(solution)/shard_map/all_gather | solution.py:25
  179.4 1.8 reduce_sum.35
  (45 shorter events, 12.9 us)
Async XLA Ops:
  7.2 63.9 %copy-start = (bf16[640,640]{1,0:T(8,128)(2,1)S(1)}, bf16[640,640]{1,0:T(8,128)(2,1)}, u32[]{:S(2)}) copy-start(bf16[640,640]{1,0:T(8,128)(2,1)} %param.6) | copy-start | bytes 2457604
  7.2 70.2 %all-gather.3.cloned.1.call-start = ((), (), s32[]{:S(2)}) async-start(), calls=%async_computation.3 | async-start | bytes 1114112 | tf_op jit(solution)/shard_map/all_gather | solution.py:56
  43.8 2.2 %copy-start.3 = (bf16[640,512]{1,0:T(8,128)(2,1)}, bf16[640,512]{1,0:T(8,128)(2,1)S(1)}, u32[]{:S(2)}) copy-start(bf16[640,512]{1,0:T(8,128)(2,1)S(1)} %all_gather.24) | copy-start | bytes 1966084
  70.2 0.8 copy-start.5
  72.9 61.4 %all-to-all-start.1 = ((bf16[16,40,512]{2,1,0:T(8,128)(2,1)}), bf16[16,40,512]{2,1,0:T(8,128)(2,1)S(1)}, u32[]{:S(2)}, u32[]{:S(2)}) async-start(bf16[16,40,512]{2,1,0:T(8,128)(2,1)} %bitcast.3), calls=%async_computation.1 | async-start | bytes 1310720 | tf_op jit(solution)/shard_map/all_to_all | solution.py:30
  78.6 10.7 %copy-start.6 = (bf16[512,640]{1,0:T(8,128)(2,1)S(1)}, bf16[512,640]{1,0:T(8,128)(2,1)}, u32[]{:S(2)}) copy-start(bf16[512,640]{1,0:T(8,128)(2,1)} %copy-done.5) | copy-start | bytes 1966084
  79.4 10.6 %collective-permute-start = (bf16[128,640]{1,0:T(8,128)(2,1)S(1)}, bf16[128,640]{1,0:T(8,128)(2,1)S(1)}, u32[]{:S(2)}, u32[]{:S(2)}) collective-permute-start(bf16[128,640]{1,0:T(8,128)(2,1)S(1)} %get-tuple-element.11), channel_id=1, source_target_pairs={{0,256},{128,384},{256,0},{384,128},{1,257},{129,385},{257,1},{385... | collective-permute-start | bytes 491528 | tf_op jit(solution)/shard_map/ppermute | solution.py:41
  83.9 6.4 %collective-permute-start.2 = (bf16[128,640]{1,0:T(8,128)(2,1)S(1)}, bf16[128,640]{1,0:T(8,128)(2,1)S(1)}, u32[]{:S(2)}, u32[]{:S(2)}) collective-permute-start(bf16[128,640]{1,0:T(8,128)(2,1)S(1)} %get-tuple-element.12), channel_id=1, source_target_pairs={{0,384},{128,0},{256,128},{384,256},{1,385},{129,1},{257,129},{385... | collective-permute-start | bytes 491528 | tf_op jit(solution)/shard_map/ppermute | solution.py:41
  86.4 19.9 %copy-start.4 = (bf16[640,512]{1,0:T(8,128)(2,1)S(1)}, bf16[640,512]{1,0:T(8,128)(2,1)}, u32[]{:S(2)}) copy-start(bf16[640,512]{1,0:T(8,128)(2,1)} %copy-done.3) | copy-start | bytes 1966084
  86.4 7.4 %collective-permute-start.1 = (bf16[128,640]{1,0:T(8,128)(2,1)S(1)}, bf16[128,640]{1,0:T(8,128)(2,1)S(1)}, u32[]{:S(2)}, u32[]{:S(2)}) collective-permute-start(bf16[128,640]{1,0:T(8,128)(2,1)S(1)} %get-tuple-element.13), channel_id=1, source_target_pairs={{0,128},{128,256},{256,384},{384,0},{1,129},{129,257},{257,385},{3... | collective-permute-start | bytes 491528 | tf_op jit(solution)/shard_map/ppermute | solution.py:41
  107.3 23.2 %copy-start.7 = (bf16[640,640]{1,0:T(8,128)(2,1)S(1)}, bf16[640,640]{1,0:T(8,128)(2,1)}, u32[]{:S(2)}) copy-start(bf16[640,640]{1,0:T(8,128)(2,1)} %param.5) | copy-start | bytes 2457604
  108.3 32.2 %collective-permute-start.3 = (bf16[640,640]{1,0:T(8,128)(2,1)}, bf16[640,640]{1,0:T(8,128)(2,1)}, u32[]{:S(2)}, u32[]{:S(2)}) collective-permute-start(bf16[640,640]{1,0:T(8,128)(2,1)} %dynamic-slice_bitcast_fusion), channel_id=1, source_target_pairs={{0,1},{1,0},{2,3},{3,2},{4,5},{5,4},{6,7},{7,6},{8,9},{9,8},{10,11... | collective-permute-start | bytes 2457608 | tf_op jit(solution)/shard_map/ppermute | solution.py:50
  134.4 6.1 %copy-start.1 = (bf16[16,40,512]{2,1,0:T(8,128)(2,1)}, bf16[16,40,512]{2,1,0:T(8,128)(2,1)S(1)}, u32[]{:S(2)}) copy-start(bf16[16,40,512]{2,1,0:T(8,128)(2,1)S(1)} %all-to-all-done.1) | copy-start | bytes 1966084
  134.4 45.0 %all-to-all-start.2 = ((bf16[16,40,512]{2,1,0:T(8,128)(2,1)}), bf16[16,40,512]{2,1,0:T(8,128)(2,1)}, u32[]{:S(2)}, u32[]{:S(2)}) async-start(bf16[16,40,512]{2,1,0:T(8,128)(2,1)} %bitcast.61), calls=%async_computation.2 | async-start | bytes 1310720 | tf_op jit(solution)/shard_map/all_to_all | solution.py:30
  141.8 10.7 %copy-start.2 = (bf16[16,40,512]{2,1,0:T(8,128)(2,1)S(1)}, bf16[16,40,512]{2,1,0:T(8,128)(2,1)}, u32[]{:S(2)}) copy-start(bf16[16,40,512]{2,1,0:T(8,128)(2,1)} %copy-done.1) | copy-start | bytes 1966084
  142.6 10.7 %collective-permute-start.4 = (bf16[160,640]{1,0:T(8,128)(2,1)}, bf16[160,640]{1,0:T(8,128)(2,1)S(1)}, u32[]{:S(2)}, u32[]{:S(2)}) collective-permute-start(bf16[160,640]{1,0:T(8,128)(2,1)} %get-tuple-element.8), channel_id=1, source_target_pairs={{0,4},{2,6},{4,0},{6,2},{1,5},{3,7},{5,1},{7,3},{8,12},{10,14},{12... | collective-permute-start | bytes 614408 | tf_op jit(solution)/shard_map/ppermute | solution.py:41
  147.2 9.8 %collective-permute-start.6 = (bf16[160,640]{1,0:T(8,128)(2,1)S(1)}, bf16[160,640]{1,0:T(8,128)(2,1)S(1)}, u32[]{:S(2)}, u32[]{:S(2)}) collective-permute-start(bf16[160,640]{1,0:T(8,128)(2,1)S(1)} %get-tuple-element.9), channel_id=1, source_target_pairs={{0,6},{2,0},{4,2},{6,4},{1,7},{3,1},{5,3},{7,5},{8,14},{10,8},{12,... | collective-permute-start | bytes 614408 | tf_op jit(solution)/shard_map/ppermute | solution.py:41
  150.0 9.0 %collective-permute-start.5 = (bf16[160,640]{1,0:T(8,128)(2,1)S(1)}, bf16[160,640]{1,0:T(8,128)(2,1)S(1)}, u32[]{:S(2)}, u32[]{:S(2)}) collective-permute-start(bf16[160,640]{1,0:T(8,128)(2,1)S(1)} %get-tuple-element.10), channel_id=1, source_target_pairs={{0,2},{2,4},{4,6},{6,0},{1,3},{3,5},{5,7},{7,1},{8,10},{10,12},{12... | collective-permute-start | bytes 614408 | tf_op jit(solution)/shard_map/ppermute | solution.py:41
Sparse Core Ops, SparseCore 0:
  10.1 66.8 all-gather.2

commit v3 on v2

--- a/solution.py
+++ b/solution.py
@@ -51,28 +51,59 @@
     return (mine.astype(f32) + got.astype(f32)).astype(bf16)
 
 
+def spread(block, axis, count):
+    copies = jnp.broadcast_to(block[None], (count,) + block.shape)
+    return lax.all_to_all(copies, axis, 0, 0, tiled=True).reshape((-1,) + block.shape[1:])
+
+
+def spread_steps(block, axis, count):
+    me = lax.axis_index(axis)
+    rows = jnp.zeros((count,) + block.shape, block.dtype)
+    rows = lax.dynamic_update_index_in_dim(rows, block, me, 0)
+    for step in (2, 1, 3):
+        pairs = [(i, (i + step) % count) for i in range(count)]
+        got = lax.ppermute(block, axis, pairs)
+        rows = lax.dynamic_update_index_in_dim(rows, got, lax.rem(me - step + count, count), 0)
+    return rows.reshape((-1,) + block.shape[1:])
+
+
+def ordered(value, earlier):
+    return lax.optimization_barrier((value, earlier))[0]
+
+
 def per_device(inputs, w_in, w_out, y_cot):
-    cot_pad = jnp.pad(y_cot.T, ((0, 24), (0, 0)))
-    cot_t = lax.all_gather(cot_pad, "col", axis=0)[:, :40].reshape(640, 512)
-    x_t = gather(inputs.T, "col")
-    hidden = scatter_sum(dot(x_t, w_in, "dt,df->tf"), "row", n_row)
-    value, slope = gelu_pair(hidden)
-    act_rows = gather(value.astype(bf16), "row")
-    y_out = scatter_sum(dot(w_out, act_rows, "fd,tf->dt"), "col", n_col)
-    cot_t, _ = lax.optimization_barrier((cot_t, act_rows))
-    act_grad = scatter_sum_steps(dot(cot_t, w_out, "dt,fd->tf"), "row", n_row)
-    grad_rows = gather((act_grad * slope).astype(bf16), "row")
-    x_grad = scatter_sum(dot(w_in, grad_rows, "df,tf->dt"), "col", n_col)
-    w_terms = jnp.concatenate(
-        [dot(x_t, grad_rows, "dt,tf->df"), dot(act_rows, cot_t, "tf,dt->fd")], 0
+    both = gather(jnp.concatenate([inputs.T, y_cot.T[:16]], 0), "col").reshape(n_col, 56, 512)
+    rest = ordered(y_cot.T[16:], both)
+    rest = spread(rest, "col", n_col).reshape(n_col, 24, 512)
+    x_t = both[:, :40].reshape(640, 512)
+    hidden_terms = dot(x_t, w_in, "dt,df->tf")
+    cot_t = jnp.concatenate([both[:, 40:], rest], 1).reshape(640, 512)
+    grad_terms = dot(cot_t, w_out, "dt,fd->tf")
+    terms = jnp.stack([hidden_terms.reshape(4, 128, 640), grad_terms.reshape(4, 128, 640)], 1)
+    got = lax.all_to_all(terms, "row", 0, 0, tiled=True).astype(f32)
+    sums = jnp.sum(got, axis=0)
+    value, slope = gelu_pair(sums[0])
+    pair = jnp.stack([value.astype(bf16), (sums[1] * slope).astype(bf16)])
+    rows = spread(pair[None], "row", n_row)
+    act_rows = rows[:, 0].reshape(512, 640)
+    grad_rows = rows[:, 1].reshape(512, 640)
+    out_terms = jnp.stack(
+        [
+            dot(w_out, act_rows, "fd,tf->dt").reshape(16, 40, 512),
+            dot(w_in, grad_rows, "df,tf->dt").reshape(16, 40, 512),
+        ],
+        1,
     )
+    out_got = lax.all_to_all(out_terms, "col", 0, 0, tiled=True).astype(f32)
+    outs = jnp.sum(out_got, axis=0).astype(bf16)
+    w_terms = jnp.stack([dot(x_t, grad_rows, "dt,tf->df"), dot(act_rows, cot_t, "tf,dt->fd")])
     w_terms = w_terms.reshape(2, 2, 320, 640).swapaxes(0, 1).reshape(1280, 640)
     half = core_half_sum(w_terms)
     quarter = scatter_sum_steps(half, "chip", n_chip).astype(bf16)
     half = gather(quarter, "chip")
     w_in_sum = gather(half[:320], "core")
     w_out_sum = gather(half[320:], "core")
-    return (y_out.astype(bf16).T, x_grad.astype(bf16).T, w_in_sum, w_out_sum)
+    return (outs[0].T, outs[1].T, w_in_sum, w_out_sum)
 
 
 def solution(mesh):

time: 191 us -> 170 us (0.89)
  the two profiles are of different devices: /device:TPU:1 before, /device:TPU:24 now
where the time goes in v3:
time: 170 us; the launch traced here: 169 us
  blocking collectives  95.6 us (56%)
  waiting for transfers between devices  29.2 us (17%)
  starting transfers between devices  23.4 us (14%)
  local copies, waits for them, and re-layouts  9.3 us (5%)
  matrix products  6.47 us (4%)
  other arithmetic  4.69 us (3%)
    all_gather x4, blocking collectives, gather(): return lax.all_gather(block, axis, axis=0, tiled=True)  59.1 us
    all_to_all x1, blocking collectives, per_device(): got = lax.all_to_all(terms, 'row', 0, 0, tiled=True).astype(f32)  21.7 us
    all_to_all x1, waiting for transfers between devices, spread(): lax.all_to_all(copies, axis, 0, 0, tiled=True)  16.9 us
    all_to_all x1, blocking collectives, spread(): lax.all_to_all(copies, axis, 0, 0, tiled=True)  14.7 us
    ppermute x3, starting transfers between devices, scatter_sum_steps(): total = total + lax.ppermute(block, axis, pairs).astype(f32)  10.2 us
    all_to_all x1, starting transfers between devices, spread(): lax.all_to_all(copies, axis, 0, 0, tiled=True)  6.73 us
    dot_general x6, matrix products, dot(): return jnp.einsum(spec, a, b, preferred_element_type=f32).astype(bf16)  6.47 us
    all_to_all x1, waiting for transfers between devices, per_device(): out_got = lax.all_to_all(out_terms, 'col', 0, 0, tiled=True).astype(f32)  5.19 us
  transfers between devices with their start and end apart: 6, of which 5 were waited for; matrix products, arithmetic and copies ran while one was open for 2% of the time, Pallas kernels for 0%

profile of v3, /device:TPU:24, one launch (start us, length us, event | category | flops | bytes accessed | tf_op | source)
XLA Modules:
  0.0 169.5 jit_solution(5560570513283652313)
XLA Ops:
  3.0 40.7 %all_gather.12 = bf16[896,512]{1,0:T(8,128)(2,1)S(1)} all-gather(bf16[56,512]{1,0:T(8,128)(2,1)S(1)} %pad_maximum_fusion.5), channel_id=1, replica_groups=mesh['row'=4,'col'=16,'chip'=4,'core'=2] {'col'}, dimensions={0}, use_global_device_ids=true | all-gather | bytes 974848 | tf_op jit(solution)/shard_map/all_gather | solution.py:25
  44.4 6.7 %all-to-all-start = ((bf16[16,24,512]{2,1,0:T(8,128)(2,1)}), bf16[16,24,512]{2,1,0:T(8,128)(2,1)S(1)}, u32[]{:S(2)}, u32[]{:S(2)}) async-start(bf16[16,24,512]{2,1,0:T(8,128)(2,1)} %broadcast_in_dim.4), calls=%async_computation | async-start | bytes 786432 | tf_op jit(solution)/shard_map/all_to_all | solution.py:56
  52.8 16.9 %all-to-all-done = bf16[16,24,512]{2,1,0:T(8,128)(2,1)S(1)} async-done(((bf16[16,24,512]{2,1,0:T(8,128)(2,1)}), bf16[16,24,512]{2,1,0:T(8,128)(2,1)S(1)}, u32[]{:S(2)}, u32[]{:S(2)}) %all-to-all-start) | async-done | bytes 393248 | tf_op jit(solution)/shard_map/all_to_all | solution.py:56
  70.8 21.7 %all_to_all.20 = bf16[4,2,128,640]{3,2,1,0:T(8,128)(2,1)S(1)} all-to-all(bf16[4,2,128,640]{3,2,1,0:T(8,128)(2,1)S(1)} %pad_maximum_fusion.1), channel_id=1, replica_groups=mesh['row'=4,'col'=16,'chip'=4,'core'=2] {'row'}, dimensions={0} | all-to-all | bytes 2621440 | tf_op jit(solution)/shard_map/all_to_all | solution.py:83
  93.1 14.7 %all_to_all.21 = bf16[4,1,2,128,640]{4,3,2,1,0:T(8,128)(2,1)S(1)} all-to-all(bf16[4,1,2,128,640]{4,3,2,1,0:T(8,128)(2,1)S(1)} %broadcast_in_dim.5), channel_id=1, replica_groups=mesh['row'=4,'col'=16,'chip'=4,'core'=2] {'row'}, dimensions={0} | all-to-all | bytes 2621440 | tf_op jit(solution)/shard_map/all_to_all | solution.py:56
  109.0 2.7 %fusion.1 = bf16[640,512]{0,1:T(8,128)(2,1)} fusion(bf16[512,640]{1,0:T(8,128)(2,1)S(1)} %bitcast.75, bf16[640,640]{1,0:T(8,128)(2,1)} %param.6), kind=kOutput, calls=%fused_computation.12 | convolution fusion | flops 419758080 | bytes 2129920 | tf_op jit(solution)/shard_map/fd,tf->dt/dot_general | solution.py:21
  111.8 1.3 copy.14
  113.2 1.2 copy.16
  114.4 4.5 %all-to-all-start.3 = ((bf16[16,2,40,512]{3,2,1,0:T(8,128)(2,1)}), bf16[16,2,40,512]{3,2,1,0:T(8,128)(2,1)}, u32[]{:S(2)}, u32[]{:S(2)}) async-start(bf16[16,2,40,512]{3,2,1,0:T(8,128)(2,1)} %copy.16), calls=%async_computation.3 | async-start | bytes 2621440 | tf_op jit(solution)/shard_map/all_to_all | solution.py:97
  121.0 1.9 %collective-permute-start = (bf16[640,640]{1,0:T(8,128)(2,1)S(1)}, bf16[640,640]{1,0:T(8,128)(2,1)}, u32[]{:S(2)}, u32[]{:S(2)}) collective-permute-start(bf16[640,640]{1,0:T(8,128)(2,1)S(1)} %dynamic-slice_bitcast_fusion), channel_id=1, source_target_pairs={{0,1},{1,0},{2,3},{3,2},{4,5},{5,4},{6,7},{7,6},{8,9},{9,8},{10,11... | collective-permute-start | bytes 2457608 | tf_op jit(solution)/shard_map/ppermute | solution.py:50
  123.0 2.4 %collective-permute-done = bf16[640,640]{1,0:T(8,128)(2,1)} collective-permute-done((bf16[640,640]{1,0:T(8,128)(2,1)S(1)}, bf16[640,640]{1,0:T(8,128)(2,1)}, u32[]{:S(2)}, u32[]{:S(2)}) %collective-permute-start) | collective-permute-done | bytes 819232 | tf_op jit(solution)/shard_map/ppermute | solution.py:50
  125.4 1.3 fusion
  126.8 3.1 %collective-permute-start.1 = (bf16[160,640]{1,0:T(8,128)(2,1)S(1)}, bf16[160,640]{1,0:T(8,128)(2,1)S(1)}, u32[]{:S(2)}, u32[]{:S(2)}) collective-permute-start(bf16[160,640]{1,0:T(8,128)(2,1)S(1)} %get-tuple-element.10), channel_id=1, source_target_pairs={{0,4},{2,6},{4,0},{6,2},{1,5},{3,7},{5,1},{7,3},{8,12},{10,14},{12... | collective-permute-start | bytes 614408 | tf_op jit(solution)/shard_map/ppermute | solution.py:41
  130.0 1.9 %collective-permute-start.3 = (bf16[160,640]{1,0:T(8,128)(2,1)S(1)}, bf16[160,640]{1,0:T(8,128)(2,1)S(1)}, u32[]{:S(2)}, u32[]{:S(2)}) collective-permute-start(bf16[160,640]{1,0:T(8,128)(2,1)S(1)} %get-tuple-element.11), channel_id=1, source_target_pairs={{0,6},{2,0},{4,2},{6,4},{1,7},{3,1},{5,3},{7,5},{8,14},{10,8},{12,... | collective-permute-start | bytes 614408 | tf_op jit(solution)/shard_map/ppermute | solution.py:41
  131.9 5.1 %collective-permute-start.2 = (bf16[160,640]{1,0:T(8,128)(2,1)S(1)}, bf16[160,640]{1,0:T(8,128)(2,1)S(1)}, u32[]{:S(2)}, u32[]{:S(2)}) collective-permute-start(bf16[160,640]{1,0:T(8,128)(2,1)S(1)} %get-tuple-element.12), channel_id=1, source_target_pairs={{0,2},{2,4},{4,6},{6,0},{1,3},{3,5},{5,7},{7,1},{8,10},{10,12},{12... | collective-permute-start | bytes 614408 | tf_op jit(solution)/shard_map/ppermute | solution.py:41
  137.1 1.1 collective-permute-done.1
  138.1 3.6 %collective-permute-done.3 = bf16[160,640]{1,0:T(8,128)(2,1)S(1)} collective-permute-done((bf16[160,640]{1,0:T(8,128)(2,1)S(1)}, bf16[160,640]{1,0:T(8,128)(2,1)S(1)}, u32[]{:S(2)}, u32[]{:S(2)}) %collective-permute-start.3) | collective-permute-done | bytes 204832 | tf_op jit(solution)/shard_map/ppermute | solution.py:41
  141.9 13.7 %all_gather.13 = bf16[640,640]{1,0:T(8,128)(2,1)S(1)} all-gather(bf16[160,640]{1,0:T(8,128)(2,1)S(1)} %fusion.5), channel_id=1, replica_groups=mesh['row'=4,'col'=16,'chip'=4,'core'=2] {'chip'}, dimensions={0}, use_global_device_ids=true | all-gather | bytes 1024000 | tf_op jit(solution)/shard_map/all_gather | solution.py:25
  155.6 2.4 %all_gather.15 = bf16[640,640]{1,0:T(8,128)(2,1)S(1)} all-gather(bf16[320,640]{1,0:T(8,128)(2,1)S(1)} %get-tuple-element.8), channel_id=1, replica_groups=mesh['row'=4,'col'=16,'chip'=4,'core'=2] {'core'}, dimensions={0}, use_global_device_ids=true | all-gather | bytes 1228800 | tf_op jit(solution)/shard_map/all_gather | solution.py:25
  158.0 2.4 %all_gather.14 = bf16[640,640]{1,0:T(8,128)(2,1)S(1)} all-gather(bf16[320,640]{1,0:T(8,128)(2,1)S(1)} %get-tuple-element.9), channel_id=1, replica_groups=mesh['row'=4,'col'=16,'chip'=4,'core'=2] {'core'}, dimensions={0}, use_global_device_ids=true | all-gather | bytes 1228800 | tf_op jit(solution)/shard_map/all_gather | solution.py:25
  160.4 5.2 %all-to-all-done.3 = bf16[16,2,40,512]{3,2,1,0:T(8,128)(2,1)} async-done(((bf16[16,2,40,512]{3,2,1,0:T(8,128)(2,1)}), bf16[16,2,40,512]{3,2,1,0:T(8,128)(2,1)}, u32[]{:S(2)}, u32[]{:S(2)}) %all-to-all-start.3) | async-done | bytes 1310752 | tf_op jit(solution)/shard_map/all_to_all | solution.py:97
  165.6 1.5 reduce_sum.22
  167.7 0.9 copy.21
  168.6 0.9 copy.22
  (39 shorter events, 10.6 us)
Async XLA Ops:
  0.6 51.4 %copy-start = (bf16[640,640]{1,0:T(8,128)(2,1)S(1)}, bf16[640,640]{1,0:T(8,128)(2,1)}, u32[]{:S(2)}) copy-start(bf16[640,640]{1,0:T(8,128)(2,1)} %param.5) | copy-start | bytes 2457604
  44.4 25.4 %all-to-all-start = ((bf16[16,24,512]{2,1,0:T(8,128)(2,1)}), bf16[16,24,512]{2,1,0:T(8,128)(2,1)S(1)}, u32[]{:S(2)}, u32[]{:S(2)}) async-start(bf16[16,24,512]{2,1,0:T(8,128)(2,1)} %broadcast_in_dim.4), calls=%async_computation | async-start | bytes 786432 | tf_op jit(solution)/shard_map/all_to_all | solution.py:56
  51.2 0.8 copy-start.1
  52.0 17.8 %copy-start.5 = (bf16[640,640]{1,0:T(8,128)(2,1)S(1)}, bf16[640,640]{1,0:T(8,128)(2,1)}, u32[]{:S(2)}) copy-start(bf16[640,640]{1,0:T(8,128)(2,1)} %param.6) | copy-start | bytes 2457604
  69.8 0.8 copy-start.3
  114.4 4.5 %copy-start.2 = (bf16[16,40,512]{2,1,0:T(8,128)(2,1)S(1)}, bf16[16,40,512]{2,1,0:T(8,128)(2,1)}, u32[]{:S(2)}) copy-start(bf16[16,40,512]{2,1,0:T(8,128)(2,1)} %copy-done.1) | copy-start | bytes 1966084
  114.4 51.1 %all-to-all-start.3 = ((bf16[16,2,40,512]{3,2,1,0:T(8,128)(2,1)}), bf16[16,2,40,512]{3,2,1,0:T(8,128)(2,1)}, u32[]{:S(2)}, u32[]{:S(2)}) async-start(bf16[16,2,40,512]{3,2,1,0:T(8,128)(2,1)} %copy.16), calls=%async_computation.3 | async-start | bytes 2621440 | tf_op jit(solution)/shard_map/all_to_all | solution.py:97
  119.0 1.1 copy-start.4
  121.0 4.4 %collective-permute-start = (bf16[640,640]{1,0:T(8,128)(2,1)S(1)}, bf16[640,640]{1,0:T(8,128)(2,1)}, u32[]{:S(2)}, u32[]{:S(2)}) collective-permute-start(bf16[640,640]{1,0:T(8,128)(2,1)S(1)} %dynamic-slice_bitcast_fusion), channel_id=1, source_target_pairs={{0,1},{1,0},{2,3},{3,2},{4,5},{5,4},{6,7},{7,6},{8,9},{9,8},{10,11... | collective-permute-start | bytes 2457608 | tf_op jit(solution)/shard_map/ppermute | solution.py:50
  126.8 11.3 %collective-permute-start.1 = (bf16[160,640]{1,0:T(8,128)(2,1)S(1)}, bf16[160,640]{1,0:T(8,128)(2,1)S(1)}, u32[]{:S(2)}, u32[]{:S(2)}) collective-permute-start(bf16[160,640]{1,0:T(8,128)(2,1)S(1)} %get-tuple-element.10), channel_id=1, source_target_pairs={{0,4},{2,6},{4,0},{6,2},{1,5},{3,7},{5,1},{7,3},{8,12},{10,14},{12... | collective-permute-start | bytes 614408 | tf_op jit(solution)/shard_map/ppermute | solution.py:41
  130.0 11.8 %collective-permute-start.3 = (bf16[160,640]{1,0:T(8,128)(2,1)S(1)}, bf16[160,640]{1,0:T(8,128)(2,1)S(1)}, u32[]{:S(2)}, u32[]{:S(2)}) collective-permute-start(bf16[160,640]{1,0:T(8,128)(2,1)S(1)} %get-tuple-element.11), channel_id=1, source_target_pairs={{0,6},{2,0},{4,2},{6,4},{1,7},{3,1},{5,3},{7,5},{8,14},{10,8},{12,... | collective-permute-start | bytes 614408 | tf_op jit(solution)/shard_map/ppermute | solution.py:41
  131.9 9.8 %collective-permute-start.2 = (bf16[160,640]{1,0:T(8,128)(2,1)S(1)}, bf16[160,640]{1,0:T(8,128)(2,1)S(1)}, u32[]{:S(2)}, u32[]{:S(2)}) collective-permute-start(bf16[160,640]{1,0:T(8,128)(2,1)S(1)} %get-tuple-element.12), channel_id=1, source_target_pairs={{0,2},{2,4},{4,6},{6,0},{1,3},{3,5},{5,7},{7,1},{8,10},{10,12},{12... | collective-permute-start | bytes 614408 | tf_op jit(solution)/shard_map/ppermute | solution.py:41

commit v4 on v3

--- a/solution.py
+++ b/solution.py
@@ -1,6 +1,10 @@
+import math
+
 import jax
 import jax.numpy as jnp
 from jax import lax
+from jax.experimental import pallas as pl
+from jax.experimental.pallas import tpu as pltpu
 from jax.sharding import PartitionSpec as P
 
 gelu_c = 0.7978845608
@@ -71,39 +75,137 @@
     return lax.optimization_barrier((value, earlier))[0]
 
 
+def permute(block, axis, count, step):
+    return lax.ppermute(block, axis, [(i, (i + step) % count) for i in range(count)])
+
+
+vmem = pl.BlockSpec(memory_space=pltpu.VMEM)
+smem = pl.BlockSpec(memory_space=pltpu.SMEM)
+
+
+def kernel_call(body, outs, flops, *args, scratch=()):
+    shapes = tuple(jax.ShapeDtypeStruct(shape, bf16) for shape in outs)
+    moved = sum(2 * math.prod(a.shape) for a in args) + sum(2 * math.prod(s) for s in outs)
+    return pl.pallas_call(
+        body,
+        out_shape=shapes,
+        in_specs=[smem if a.dtype == jnp.int32 else vmem for a in args],
+        out_specs=(vmem,) * len(shapes),
+        scratch_shapes=[pltpu.VMEM(shape, bf16) for shape in scratch],
+        cost_estimate=pl.CostEstimate(flops=flops, bytes_accessed=moved, transcendentals=0),
+        compiler_params=pltpu.CompilerParams(vmem_limit_bytes=32 * 1024 * 1024),
+    )(*args)
+
+
+def contract(a, b, dim_a, dim_b):
+    return lax.dot_general(a, b, (((dim_a,), (dim_b,)), ((), ())), preferred_element_type=f32)
+
+
+def first_kernel(x_ref, cot_ref, first_ref, rest_ref):
+    for block in range(4):
+        first_ref[block] = x_ref[:, block * 128 : (block + 1) * 128]
+    for block in range(2):
+        first_ref[4 + block] = cot_ref[:, block * 128 : (block + 1) * 128]
+        for copy in range(16):
+            rest_ref[copy, block] = cot_ref[:, (2 + block) * 128 : (3 + block) * 128]
+
+
+def hidden_kernel(both_ref, weight_ref, x_ref, terms_ref):
+    weight = weight_ref[...]
+    for block in range(4):
+        rows = both_ref[:, block].reshape(640, 128)
+        x_ref[:, block * 128 : (block + 1) * 128] = rows
+        terms_ref[block] = contract(rows, weight, 0, 0).astype(bf16)
+
+
+def grad_kernel(both_ref, rest_ref, weight_ref, hidden_ref, cot_ref, terms_ref):
+    weight = weight_ref[...]
+    for block in range(4):
+        rows = (both_ref[:, 4 + block] if block < 2 else rest_ref[:, block - 2]).reshape(640, 128)
+        cot_ref[:, block * 128 : (block + 1) * 128] = rows
+        terms_ref[block, 0] = hidden_ref[block]
+        terms_ref[block, 1] = contract(rows, weight, 0, 0).astype(bf16)
+
+
+def out_kernel(out_w_ref, in_w_ref, rows_ref, terms_ref):
+    for stream, weight_ref in ((0, out_w_ref), (1, in_w_ref)):
+        rows = rows_ref[:, stream].reshape(512, 640)
+        terms = contract(weight_ref[...], rows, 1, 1)
+        terms_ref[:, stream] = terms.astype(bf16).reshape(16, 40, 512)
+
+
+def weight_kernel(core_ref, x_ref, cot_ref, rows_ref, mine_ref, other_ref, whole_ref):
+    core = core_ref[0]
+    whole_ref[0] = contract(x_ref[...], rows_ref[:, 1].reshape(512, 640), 1, 0).astype(bf16)
+    whole_ref[1] = contract(rows_ref[:, 0].reshape(512, 640), cot_ref[...], 0, 1).astype(bf16)
+    for grad in range(2):
+        mine_ref[grad] = whole_ref[grad, pl.ds(pl.multiple_of(core * 320, 320), 320)]
+        other_ref[grad] = whole_ref[grad, pl.ds(pl.multiple_of(320 - core * 320, 320), 320)]
+
+
+def sum_kernel(got_ref, y_ref, x_ref):
+    for stream, out_ref in ((0, y_ref), (1, x_ref)):
+        total = got_ref[0, stream].astype(f32)
+        for source in range(1, 16):
+            total = total + got_ref[source, stream].astype(f32)
+        out_ref[...] = total.astype(bf16)
+
+
+def join_kernel(core_ref, mine_ref, other_ref, in_ref, out_ref):
+    core = core_ref[0]
+    for grad, whole_ref in ((0, in_ref), (1, out_ref)):
+        part = slice(grad * 320, (grad + 1) * 320)
+        whole_ref[pl.ds(pl.multiple_of(core * 320, 320), 320)] = mine_ref[part]
+        whole_ref[pl.ds(pl.multiple_of(320 - core * 320, 320), 320)] = other_ref[part]
+
+
 def per_device(inputs, w_in, w_out, y_cot):
-    both = gather(jnp.concatenate([inputs.T, y_cot.T[:16]], 0), "col").reshape(n_col, 56, 512)
-    rest = ordered(y_cot.T[16:], both)
-    rest = spread(rest, "col", n_col).reshape(n_col, 24, 512)
-    x_t = both[:, :40].reshape(640, 512)
-    hidden_terms = dot(x_t, w_in, "dt,df->tf")
-    cot_t = jnp.concatenate([both[:, 40:], rest], 1).reshape(640, 512)
-    grad_terms = dot(cot_t, w_out, "dt,fd->tf")
-    terms = jnp.stack([hidden_terms.reshape(4, 128, 640), grad_terms.reshape(4, 128, 640)], 1)
+    core_id = lax.axis_index("core").astype(jnp.int32)[None]
+    first, rest = kernel_call(
+        first_kernel, [(6, 40, 128), (16, 2, 40, 128)], 0, inputs.T, y_cot.T
+    )
+    both = gather(first.reshape(240, 128), "col").reshape(16, 6, 40, 128)
+    rest = lax.all_to_all(ordered(rest, both).reshape(16, 80, 128), "col", 0, 0, tiled=True)
+    out_w = ordered(w_out.T, both)
+    x_t, hidden_terms = kernel_call(
+        hidden_kernel, [(640, 512), (4, 128, 640)], 2 * 512 * 640 * 640, both, w_in
+    )
+    cot_t, terms = kernel_call(
+        grad_kernel,
+        [(640, 512), (4, 2, 128, 640)],
+        2 * 512 * 640 * 640,
+        both,
+        ordered(rest, hidden_terms).reshape(16, 2, 40, 128),
+        out_w,
+        hidden_terms,
+    )
     got = lax.all_to_all(terms, "row", 0, 0, tiled=True).astype(f32)
-    sums = jnp.sum(got, axis=0)
-    value, slope = gelu_pair(sums[0])
-    pair = jnp.stack([value.astype(bf16), (sums[1] * slope).astype(bf16)])
+    hidden, act_grad = jnp.sum(got[:, 0], axis=0), jnp.sum(got[:, 1], axis=0)
+    value, slope = gelu_pair(hidden)
+    pair = jnp.stack([value.astype(bf16), (act_grad * slope).astype(bf16)])
     rows = spread(pair[None], "row", n_row)
-    act_rows = rows[:, 0].reshape(512, 640)
-    grad_rows = rows[:, 1].reshape(512, 640)
-    out_terms = jnp.stack(
-        [
-            dot(w_out, act_rows, "fd,tf->dt").reshape(16, 40, 512),
-            dot(w_in, grad_rows, "df,tf->dt").reshape(16, 40, 512),
-        ],
-        1,
-    )
-    out_got = lax.all_to_all(out_terms, "col", 0, 0, tiled=True).astype(f32)
-    outs = jnp.sum(out_got, axis=0).astype(bf16)
-    w_terms = jnp.stack([dot(x_t, grad_rows, "dt,tf->df"), dot(act_rows, cot_t, "tf,dt->fd")])
-    w_terms = w_terms.reshape(2, 2, 320, 640).swapaxes(0, 1).reshape(1280, 640)
-    half = core_half_sum(w_terms)
+    (out_terms,) = kernel_call(
+        out_kernel, [(16, 2, 40, 512)], 4 * 512 * 640 * 640, out_w, w_in, rows
+    )
+    out_got = lax.all_to_all(out_terms, "col", 0, 0, tiled=True)
+    y_t, x_grad_t = kernel_call(sum_kernel, [(40, 512)] * 2, 2 * 16 * 40 * 512, out_got)
+    mine, other = kernel_call(
+        weight_kernel,
+        [(2, 320, 640), (2, 320, 640)],
+        4 * 512 * 640 * 640,
+        core_id,
+        x_t,
+        cot_t,
+        rows,
+        scratch=[(2, 640, 640)],
+    )
+    got = lax.ppermute(other, "core", [(0, 1), (1, 0)])
+    half = (mine.astype(f32) + got.astype(f32)).astype(bf16).reshape(640, 640)
     quarter = scatter_sum_steps(half, "chip", n_chip).astype(bf16)
     half = gather(quarter, "chip")
-    w_in_sum = gather(half[:320], "core")
-    w_out_sum = gather(half[320:], "core")
-    return (outs[0].T, outs[1].T, w_in_sum, w_out_sum)
+    other = lax.ppermute(half, "core", [(0, 1), (1, 0)])
+    w_in_sum, w_out_sum = kernel_call(join_kernel, [(640, 640)] * 2, 0, core_id, half, other)
+    return (y_t.T, x_grad_t.T, w_in_sum, w_out_sum)
 
 
 def solution(mesh):

time: 170 us -> 162 us (0.953)
  Pallas kernels: 0 us -> 8.98 us
  blocking collectives: 95.6 us -> 88.3 us
  matrix products: 6.47 us -> 0 us
  waiting for transfers between devices: 29.2 us -> 23 us
  starting transfers between devices: 23.4 us -> 28.6 us
  other arithmetic: 4.69 us -> 2.04 us
    all_to_all x2, waiting for transfers between devices: 22.1 us -> 10.5 us  [the longest x1 10.3 us: per_device(): lax.all_to_all(ordered(rest, both).reshape(16, 80, 128), 'col', 0, 0, til...]
    pallas_call x0 -> x7, Pallas kernels: none -> 8.98 us  [kernel_call(): pl.pallas_call(body, out_shape=shapes, in_specs=[smem if a.dtype == jnp.i...]
    dot_general x6 -> x0, matrix products: 6.47 us -> none  [dot(): return jnp.einsum(spec, a, b, preferred_element_type=f32).astype(bf16)]
    unnamed x14 -> x23, local copies, waits for them, and re-layouts: 3.03 us -> 9.21 us
    all_to_all x2, starting transfers between devices: 11.2 us -> 15.6 us  [the longest x1 8.72 us: per_device(): out_got = lax.all_to_all(out_terms, 'col', 0, 0, tiled=True)]
    all_gather x4 -> x2, blocking collectives: 59.1 us -> 54.8 us  [gather(): return lax.all_gather(block, axis, axis=0, tiled=True)]
    all_to_all x1, blocking collectives: 21.7 us -> 18.6 us  [per_device(): got = lax.all_to_all(terms, 'row', 0, 0, tiled=True).astype(f32)]
    ppermute x3, waiting for transfers between devices: 4.69 us -> 7.73 us  [scatter_sum_steps(): total = total + lax.ppermute(block, axis, pairs).astype(f32)]
  transfers between devices with their start and end apart: 6 -> 7, of which waited for: 5 -> 7; matrix products, arithmetic and copies ran while one was open for 2% -> 2% of each run, Pallas kernels for 0% -> 3%
where the time goes in v4:
time: 162 us; the launch traced here: 161 us
  blocking collectives  88.3 us (55%)
  starting transfers between devices  28.6 us (18%)
  waiting for transfers between devices  23 us (14%)
  local copies, waits for them, and re-layouts  9.4 us (6%)
  Pallas kernels  8.98 us (6%)
  other arithmetic  2.04 us (1%)
    all_gather x2, blocking collectives, gather(): return lax.all_gather(block, axis, axis=0, tiled=True)  54.8 us
    all_to_all x1, blocking collectives, per_device(): got = lax.all_to_all(terms, 'row', 0, 0, tiled=True).astype(f32)  18.6 us
    all_to_all x1, blocking collectives, spread(): lax.all_to_all(copies, axis, 0, 0, tiled=True)  14.9 us
    all_to_all x1, waiting for transfers between devices, per_device(): lax.all_to_all(ordered(rest, both).reshape(16, 80, 128), 'col', 0, 0, til...  10.3 us
    unnamed x23, local copies, waits for them, and re-layouts  9.21 us
    ppermute x3, starting transfers between devices, scatter_sum_steps(): total = total + lax.ppermute(block, axis, pairs).astype(f32)  9.15 us
    pallas_call x7, Pallas kernels, kernel_call(): pl.pallas_call(body, out_shape=shapes, in_specs=[smem if a.dtype == jnp.i...  8.98 us
    all_to_all x1, starting transfers between devices, per_device(): out_got = lax.all_to_all(out_terms, 'col', 0, 0, tiled=True)  8.72 us
  transfers between devices with their start and end apart: 7, of which 7 were waited for; matrix products, arithmetic and copies ran while one was open for 2% of the time, Pallas kernels for 3%

profile of v4, /device:TPU:24, one launch (start us, length us, event | category | flops | bytes accessed | tf_op | source)
XLA Modules:
  0.0 161.1 jit_solution(6070163522927082623)
XLA Ops:
  3.0 41.1 %all_gather.6 = bf16[3840,128]{1,0:T(8,128)(2,1)S(1)} all-gather(bf16[240,128]{1,0:T(8,128)(2,1)S(1)} %bitcast.42), channel_id=1, replica_groups=mesh['row'=4,'col'=16,'chip'=4,'core'=2] {'col'}, dimensions={0}, use_global_device_ids=true | all-gather | bytes 1044480 | tf_op jit(solution)/shard_map/all_gather | solution.py:29
  44.0 6.9 %all-to-all-start = ((bf16[16,80,128]{2,1,0:T(8,128)(2,1)}), bf16[16,80,128]{2,1,0:T(8,128)(2,1)S(1)}, u32[]{:S(2)}, u32[]{:S(2)}) async-start(bf16[16,80,128]{2,1,0:T(8,128)(2,1)} %bitcast.5), calls=%async_computation | async-start | bytes 655360 | tf_op jit(solution)/shard_map/all_to_all | solution.py:168
  50.9 1.8 %copy.9 = bf16[640,640]{0,1:T(8,128)(2,1)S(1)} copy(bf16[640,640]{1,0:T(8,128)(2,1)} %param.6) | data formatting | bytes 1638400 | tf_op args[2]
  55.3 10.3 %all-to-all-done = bf16[16,80,128]{2,1,0:T(8,128)(2,1)S(1)} async-done(((bf16[16,80,128]{2,1,0:T(8,128)(2,1)}), bf16[16,80,128]{2,1,0:T(8,128)(2,1)S(1)}, u32[]{:S(2)}, u32[]{:S(2)}) %all-to-all-start) | async-done | bytes 327712 | tf_op jit(solution)/shard_map/all_to_all | solution.py:168
  65.5 1.1 copy-done.4
  67.5 18.6 %all_to_all.20 = bf16[4,2,128,640]{3,2,1,0:T(8,128)(2,1)S(1)} all-to-all(bf16[4,2,128,640]{3,2,1,0:T(8,128)(2,1)S(1)} %get-tuple-element.25), channel_id=1, replica_groups=mesh['row'=4,'col'=16,'chip'=4,'core'=2] {'row'}, dimensions={0} | all-to-all | bytes 2621440 | tf_op jit(solution)/shard_map/all_to_all | solution.py:182
  86.8 14.9 %all_to_all.21 = bf16[4,1,2,128,640]{4,3,2,1,0:T(8,128)(2,1)S(1)} all-to-all(bf16[4,1,2,128,640]{4,3,2,1,0:T(8,128)(2,1)S(1)} %broadcast_in_dim.8), channel_id=1, replica_groups=mesh['row'=4,'col'=16,'chip'=4,'core'=2] {'row'}, dimensions={0} | all-to-all | bytes 2621440 | tf_op jit(solution)/shard_map/all_to_all | solution.py:60
  101.7 2.3 %shard_map.78 = bf16[16,2,40,512]{3,2,1,0:T(8,128)(2,1)} custom-call(bf16[640,640]{1,0:T(8,128)(2,1)S(1)} %bitcast.38, bf16[640,640]{1,0:T(8,128)(2,1)S(1)} %copy-done.1, bf16[4,2,128,640]{3,2,1,0:T(8,128)(2,1)S(1)} %bitcast.39), custom_call_target="tpu_custom_call" | custom-call | flops 838860800 | bytes 4259840 | tf_op jit(solution)/shard_map/pallas_call | solution.py:89
  103.9 8.7 %all-to-all-start.3 = ((bf16[16,2,40,512]{3,2,1,0:T(8,128)(2,1)}), bf16[16,2,40,512]{3,2,1,0:T(8,128)(2,1)S(1)}, u32[]{:S(2)}, u32[]{:S(2)}) async-start(bf16[16,2,40,512]{3,2,1,0:T(8,128)(2,1)} %shard_map.78), calls=%async_computation.3 | async-start | bytes 2621440 | tf_op jit(solution)/shard_map/all_to_all | solution.py:190
  113.8 1.1 copy-done.10
  114.9 2.2 %shard_map.80 = (bf16[2,320,640]{2,1,0:T(8,128)(2,1)S(1)}, bf16[2,320,640]{2,1,0:T(8,128)(2,1)}) custom-call(s32[1]{0:T(128)} %bitcast.12.core_ref, bf16[640,512]{1,0:T(8,128)(2,1)S(1)} %copy-done.8, bf16[640,512]{1,0:T(8,128)(2,1)S(1)} %copy-done.10, bf16[4,2,128,640]{3,2,1,0:T(8,128)(2,1)S(1)} %bitcast.40), custom_call_target="tpu_custom_call" | custom-call | flops 838860800 | bytes 4259842 | tf_op jit(solution)/shard_map/pallas_call | solution.py:89
  117.9 1.9 %collective-permute-start = (bf16[2,320,640]{2,1,0:T(8,128)(2,1)}, bf16[2,320,640]{2,1,0:T(8,128)(2,1)S(1)}, u32[]{:S(2)}, u32[]{:S(2)}) collective-permute-start(bf16[2,320,640]{2,1,0:T(8,128)(2,1)} %get-tuple-element.31), channel_id=1, source_target_pairs={{0,1},{1,0},{2,3},{3,2},{4,5},{5,4},{6,7},{7,6},{8,9},{9,8},{10,11... | collective-permute-start | bytes 2457608 | tf_op jit(solution)/shard_map/ppermute | solution.py:202
  119.9 2.5 %collective-permute-done = bf16[2,320,640]{2,1,0:T(8,128)(2,1)S(1)} collective-permute-done((bf16[2,320,640]{2,1,0:T(8,128)(2,1)}, bf16[2,320,640]{2,1,0:T(8,128)(2,1)S(1)}, u32[]{:S(2)}, u32[]{:S(2)}) %collective-permute-start) | collective-permute-done | bytes 819232 | tf_op jit(solution)/shard_map/ppermute | solution.py:202
  122.4 1.3 add_convert_fusion
  123.8 3.2 %collective-permute-start.1 = (bf16[160,640]{1,0:T(8,128)(2,1)S(1)}, bf16[160,640]{1,0:T(8,128)(2,1)S(1)}, u32[]{:S(2)}, u32[]{:S(2)}) collective-permute-start(bf16[160,640]{1,0:T(8,128)(2,1)S(1)} %get-tuple-element.36), channel_id=1, source_target_pairs={{0,4},{2,6},{4,0},{6,2},{1,5},{3,7},{5,1},{7,3},{8,12},{10,14},{12... | collective-permute-start | bytes 614408 | tf_op jit(solution)/shard_map/ppermute | solution.py:45
  127.0 4.1 %collective-permute-start.2 = (bf16[160,640]{1,0:T(8,128)(2,1)S(1)}, bf16[160,640]{1,0:T(8,128)(2,1)S(1)}, u32[]{:S(2)}, u32[]{:S(2)}) collective-permute-start(bf16[160,640]{1,0:T(8,128)(2,1)S(1)} %get-tuple-element.38), channel_id=1, source_target_pairs={{0,2},{2,4},{4,6},{6,0},{1,3},{3,5},{5,7},{7,1},{8,10},{10,12},{12... | collective-permute-start | bytes 614408 | tf_op jit(solution)/shard_map/ppermute | solution.py:45
  131.1 1.9 %collective-permute-start.3 = (bf16[160,640]{1,0:T(8,128)(2,1)S(1)}, bf16[160,640]{1,0:T(8,128)(2,1)S(1)}, u32[]{:S(2)}, u32[]{:S(2)}) collective-permute-start(bf16[160,640]{1,0:T(8,128)(2,1)S(1)} %get-tuple-element.37), channel_id=1, source_target_pairs={{0,6},{2,0},{4,2},{6,4},{1,7},{3,1},{5,3},{7,5},{8,14},{10,8},{12,... | collective-permute-start | bytes 614408 | tf_op jit(solution)/shard_map/ppermute | solution.py:45
  133.0 1.3 collective-permute-done.1
  134.3 1.9 %collective-permute-done.2 = bf16[160,640]{1,0:T(8,128)(2,1)S(1)} collective-permute-done((bf16[160,640]{1,0:T(8,128)(2,1)S(1)}, bf16[160,640]{1,0:T(8,128)(2,1)S(1)}, u32[]{:S(2)}, u32[]{:S(2)}) %collective-permute-start.2) | collective-permute-done | bytes 204832 | tf_op jit(solution)/shard_map/ppermute | solution.py:45
  136.3 4.5 %collective-permute-done.3 = bf16[160,640]{1,0:T(8,128)(2,1)S(1)} collective-permute-done((bf16[160,640]{1,0:T(8,128)(2,1)S(1)}, bf16[160,640]{1,0:T(8,128)(2,1)S(1)}, u32[]{:S(2)}, u32[]{:S(2)}) %collective-permute-start.3) | collective-permute-done | bytes 204832 | tf_op jit(solution)/shard_map/ppermute | solution.py:45
  140.8 13.7 %all_gather.7.mine_ref = bf16[640,640]{1,0:T(8,128)(2,1)S(1)} all-gather(bf16[160,640]{1,0:T(8,128)(2,1)S(1)} %fusion.2), channel_id=1, replica_groups=mesh['row'=4,'col'=16,'chip'=4,'core'=2] {'chip'}, dimensions={0}, use_global_device_ids=true | all-gather | bytes 1024000 | tf_op jit(solution)/shard_map/all_gather | solution.py:29
  154.5 1.9 %collective-permute-start.4 = (bf16[640,640]{1,0:T(8,128)(2,1)S(1)}, bf16[640,640]{1,0:T(8,128)(2,1)S(1)}, u32[]{:S(2)}, u32[]{:S(2)}) collective-permute-start(bf16[640,640]{1,0:T(8,128)(2,1)S(1)} %all_gather.7.mine_ref), channel_id=1, source_target_pairs={{0,1},{1,0},{2,3},{3,2},{4,5},{5,4},{6,7},{7,6},{8,9},{9,8},{10,11... | collective-permute-start | bytes 2457608 | tf_op jit(solution)/shard_map/ppermute | solution.py:206
  156.5 2.3 %collective-permute-done.4.other_ref = bf16[640,640]{1,0:T(8,128)(2,1)S(1)} collective-permute-done((bf16[640,640]{1,0:T(8,128)(2,1)S(1)}, bf16[640,640]{1,0:T(8,128)(2,1)S(1)}, u32[]{:S(2)}, u32[]{:S(2)}) %collective-permute-start.4) | collective-permute-done | bytes 819232 | tf_op jit(solution)/shard_map/ppermute | solution.py:206
  158.8 1.3 shard_map.81
  (32 shorter events, 9.5 us)
Async XLA Ops:
  0.6 0.8 copy-start.5
  1.4 0.8 copy-start.6
  44.0 8.7 %copy-start = (bf16[640,640]{1,0:T(8,128)(2,1)S(1)}, bf16[640,640]{1,0:T(8,128)(2,1)}, u32[]{:S(2)}) copy-start(bf16[640,640]{1,0:T(8,128)(2,1)} %in_w_ref.1) | copy-start | bytes 2457604
  44.0 21.5 %all-to-all-start = ((bf16[16,80,128]{2,1,0:T(8,128)(2,1)}), bf16[16,80,128]{2,1,0:T(8,128)(2,1)S(1)}, u32[]{:S(2)}, u32[]{:S(2)}) async-start(bf16[16,80,128]{2,1,0:T(8,128)(2,1)} %bitcast.5), calls=%async_computation | async-start | bytes 655360 | tf_op jit(solution)/shard_map/all_to_all | solution.py:168
  53.6 0.8 copy-start.3
  54.4 0.8 copy-start.7
  65.5 1.1 copy-start.4
  67.5 18.6 %copy-start.9 = (bf16[640,512]{1,0:T(8,128)(2,1)}, bf16[640,512]{1,0:T(8,128)(2,1)S(1)}, u32[]{:S(2)}) copy-start(bf16[640,512]{1,0:T(8,128)(2,1)S(1)} %get-tuple-element.29.cot_ref) | copy-start | bytes 1966084
  86.8 14.9 %copy-start.1 = (bf16[640,640]{1,0:T(8,128)(2,1)S(1)}, bf16[640,640]{1,0:T(8,128)(2,1)}, u32[]{:S(2)}) copy-start(bf16[640,640]{1,0:T(8,128)(2,1)} %in_w_ref.1) | copy-start | bytes 2457604
  103.9 56.3 %all-to-all-start.3 = ((bf16[16,2,40,512]{3,2,1,0:T(8,128)(2,1)}), bf16[16,2,40,512]{3,2,1,0:T(8,128)(2,1)S(1)}, u32[]{:S(2)}, u32[]{:S(2)}) async-start(bf16[16,2,40,512]{3,2,1,0:T(8,128)(2,1)} %shard_map.78), calls=%async_computation.3 | async-start | bytes 2621440 | tf_op jit(solution)/shard_map/all_to_all | solution.py:190
  112.7 1.1 copy-start.8
  113.8 1.1 copy-start.10
  117.1 0.9 copy-start.2
  117.9 4.4 %collective-permute-start = (bf16[2,320,640]{2,1,0:T(8,128)(2,1)}, bf16[2,320,640]{2,1,0:T(8,128)(2,1)S(1)}, u32[]{:S(2)}, u32[]{:S(2)}) collective-permute-start(bf16[2,320,640]{2,1,0:T(8,128)(2,1)} %get-tuple-element.31), channel_id=1, source_target_pairs={{0,1},{1,0},{2,3},{3,2},{4,5},{5,4},{6,7},{7,6},{8,9},{9,8},{10,11... | collective-permute-start | bytes 2457608 | tf_op jit(solution)/shard_map/ppermute | solution.py:202
  123.8 10.5 %collective-permute-start.1 = (bf16[160,640]{1,0:T(8,128)(2,1)S(1)}, bf16[160,640]{1,0:T(8,128)(2,1)S(1)}, u32[]{:S(2)}, u32[]{:S(2)}) collective-permute-start(bf16[160,640]{1,0:T(8,128)(2,1)S(1)} %get-tuple-element.36), channel_id=1, source_target_pairs={{0,4},{2,6},{4,0},{6,2},{1,5},{3,7},{5,1},{7,3},{8,12},{10,14},{12... | collective-permute-start | bytes 614408 | tf_op jit(solution)/shard_map/ppermute | solution.py:45
  127.0 9.3 %collective-permute-start.2 = (bf16[160,640]{1,0:T(8,128)(2,1)S(1)}, bf16[160,640]{1,0:T(8,128)(2,1)S(1)}, u32[]{:S(2)}, u32[]{:S(2)}) collective-permute-start(bf16[160,640]{1,0:T(8,128)(2,1)S(1)} %get-tuple-element.38), channel_id=1, source_target_pairs={{0,2},{2,4},{4,6},{6,0},{1,3},{3,5},{5,7},{7,1},{8,10},{10,12},{12... | collective-permute-start | bytes 614408 | tf_op jit(solution)/shard_map/ppermute | solution.py:45
  131.1 9.7 %collective-permute-start.3 = (bf16[160,640]{1,0:T(8,128)(2,1)S(1)}, bf16[160,640]{1,0:T(8,128)(2,1)S(1)}, u32[]{:S(2)}, u32[]{:S(2)}) collective-permute-start(bf16[160,640]{1,0:T(8,128)(2,1)S(1)} %get-tuple-element.37), channel_id=1, source_target_pairs={{0,6},{2,0},{4,2},{6,4},{1,7},{3,1},{5,3},{7,5},{8,14},{10,8},{12,... | collective-permute-start | bytes 614408 | tf_op jit(solution)/shard_map/ppermute | solution.py:45
  154.5 4.2 %collective-permute-start.4 = (bf16[640,640]{1,0:T(8,128)(2,1)S(1)}, bf16[640,640]{1,0:T(8,128)(2,1)S(1)}, u32[]{:S(2)}, u32[]{:S(2)}) collective-permute-start(bf16[640,640]{1,0:T(8,128)(2,1)S(1)} %all_gather.7.mine_ref), channel_id=1, source_target_pairs={{0,1},{1,0},{2,3},{3,2},{4,5},{5,4},{6,7},{7,6},{8,9},{9,8},{10,11... | collective-permute-start | bytes 2457608 | tf_op jit(solution)/shard_map/ppermute | solution.py:206

commit v5 on v4

--- a/solution.py
+++ b/solution.py
@@ -101,30 +101,18 @@
     return lax.dot_general(a, b, (((dim_a,), (dim_b,)), ((), ())), preferred_element_type=f32)
 
 
-def first_kernel(x_ref, cot_ref, first_ref, rest_ref):
-    for block in range(4):
-        first_ref[block] = x_ref[:, block * 128 : (block + 1) * 128]
-    for block in range(2):
-        first_ref[4 + block] = cot_ref[:, block * 128 : (block + 1) * 128]
-        for copy in range(16):
-            rest_ref[copy, block] = cot_ref[:, (2 + block) * 128 : (3 + block) * 128]
-
-
-def hidden_kernel(both_ref, weight_ref, x_ref, terms_ref):
-    weight = weight_ref[...]
-    for block in range(4):
-        rows = both_ref[:, block].reshape(640, 128)
-        x_ref[:, block * 128 : (block + 1) * 128] = rows
-        terms_ref[block] = contract(rows, weight, 0, 0).astype(bf16)
-
-
-def grad_kernel(both_ref, rest_ref, weight_ref, hidden_ref, cot_ref, terms_ref):
-    weight = weight_ref[...]
-    for block in range(4):
-        rows = (both_ref[:, 4 + block] if block < 2 else rest_ref[:, block - 2]).reshape(640, 128)
-        cot_ref[:, block * 128 : (block + 1) * 128] = rows
-        terms_ref[block, 0] = hidden_ref[block]
-        terms_ref[block, 1] = contract(rows, weight, 0, 0).astype(bf16)
+def terms_kernel(
+    odd_ref, own_ref, x_other_ref, cot_other_ref, in_w_ref, out_w_ref, x_ref, cot_ref, terms_ref
+):
+    odd = odd_ref[0]
+    for stream, other_ref, weight_ref, whole_ref in (
+        (0, x_other_ref, in_w_ref, x_ref), (1, cot_other_ref, out_w_ref, cot_ref)
+    ):
+        for high in range(8):
+            whole_ref[2 * high + odd] = own_ref[high, stream * 40 : (stream + 1) * 40]
+            whole_ref[2 * high + 1 - odd] = other_ref[high]
+        terms = contract(whole_ref[...].reshape(640, 512), weight_ref[...], 0, 0)
+        terms_ref[:, stream] = terms.astype(bf16).reshape(4, 128, 640)
 
 
 def out_kernel(out_w_ref, in_w_ref, rows_ref, terms_ref):
@@ -146,39 +134,59 @@
 def sum_kernel(got_ref, y_ref, x_ref):
     for stream, out_ref in ((0, y_ref), (1, x_ref)):
         total = got_ref[0, stream].astype(f32)
-        for source in range(1, 16):
+        for source in range(1, got_ref.shape[0]):
             total = total + got_ref[source, stream].astype(f32)
         out_ref[...] = total.astype(bf16)
 
 
-def join_kernel(core_ref, mine_ref, other_ref, in_ref, out_ref):
+def join_kernel(core_ref, in_mine_ref, out_mine_ref, in_other_ref, out_other_ref, in_ref, out_ref):
     core = core_ref[0]
-    for grad, whole_ref in ((0, in_ref), (1, out_ref)):
-        part = slice(grad * 320, (grad + 1) * 320)
-        whole_ref[pl.ds(pl.multiple_of(core * 320, 320), 320)] = mine_ref[part]
-        whole_ref[pl.ds(pl.multiple_of(320 - core * 320, 320), 320)] = other_ref[part]
+    mine = pl.ds(pl.multiple_of(core * 320, 320), 320)
+    other = pl.ds(pl.multiple_of(320 - core * 320, 320), 320)
+    in_ref[mine] = in_mine_ref[...]
+    in_ref[other] = in_other_ref[...]
+    out_ref[mine] = out_mine_ref[...]
+    out_ref[other] = out_other_ref[...]
+
+
+def add(a, b):
+    return (a.astype(f32) + b.astype(f32)).astype(bf16)
+
+
+EVEN = [(0, 1), (1, 0), (2, 3), (3, 2)]
+ODD = [(1, 2), (2, 1), (3, 0), (0, 3)]
+
+
+def chip_sum(in_half, out_half):
+    in_got, out_got = lax.ppermute(in_half, "chip", EVEN), lax.ppermute(out_half, "chip", ODD)
+    in_half, out_half = add(in_half, in_got), add(out_half, out_got)
+    in_got, out_got = lax.ppermute(in_half, "chip", ODD), lax.ppermute(out_half, "chip", EVEN)
+    return add(in_half, in_got), add(out_half, out_got)
+
+
+COL = ("high", "low")
 
 
 def per_device(inputs, w_in, w_out, y_cot):
     core_id = lax.axis_index("core").astype(jnp.int32)[None]
-    first, rest = kernel_call(
-        first_kernel, [(6, 40, 128), (16, 2, 40, 128)], 0, inputs.T, y_cot.T
-    )
-    both = gather(first.reshape(240, 128), "col").reshape(16, 6, 40, 128)
-    rest = lax.all_to_all(ordered(rest, both).reshape(16, 80, 128), "col", 0, 0, tiled=True)
-    out_w = ordered(w_out.T, both)
-    x_t, hidden_terms = kernel_call(
-        hidden_kernel, [(640, 512), (4, 128, 640)], 2 * 512 * 640 * 640, both, w_in
-    )
-    cot_t, terms = kernel_call(
-        grad_kernel,
-        [(640, 512), (4, 2, 128, 640)],
-        2 * 512 * 640 * 640,
-        both,
-        ordered(rest, hidden_terms).reshape(16, 2, 40, 128),
+    odd = lax.axis_index("low").astype(jnp.int32)[None]
+    both = jnp.concatenate([inputs.T, y_cot.T], 0)
+    far = lax.all_gather(both, "high", axis=0)
+    x_other = permute(far[:, :40], COL, 16, 1)
+    cot_other = permute(far[:, 40:], COL, 16, 15)
+    out_w = ordered(w_out.T, far)
+    x_t, cot_t, terms = kernel_call(
+        terms_kernel,
+        [(16, 40, 512), (16, 40, 512), (4, 2, 128, 640)],
+        4 * 512 * 640 * 640,
+        odd,
+        far,
+        x_other,
+        cot_other,
+        w_in,
         out_w,
-        hidden_terms,
-    )
+    )
+    x_t, cot_t = x_t.reshape(640, 512), cot_t.reshape(640, 512)
     got = lax.all_to_all(terms, "row", 0, 0, tiled=True).astype(f32)
     hidden, act_grad = jnp.sum(got[:, 0], axis=0), jnp.sum(got[:, 1], axis=0)
     value, slope = gelu_pair(hidden)
@@ -187,7 +195,7 @@
     (out_terms,) = kernel_call(
         out_kernel, [(16, 2, 40, 512)], 4 * 512 * 640 * 640, out_w, w_in, rows
     )
-    out_got = lax.all_to_all(out_terms, "col", 0, 0, tiled=True)
+    out_got = lax.all_to_all(out_terms, COL, 0, 0, tiled=True)
     y_t, x_grad_t = kernel_call(sum_kernel, [(40, 512)] * 2, 2 * 16 * 40 * 512, out_got)
     mine, other = kernel_call(
         weight_kernel,
@@ -200,25 +208,27 @@
         scratch=[(2, 640, 640)],
     )
     got = lax.ppermute(other, "core", [(0, 1), (1, 0)])
-    half = (mine.astype(f32) + got.astype(f32)).astype(bf16).reshape(640, 640)
-    quarter = scatter_sum_steps(half, "chip", n_chip).astype(bf16)
-    half = gather(quarter, "chip")
-    other = lax.ppermute(half, "core", [(0, 1), (1, 0)])
-    w_in_sum, w_out_sum = kernel_call(join_kernel, [(640, 640)] * 2, 0, core_id, half, other)
+    in_half, out_half = chip_sum(add(mine[0], got[0]), add(mine[1], got[1]))
+    in_other = lax.ppermute(in_half, "core", [(0, 1), (1, 0)])
+    out_other = lax.ppermute(out_half, "core", [(0, 1), (1, 0)])
+    w_in_sum, w_out_sum = kernel_call(
+        join_kernel, [(640, 640)] * 2, 0, core_id, in_half, out_half, in_other, out_other
+    )
     return (y_t.T, x_grad_t.T, w_in_sum, w_out_sum)
 
 
 def solution(mesh):
     shape = mesh.devices.shape
     fine = jax.sharding.Mesh(
-        mesh.devices.reshape(shape[0], shape[1], shape[2] // 2, 2), ("row", "col", "chip", "core")
+        mesh.devices.reshape(shape[0], shape[1] // 2, 2, shape[2] // 2, 2),
+        ("row", "high", "low", "chip", "core"),
     )
     depth = ("chip", "core")
-    acts = P(depth, ("row", "col"))
+    acts = P(depth, ("row",) + COL)
     return jax.shard_map(
         per_device,
         mesh=fine,
-        in_specs=(acts, P("row", "col"), P("col", "row"), acts),
-        out_specs=(acts, acts, P("row", "col"), P("col", "row")),
+        in_specs=(acts, P("row", COL), P(COL, "row"), acts),
+        out_specs=(acts, acts, P("row", COL), P(COL, "row")),
         check_vma=False,
     )

time: 162 us -> 152 us (0.938)
  blocking collectives: 88.3 us -> 69.2 us
  waiting for transfers between devices: 23 us -> 39.4 us
  local copies, waits for them, and re-layouts: 9.4 us -> 3.81 us
  Pallas kernels: 8.98 us -> 7.12 us
    all_gather x2 -> x1, blocking collectives: 54.8 us -> 37.9 us  [per_device(): far = lax.all_gather(both, 'high', axis=0)]
    ppermute x4 -> x8, waiting for transfers between devices: 10 us -> 25.9 us  [the longest x1 9.59 us: chip_sum(): lax.ppermute(out_half, 'chip', ODD)]
    ppermute x4 -> x8, starting transfers between devices: 11.1 us -> 20.1 us  [the longest x2 5.83 us: permute(): lax.ppermute(block, axis, [(i, (i + step) % count) for i in range(count)])]
    all_to_all x2 -> x1, starting transfers between devices: 15.6 us -> 7.09 us  [per_device(): out_got = lax.all_to_all(out_terms, COL, 0, 0, tiled=True)]
    unnamed x23 -> x11, local copies, waits for them, and re-layouts: 9.21 us -> 2.94 us
    all_to_all x1, blocking collectives: 18.6 us -> 16.6 us  [per_device(): got = lax.all_to_all(terms, 'row', 0, 0, tiled=True).astype(f32)]
    pallas_call x7 -> x5, Pallas kernels: 8.98 us -> 7.12 us  [kernel_call(): pl.pallas_call(body, out_shape=shapes, in_specs=[smem if a.dtype == jnp.i...]
    all_to_all x2 -> x1, waiting for transfers between devices: 10.5 us -> 11.2 us  [per_device(): out_got = lax.all_to_all(out_terms, COL, 0, 0, tiled=True)]
  transfers between devices with their start and end apart: 7 -> 10, of which waited for: 7 -> 8; matrix products, arithmetic and copies ran while one was open for 2% -> 2% of each run, Pallas kernels for 3% -> 2%
where the time goes in v5:
time: 152 us
  blocking collectives  69.2 us (46%)
  waiting for transfers between devices  39.4 us (26%)
  starting transfers between devices  29.1 us (19%)
  Pallas kernels  7.12 us (5%)
  local copies, waits for them, and re-layouts  3.81 us (3%)
  other arithmetic  2.01 us (1%)
    all_gather x1, blocking collectives, per_device(): far = lax.all_gather(both, 'high', axis=0)  37.9 us
    all_to_all x1, blocking collectives, per_device(): got = lax.all_to_all(terms, 'row', 0, 0, tiled=True).astype(f32)  16.6 us
    all_to_all x1, blocking collectives, spread(): lax.all_to_all(copies, axis, 0, 0, tiled=True)  14.7 us
    all_to_all x1, waiting for transfers between devices, per_device(): out_got = lax.all_to_all(out_terms, COL, 0, 0, tiled=True)  11.2 us
    ppermute x1, waiting for transfers between devices, chip_sum(): lax.ppermute(out_half, 'chip', ODD)  9.59 us
    pallas_call x5, Pallas kernels, kernel_call(): pl.pallas_call(body, out_shape=shapes, in_specs=[smem if a.dtype == jnp.i...  7.12 us
    all_to_all x1, starting transfers between devices, per_device(): out_got = lax.all_to_all(out_terms, COL, 0, 0, tiled=True)  7.09 us
    ppermute x1, waiting for transfers between devices, chip_sum(): lax.ppermute(out_half, 'chip', EVEN)  7 us
  transfers between devices with their start and end apart: 10, of which 8 were waited for; matrix products, arithmetic and copies ran while one was open for 2% of the time, Pallas kernels for 2%

profile of v5, /device:TPU:24, one launch (start us, length us, event | category | flops | bytes accessed | tf_op | source)
XLA Modules:
  0.0 151.6 jit_solution(5382963519460235057)
XLA Ops:
  1.4 37.9 %all-gather = bf16[640,512]{1,0:T(8,128)(2,1)S(1)} all-gather(bf16[80,512]{1,0:T(8,128)(2,1)S(1)} %pad_maximum_fusion.1), channel_id=2, replica_groups=mesh['row'=4,'high'=8,'low'=2,'chip'=4,'core'=2] {'high'}, dimensions={0}, use_global_device_ids=true | all-gather | bytes 737280 | tf_op jit(solution)/shard_map/all_gather | solution.py:174
  40.1 3.9 %collective-permute-start.1 = (bf16[8,40,512]{2,1,0:T(8,128)(2,1)}, bf16[8,40,512]{2,1,0:T(8,128)(2,1)S(1)}, u32[]{:S(2)}, u32[]{:S(2)}) collective-permute-start(bf16[8,40,512]{2,1,0:T(8,128)(2,1)} %get-tuple-element.28), channel_id=1, source_target_pairs={{0,120},{8,0},{16,8},{24,16},{32,24},{40,32},{48,40},{56,48},{64,5... | collective-permute-start | bytes 983048 | tf_op jit(solution)/shard_map/ppermute | solution.py:79
  44.0 1.9 %collective-permute-start = (bf16[8,40,512]{2,1,0:T(8,128)(2,1)S(1)}, bf16[8,40,512]{2,1,0:T(8,128)(2,1)S(1)}, u32[]{:S(2)}, u32[]{:S(2)}) collective-permute-start(bf16[8,40,512]{2,1,0:T(8,128)(2,1)S(1)} %get-tuple-element.29), channel_id=1, source_target_pairs={{0,8},{8,16},{16,24},{24,32},{32,40},{40,48},{48,56},{56,64},{64,7... | collective-permute-start | bytes 983048 | tf_op jit(solution)/shard_map/ppermute | solution.py:79
  46.0 1.8 %copy.9 = bf16[640,640]{0,1:T(8,128)(2,1)S(1)} copy(bf16[640,640]{1,0:T(8,128)(2,1)} %param.6) | data formatting | bytes 1638400 | tf_op args[2]
  47.8 1.5 collective-permute-done.1.cot_other_ref
  49.3 4.9 %collective-permute-done.x_other_ref = bf16[8,40,512]{2,1,0:T(8,128)(2,1)S(1)} collective-permute-done((bf16[8,40,512]{2,1,0:T(8,128)(2,1)S(1)}, bf16[8,40,512]{2,1,0:T(8,128)(2,1)S(1)}, u32[]{:S(2)}, u32[]{:S(2)}) %collective-permute-start) | collective-permute-done | bytes 327712 | tf_op jit(solution)/shard_map/ppermute | solution.py:79
  54.2 1.4 shard_map.75
  55.6 16.6 %all_to_all.15 = bf16[4,2,128,640]{3,2,1,0:T(8,128)(2,1)S(1)} all-to-all(bf16[4,2,128,640]{3,2,1,0:T(8,128)(2,1)S(1)} %get-tuple-element.15), channel_id=1, replica_groups=mesh['row'=4,'high'=8,'low'=2,'chip'=4,'core'=2] {'row'}, dimensions={0} | all-to-all | bytes 2621440 | tf_op jit(solution)/shard_map/all_to_all | solution.py:190
  73.0 14.7 %all_to_all.16 = bf16[4,1,2,128,640]{4,3,2,1,0:T(8,128)(2,1)S(1)} all-to-all(bf16[4,1,2,128,640]{4,3,2,1,0:T(8,128)(2,1)S(1)} %broadcast_in_dim.12), channel_id=1, replica_groups=mesh['row'=4,'high'=8,'low'=2,'chip'=4,'core'=2] {'row'}, dimensions={0} | all-to-all | bytes 2621440 | tf_op jit(solution)/shard_map/all_to_all | solution.py:60
  87.7 2.3 %shard_map.76 = bf16[16,2,40,512]{3,2,1,0:T(8,128)(2,1)} custom-call(bf16[640,640]{1,0:T(8,128)(2,1)S(1)} %bitcast.32, bf16[640,640]{1,0:T(8,128)(2,1)S(1)} %copy-done, bf16[4,2,128,640]{3,2,1,0:T(8,128)(2,1)S(1)} %bitcast.29), custom_call_target="tpu_custom_call" | custom-call | flops 838860800 | bytes 4259840 | tf_op jit(solution)/shard_map/pallas_call | solution.py:89
  90.0 7.1 %all-to-all-start.2 = ((bf16[16,2,40,512]{3,2,1,0:T(8,128)(2,1)}), bf16[16,2,40,512]{3,2,1,0:T(8,128)(2,1)S(1)}, u32[]{:S(2)}, u32[]{:S(2)}) async-start(bf16[16,2,40,512]{3,2,1,0:T(8,128)(2,1)} %shard_map.76), calls=%async_computation.2 | async-start | bytes 2621440 | tf_op jit(solution)/shard_map/all_to_all | solution.py:198
  98.2 1.3 shard_map.78
  99.5 1.9 %collective-permute-start.2 = (bf16[2,320,640]{2,1,0:T(8,128)(2,1)S(1)}, bf16[2,320,640]{2,1,0:T(8,128)(2,1)S(1)}, u32[]{:S(2)}, u32[]{:S(2)}) collective-permute-start(bf16[2,320,640]{2,1,0:T(8,128)(2,1)S(1)} %get-tuple-element.21), channel_id=1, source_target_pairs={{0,1},{1,0},{2,3},{3,2},{4,5},{5,4},{6,7},{7,6},{8,9},{9,8},{10,11... | collective-permute-start | bytes 2457608 | tf_op jit(solution)/shard_map/ppermute | solution.py:210
  101.4 2.3 %collective-permute-done.2 = bf16[2,320,640]{2,1,0:T(8,128)(2,1)S(1)} collective-permute-done((bf16[2,320,640]{2,1,0:T(8,128)(2,1)S(1)}, bf16[2,320,640]{2,1,0:T(8,128)(2,1)S(1)}, u32[]{:S(2)}, u32[]{:S(2)}) %collective-permute-start.2) | collective-permute-done | bytes 819232 | tf_op jit(solution)/shard_map/ppermute | solution.py:210
  104.0 2.1 %collective-permute-start.5 = (bf16[320,640]{1,0:T(8,128)(2,1)S(1)}, bf16[320,640]{1,0:T(8,128)(2,1)S(1)}, u32[]{:S(2)}, u32[]{:S(2)}) collective-permute-start(bf16[320,640]{1,0:T(8,128)(2,1)S(1)} %get-tuple-element.26), channel_id=1, source_target_pairs={{2,4},{4,2},{6,0},{0,6},{3,5},{5,3},{7,1},{1,7},{10,12},{12,10},{1... | collective-permute-start | bytes 1228808 | tf_op jit(solution)/shard_map/ppermute | solution.py:161
  106.1 2.9 %collective-permute-start.3 = (bf16[320,640]{1,0:T(8,128)(2,1)S(1)}, bf16[320,640]{1,0:T(8,128)(2,1)S(1)}, u32[]{:S(2)}, u32[]{:S(2)}) collective-permute-start(bf16[320,640]{1,0:T(8,128)(2,1)S(1)} %get-tuple-element.27), channel_id=1, source_target_pairs={{0,2},{2,0},{4,6},{6,4},{1,3},{3,1},{5,7},{7,5},{8,10},{10,8},{12,... | collective-permute-start | bytes 1228808 | tf_op jit(solution)/shard_map/ppermute | solution.py:161
  109.0 9.6 %collective-permute-done.5 = bf16[320,640]{1,0:T(8,128)(2,1)S(1)} collective-permute-done((bf16[320,640]{1,0:T(8,128)(2,1)S(1)}, bf16[320,640]{1,0:T(8,128)(2,1)S(1)}, u32[]{:S(2)}, u32[]{:S(2)}) %collective-permute-start.5) | collective-permute-done | bytes 409632 | tf_op jit(solution)/shard_map/ppermute | solution.py:161
  118.7 1.9 %collective-permute-start.6 = (bf16[320,640]{1,0:T(8,128)(2,1)S(1)}, bf16[320,640]{1,0:T(8,128)(2,1)S(1)}, u32[]{:S(2)}, u32[]{:S(2)}) collective-permute-start(bf16[320,640]{1,0:T(8,128)(2,1)S(1)} %add_convert_fusion.1), channel_id=1, source_target_pairs={{0,2},{2,0},{4,6},{6,4},{1,3},{3,1},{5,7},{7,5},{8,10},{10,8},{12,... | collective-permute-start | bytes 1228808 | tf_op jit(solution)/shard_map/ppermute | solution.py:163
  120.7 3.5 %collective-permute-start.4 = (bf16[320,640]{1,0:T(8,128)(2,1)S(1)}, bf16[320,640]{1,0:T(8,128)(2,1)S(1)}, u32[]{:S(2)}, u32[]{:S(2)}) collective-permute-start(bf16[320,640]{1,0:T(8,128)(2,1)S(1)} %add_convert_fusion.4), channel_id=1, source_target_pairs={{2,4},{4,2},{6,0},{0,6},{3,5},{5,3},{7,1},{1,7},{10,12},{12,10},{1... | collective-permute-start | bytes 1228808 | tf_op jit(solution)/shard_map/ppermute | solution.py:163
  124.2 7.0 %collective-permute-done.6 = bf16[320,640]{1,0:T(8,128)(2,1)S(1)} collective-permute-done((bf16[320,640]{1,0:T(8,128)(2,1)S(1)}, bf16[320,640]{1,0:T(8,128)(2,1)S(1)}, u32[]{:S(2)}, u32[]{:S(2)}) %collective-permute-start.6) | collective-permute-done | bytes 409632 | tf_op jit(solution)/shard_map/ppermute | solution.py:163
  131.4 1.9 %collective-permute-start.8 = (bf16[320,640]{1,0:T(8,128)(2,1)S(1)}, bf16[320,640]{1,0:T(8,128)(2,1)S(1)}, u32[]{:S(2)}, u32[]{:S(2)}) collective-permute-start(bf16[320,640]{1,0:T(8,128)(2,1)S(1)} %add_convert_fusion.out_mine_ref), channel_id=1, source_target_pairs={{0,1},{1,0},{2,3},{3,2},{4,5},{5,4},{6,7},{7,6},{8,9},{9,8},{10,11... | collective-permute-start | bytes 1228808 | tf_op jit(solution)/shard_map/ppermute | solution.py:213
  134.6 1.9 %collective-permute-start.7 = (bf16[320,640]{1,0:T(8,128)(2,1)S(1)}, bf16[320,640]{1,0:T(8,128)(2,1)S(1)}, u32[]{:S(2)}, u32[]{:S(2)}) collective-permute-start(bf16[320,640]{1,0:T(8,128)(2,1)S(1)} %add_convert_fusion.3.in_mine_ref), channel_id=1, source_target_pairs={{0,1},{1,0},{2,3},{3,2},{4,5},{5,4},{6,7},{7,6},{8,9},{9,8},{10,11... | collective-permute-start | bytes 1228808 | tf_op jit(solution)/shard_map/ppermute | solution.py:212
  136.6 1.7 %collective-permute-done.7.in_other_ref = bf16[320,640]{1,0:T(8,128)(2,1)S(1)} collective-permute-done((bf16[320,640]{1,0:T(8,128)(2,1)S(1)}, bf16[320,640]{1,0:T(8,128)(2,1)S(1)}, u32[]{:S(2)}, u32[]{:S(2)}) %collective-permute-start.7) | collective-permute-done | bytes 409632 | tf_op jit(solution)/shard_map/ppermute | solution.py:212
  139.5 11.2 %all-to-all-done.2.got_ref = bf16[16,2,40,512]{3,2,1,0:T(8,128)(2,1)S(1)} async-done(((bf16[16,2,40,512]{3,2,1,0:T(8,128)(2,1)}), bf16[16,2,40,512]{3,2,1,0:T(8,128)(2,1)S(1)}, u32[]{:S(2)}, u32[]{:S(2)}) %all-to-all-start.2) | async-done | bytes 1310752 | tf_op jit(solution)/shard_map/all_to_all | solution.py:198
  (27 shorter events, 7.3 us)
Async XLA Ops:
  39.3 14.9 %copy-start = (bf16[640,640]{1,0:T(8,128)(2,1)S(1)}, bf16[640,640]{1,0:T(8,128)(2,1)}, u32[]{:S(2)}) copy-start(bf16[640,640]{1,0:T(8,128)(2,1)} %in_w_ref.3) | copy-start | bytes 2457604
  40.1 9.2 %collective-permute-start.1 = (bf16[8,40,512]{2,1,0:T(8,128)(2,1)}, bf16[8,40,512]{2,1,0:T(8,128)(2,1)S(1)}, u32[]{:S(2)}, u32[]{:S(2)}) collective-permute-start(bf16[8,40,512]{2,1,0:T(8,128)(2,1)} %get-tuple-element.28), channel_id=1, source_target_pairs={{0,120},{8,0},{16,8},{24,16},{32,24},{40,32},{48,40},{56,48},{64,5... | collective-permute-start | bytes 983048 | tf_op jit(solution)/shard_map/ppermute | solution.py:79
  44.0 10.2 %collective-permute-start = (bf16[8,40,512]{2,1,0:T(8,128)(2,1)S(1)}, bf16[8,40,512]{2,1,0:T(8,128)(2,1)S(1)}, u32[]{:S(2)}, u32[]{:S(2)}) collective-permute-start(bf16[8,40,512]{2,1,0:T(8,128)(2,1)S(1)} %get-tuple-element.29), channel_id=1, source_target_pairs={{0,8},{8,16},{16,24},{24,32},{32,40},{40,48},{48,56},{56,64},{64,7... | collective-permute-start | bytes 983048 | tf_op jit(solution)/shard_map/ppermute | solution.py:79
  55.6 16.6 %copy-start.1 = (bf16[16,40,512]{2,1,0:T(8,128)(2,1)}, bf16[16,40,512]{2,1,0:T(8,128)(2,1)S(1)}, u32[]{:S(2)}) copy-start(bf16[16,40,512]{2,1,0:T(8,128)(2,1)S(1)} %get-tuple-element.18) | copy-start | bytes 1966084
  55.6 16.6 %copy-start.3 = (bf16[16,40,512]{2,1,0:T(8,128)(2,1)}, bf16[16,40,512]{2,1,0:T(8,128)(2,1)S(1)}, u32[]{:S(2)}) copy-start(bf16[16,40,512]{2,1,0:T(8,128)(2,1)S(1)} %get-tuple-element.19) | copy-start | bytes 1966084
  90.0 7.1 %copy-start.2 = (bf16[16,40,512]{2,1,0:T(8,128)(2,1)S(1)}, bf16[16,40,512]{2,1,0:T(8,128)(2,1)}, u32[]{:S(2)}) copy-start(bf16[16,40,512]{2,1,0:T(8,128)(2,1)} %copy-done.1) | copy-start | bytes 1966084
  90.0 60.8 %all-to-all-start.2 = ((bf16[16,2,40,512]{3,2,1,0:T(8,128)(2,1)}), bf16[16,2,40,512]{3,2,1,0:T(8,128)(2,1)S(1)}, u32[]{:S(2)}, u32[]{:S(2)}) async-start(bf16[16,2,40,512]{3,2,1,0:T(8,128)(2,1)} %shard_map.76), calls=%async_computation.2 | async-start | bytes 2621440 | tf_op jit(solution)/shard_map/all_to_all | solution.py:198
  97.1 1.1 copy-start.4
  99.5 4.2 %collective-permute-start.2 = (bf16[2,320,640]{2,1,0:T(8,128)(2,1)S(1)}, bf16[2,320,640]{2,1,0:T(8,128)(2,1)S(1)}, u32[]{:S(2)}, u32[]{:S(2)}) collective-permute-start(bf16[2,320,640]{2,1,0:T(8,128)(2,1)S(1)} %get-tuple-element.21), channel_id=1, source_target_pairs={{0,1},{1,0},{2,3},{3,2},{4,5},{5,4},{6,7},{7,6},{8,9},{9,8},{10,11... | collective-permute-start | bytes 2457608 | tf_op jit(solution)/shard_map/ppermute | solution.py:210
  104.0 14.6 %collective-permute-start.5 = (bf16[320,640]{1,0:T(8,128)(2,1)S(1)}, bf16[320,640]{1,0:T(8,128)(2,1)S(1)}, u32[]{:S(2)}, u32[]{:S(2)}) collective-permute-start(bf16[320,640]{1,0:T(8,128)(2,1)S(1)} %get-tuple-element.26), channel_id=1, source_target_pairs={{2,4},{4,2},{6,0},{0,6},{3,5},{5,3},{7,1},{1,7},{10,12},{12,10},{1... | collective-permute-start | bytes 1228808 | tf_op jit(solution)/shard_map/ppermute | solution.py:161
  106.1 14.5 %collective-permute-start.3 = (bf16[320,640]{1,0:T(8,128)(2,1)S(1)}, bf16[320,640]{1,0:T(8,128)(2,1)S(1)}, u32[]{:S(2)}, u32[]{:S(2)}) collective-permute-start(bf16[320,640]{1,0:T(8,128)(2,1)S(1)} %get-tuple-element.27), channel_id=1, source_target_pairs={{0,2},{2,0},{4,6},{6,4},{1,3},{3,1},{5,7},{7,5},{8,10},{10,8},{12,... | collective-permute-start | bytes 1228808 | tf_op jit(solution)/shard_map/ppermute | solution.py:161
  118.7 12.6 %collective-permute-start.6 = (bf16[320,640]{1,0:T(8,128)(2,1)S(1)}, bf16[320,640]{1,0:T(8,128)(2,1)S(1)}, u32[]{:S(2)}, u32[]{:S(2)}) collective-permute-start(bf16[320,640]{1,0:T(8,128)(2,1)S(1)} %add_convert_fusion.1), channel_id=1, source_target_pairs={{0,2},{2,0},{4,6},{6,4},{1,3},{3,1},{5,7},{7,5},{8,10},{10,8},{12,... | collective-permute-start | bytes 1228808 | tf_op jit(solution)/shard_map/ppermute | solution.py:163
  120.7 13.8 %collective-permute-start.4 = (bf16[320,640]{1,0:T(8,128)(2,1)S(1)}, bf16[320,640]{1,0:T(8,128)(2,1)S(1)}, u32[]{:S(2)}, u32[]{:S(2)}) collective-permute-start(bf16[320,640]{1,0:T(8,128)(2,1)S(1)} %add_convert_fusion.4), channel_id=1, source_target_pairs={{2,4},{4,2},{6,0},{0,6},{3,5},{5,3},{7,1},{1,7},{10,12},{12,10},{1... | collective-permute-start | bytes 1228808 | tf_op jit(solution)/shard_map/ppermute | solution.py:163
  131.4 5.2 %collective-permute-start.8 = (bf16[320,640]{1,0:T(8,128)(2,1)S(1)}, bf16[320,640]{1,0:T(8,128)(2,1)S(1)}, u32[]{:S(2)}, u32[]{:S(2)}) collective-permute-start(bf16[320,640]{1,0:T(8,128)(2,1)S(1)} %add_convert_fusion.out_mine_ref), channel_id=1, source_target_pairs={{0,1},{1,0},{2,3},{3,2},{4,5},{5,4},{6,7},{7,6},{8,9},{9,8},{10,11... | collective-permute-start | bytes 1228808 | tf_op jit(solution)/shard_map/ppermute | solution.py:213
  134.6 3.6 %collective-permute-start.7 = (bf16[320,640]{1,0:T(8,128)(2,1)S(1)}, bf16[320,640]{1,0:T(8,128)(2,1)S(1)}, u32[]{:S(2)}, u32[]{:S(2)}) collective-permute-start(bf16[320,640]{1,0:T(8,128)(2,1)S(1)} %add_convert_fusion.3.in_mine_ref), channel_id=1, source_target_pairs={{0,1},{1,0},{2,3},{3,2},{4,5},{5,4},{6,7},{7,6},{8,9},{9,8},{10,11... | collective-permute-start | bytes 1228808 | tf_op jit(solution)/shard_map/ppermute | solution.py:212

commit v6 on v5

--- a/solution.py
+++ b/solution.py
@@ -11,7 +11,10 @@
 gelu_a = 0.044715
 bf16 = jnp.bfloat16
 f32 = jnp.float32
-n_row, n_col, n_chip = 4, 16, 4
+COL = ("high", "low")
+SWAP = [(0, 1), (1, 0)]
+EVEN = [(0, 1), (1, 0), (2, 3), (3, 2)]
+ODD = [(1, 2), (2, 1), (3, 0), (0, 3)]
 
 
 def gelu_pair(h):
@@ -21,62 +24,28 @@
     return value, slope
 
 
-def dot(a, b, spec):
-    return jnp.einsum(spec, a, b, preferred_element_type=f32).astype(bf16)
-
-
-def gather(block, axis):
-    return lax.all_gather(block, axis, axis=0, tiled=True)
-
-
-def scatter_sum(terms, axis, count):
-    blocks = terms.reshape((count, -1) + terms.shape[1:])
-    got = lax.all_to_all(blocks, axis, 0, 0, tiled=True)
-    return jnp.sum(got.astype(f32), axis=0)
-
-
-def scatter_sum_steps(terms, axis, count):
-    blocks = terms.reshape((count, -1) + terms.shape[1:])
-    me = lax.axis_index(axis)
-    total = lax.dynamic_index_in_dim(blocks, me, 0, keepdims=False).astype(f32)
-    for step in (2, 1, 3):
-        block = lax.dynamic_index_in_dim(blocks, lax.rem(me + step, count), 0, keepdims=False)
-        pairs = [(i, (i + step) % count) for i in range(count)]
-        total = total + lax.ppermute(block, axis, pairs).astype(f32)
-    return total
-
-
-def core_half_sum(terms):
-    me = lax.axis_index("core")
-    halves = terms.reshape((2, -1) + terms.shape[1:])
-    mine = lax.dynamic_index_in_dim(halves, me, 0, keepdims=False)
-    other = lax.dynamic_index_in_dim(halves, 1 - me, 0, keepdims=False)
-    got = lax.ppermute(other, "core", [(0, 1), (1, 0)])
-    return (mine.astype(f32) + got.astype(f32)).astype(bf16)
-
-
-def spread(block, axis, count):
-    copies = jnp.broadcast_to(block[None], (count,) + block.shape)
-    return lax.all_to_all(copies, axis, 0, 0, tiled=True).reshape((-1,) + block.shape[1:])
-
-
-def spread_steps(block, axis, count):
-    me = lax.axis_index(axis)
-    rows = jnp.zeros((count,) + block.shape, block.dtype)
-    rows = lax.dynamic_update_index_in_dim(rows, block, me, 0)
-    for step in (2, 1, 3):
-        pairs = [(i, (i + step) % count) for i in range(count)]
-        got = lax.ppermute(block, axis, pairs)
-        rows = lax.dynamic_update_index_in_dim(rows, got, lax.rem(me - step + count, count), 0)
-    return rows.reshape((-1,) + block.shape[1:])
-
-
 def ordered(value, earlier):
     return lax.optimization_barrier((value, earlier))[0]
 
 
 def permute(block, axis, count, step):
     return lax.ppermute(block, axis, [(i, (i + step) % count) for i in range(count)])
+
+
+def spread(block, axis, count):
+    copies = jnp.broadcast_to(block[None], (count,) + block.shape)
+    return lax.all_to_all(copies, axis, 0, 0, tiled=True)
+
+
+def add(a, b):
+    return (a.astype(f32) + b.astype(f32)).astype(bf16)
+
+
+def chip_sum(in_half, out_half):
+    in_got, out_got = lax.ppermute(in_half, "chip", EVEN), lax.ppermute(out_half, "chip", ODD)
+    in_half, out_half = add(in_half, in_got), add(out_half, out_got)
+    in_got, out_got = lax.ppermute(in_half, "chip", ODD), lax.ppermute(out_half, "chip", EVEN)
+    return add(in_half, in_got), add(out_half, out_got)
 
 
 vmem = pl.BlockSpec(memory_space=pltpu.VMEM)
@@ -102,7 +71,7 @@
 
 
 def terms_kernel(
-    odd_ref, own_ref, x_other_ref, cot_other_ref, in_w_ref, out_w_ref, x_ref, cot_ref, terms_ref
+    odd_ref, own_ref, cot_other_ref, x_other_ref, in_w_ref, out_w_ref, x_ref, cot_ref, terms_ref
 ):
     odd = odd_ref[0]
     for stream, other_ref, weight_ref, whole_ref in (
@@ -149,24 +118,6 @@
     out_ref[other] = out_other_ref[...]
 
 
-def add(a, b):
-    return (a.astype(f32) + b.astype(f32)).astype(bf16)
-
-
-EVEN = [(0, 1), (1, 0), (2, 3), (3, 2)]
-ODD = [(1, 2), (2, 1), (3, 0), (0, 3)]
-
-
-def chip_sum(in_half, out_half):
-    in_got, out_got = lax.ppermute(in_half, "chip", EVEN), lax.ppermute(out_half, "chip", ODD)
-    in_half, out_half = add(in_half, in_got), add(out_half, out_got)
-    in_got, out_got = lax.ppermute(in_half, "chip", ODD), lax.ppermute(out_half, "chip", EVEN)
-    return add(in_half, in_got), add(out_half, out_got)
-
-
-COL = ("high", "low")
-
-
 def per_device(inputs, w_in, w_out, y_cot):
     core_id = lax.axis_index("core").astype(jnp.int32)[None]
     odd = lax.axis_index("low").astype(jnp.int32)[None]
@@ -181,8 +132,8 @@
         4 * 512 * 640 * 640,
         odd,
         far,
+        cot_other,
         x_other,
-        cot_other,
         w_in,
         out_w,
     )
@@ -191,9 +142,14 @@
     hidden, act_grad = jnp.sum(got[:, 0], axis=0), jnp.sum(got[:, 1], axis=0)
     value, slope = gelu_pair(hidden)
     pair = jnp.stack([value.astype(bf16), (act_grad * slope).astype(bf16)])
-    rows = spread(pair[None], "row", n_row)
+    rows = spread(pair, "row", 4)
     (out_terms,) = kernel_call(
-        out_kernel, [(16, 2, 40, 512)], 4 * 512 * 640 * 640, out_w, w_in, rows
+        out_kernel,
+        [(16, 2, 40, 512)],
+        4 * 512 * 640 * 640,
+        out_w,
+        w_in,
+        rows,
     )
     out_got = lax.all_to_all(out_terms, COL, 0, 0, tiled=True)
     y_t, x_grad_t = kernel_call(sum_kernel, [(40, 512)] * 2, 2 * 16 * 40 * 512, out_got)
@@ -207,10 +163,10 @@
         rows,
         scratch=[(2, 640, 640)],
     )
-    got = lax.ppermute(other, "core", [(0, 1), (1, 0)])
+    got = lax.ppermute(other, "core", SWAP)
     in_half, out_half = chip_sum(add(mine[0], got[0]), add(mine[1], got[1]))
-    in_other = lax.ppermute(in_half, "core", [(0, 1), (1, 0)])
-    out_other = lax.ppermute(out_half, "core", [(0, 1), (1, 0)])
+    in_other = lax.ppermute(in_half, "core", SWAP)
+    out_other = lax.ppermute(out_half, "core", SWAP)
     w_in_sum, w_out_sum = kernel_call(
         join_kernel, [(640, 640)] * 2, 0, core_id, in_half, out_half, in_other, out_other
     )

time: 152 us -> 151 us (level)
  waiting for transfers between devices: 39.4 us -> 35.7 us
  starting transfers between devices: 29.1 us -> 31.7 us
    ppermute x2, waiting for transfers between devices: 6.39 us -> 3.01 us  [permute(): lax.ppermute(block, axis, [(i, (i + step) % count) for i in range(count)])]
where the time goes in v6:
time: 151 us; the launch traced here: 150 us
  blocking collectives  69 us (46%)
  waiting for transfers between devices  35.7 us (24%)
  starting transfers between devices  31.7 us (21%)
  Pallas kernels  7.12 us (5%)
  local copies, waits for them, and re-layouts  3.81 us (3%)
  other arithmetic  2.01 us (1%)
    all_gather x1, blocking collectives, per_device(): far = lax.all_gather(both, 'high', axis=0)  37.9 us
    all_to_all x1, blocking collectives, per_device(): got = lax.all_to_all(terms, 'row', 0, 0, tiled=True).astype(f32)  16.4 us
    all_to_all x1, blocking collectives, spread(): return lax.all_to_all(copies, axis, 0, 0, tiled=True)  14.7 us
    all_to_all x1, waiting for transfers between devices, per_device(): out_got = lax.all_to_all(out_terms, COL, 0, 0, tiled=True)  10.9 us
    ppermute x1, waiting for transfers between devices, chip_sum(): lax.ppermute(out_half, 'chip', ODD)  9.59 us
    all_to_all x1, starting transfers between devices, per_device(): out_got = lax.all_to_all(out_terms, COL, 0, 0, tiled=True)  8.42 us
    pallas_call x5, Pallas kernels, kernel_call(): pl.pallas_call(body, out_shape=shapes, in_specs=[smem if a.dtype == jnp.i...  7.12 us
    ppermute x2, starting transfers between devices, permute(): lax.ppermute(block, axis, [(i, (i + step) % count) for i in range(count)])  7.04 us
  transfers between devices with their start and end apart: 10, of which 8 were waited for; matrix products, arithmetic and copies ran while one was open for 2% of the time, Pallas kernels for 2%

profile of v6, /device:TPU:24, one launch (start us, length us, event | category | flops | bytes accessed | tf_op | source)
XLA Modules:
  0.0 150.2 jit_solution(2941127033837121977)
XLA Ops:
  1.4 37.9 %all-gather = bf16[640,512]{1,0:T(8,128)(2,1)S(1)} all-gather(bf16[80,512]{1,0:T(8,128)(2,1)S(1)} %pad_maximum_fusion.1), channel_id=2, replica_groups=mesh['row'=4,'high'=8,'low'=2,'chip'=4,'core'=2] {'high'}, dimensions={0}, use_global_device_ids=true | all-gather | bytes 737280 | tf_op jit(solution)/shard_map/all_gather | solution.py:125
  40.1 2.9 %collective-permute-start.1 = (bf16[8,40,512]{2,1,0:T(8,128)(2,1)}, bf16[8,40,512]{2,1,0:T(8,128)(2,1)S(1)}, u32[]{:S(2)}, u32[]{:S(2)}) collective-permute-start(bf16[8,40,512]{2,1,0:T(8,128)(2,1)} %get-tuple-element.28), channel_id=1, source_target_pairs={{0,8},{8,16},{16,24},{24,32},{32,40},{40,48},{48,56},{56,64},{64,7... | collective-permute-start | bytes 983048 | tf_op jit(solution)/shard_map/ppermute | solution.py:32
  43.0 4.1 %collective-permute-start = (bf16[8,40,512]{2,1,0:T(8,128)(2,1)S(1)}, bf16[8,40,512]{2,1,0:T(8,128)(2,1)S(1)}, u32[]{:S(2)}, u32[]{:S(2)}) collective-permute-start(bf16[8,40,512]{2,1,0:T(8,128)(2,1)S(1)} %get-tuple-element.29), channel_id=1, source_target_pairs={{0,120},{8,0},{16,8},{24,16},{32,24},{40,32},{48,40},{56,48},{64,5... | collective-permute-start | bytes 983048 | tf_op jit(solution)/shard_map/ppermute | solution.py:32
  47.2 1.8 %copy.8 = bf16[640,640]{0,1:T(8,128)(2,1)S(1)} copy(bf16[640,640]{1,0:T(8,128)(2,1)} %param.6) | data formatting | bytes 1638400 | tf_op args[2]
  49.0 1.5 collective-permute-done.1.x_other_ref
  50.5 1.5 %collective-permute-done.cot_other_ref = bf16[8,40,512]{2,1,0:T(8,128)(2,1)S(1)} collective-permute-done((bf16[8,40,512]{2,1,0:T(8,128)(2,1)S(1)}, bf16[8,40,512]{2,1,0:T(8,128)(2,1)S(1)}, u32[]{:S(2)}, u32[]{:S(2)}) %collective-permute-start) | collective-permute-done | bytes 327712 | tf_op jit(solution)/shard_map/ppermute | solution.py:32
  52.0 1.4 shard_map.75
  53.5 16.4 %all_to_all.15 = bf16[4,2,128,640]{3,2,1,0:T(8,128)(2,1)S(1)} all-to-all(bf16[4,2,128,640]{3,2,1,0:T(8,128)(2,1)S(1)} %get-tuple-element.15), channel_id=1, replica_groups=mesh['row'=4,'high'=8,'low'=2,'chip'=4,'core'=2] {'row'}, dimensions={0} | all-to-all | bytes 2621440 | tf_op jit(solution)/shard_map/all_to_all | solution.py:141
  70.6 14.7 %all_to_all.16.rows_ref = bf16[4,2,128,640]{3,2,1,0:T(8,128)(2,1)S(1)} all-to-all(bf16[4,2,128,640]{3,2,1,0:T(8,128)(2,1)S(1)} %broadcast_in_dim.13), channel_id=1, replica_groups=mesh['row'=4,'high'=8,'low'=2,'chip'=4,'core'=2] {'row'}, dimensions={0} | all-to-all | bytes 2621440 | tf_op jit(solution)/shard_map/all_to_all | solution.py:37
  85.3 2.3 %shard_map.76 = bf16[16,2,40,512]{3,2,1,0:T(8,128)(2,1)} custom-call(bf16[640,640]{1,0:T(8,128)(2,1)S(1)} %bitcast.29, bf16[640,640]{1,0:T(8,128)(2,1)S(1)} %copy-done, bf16[4,2,128,640]{3,2,1,0:T(8,128)(2,1)S(1)} %all_to_all.16.rows_ref), custom_call_target="tpu_custom_call" | custom-call | flops 838860800 | bytes 4259840 | tf_op jit(solution)/shard_map/pallas_call | solution.py:58
  87.6 8.4 %all-to-all-start.2 = ((bf16[16,2,40,512]{3,2,1,0:T(8,128)(2,1)}), bf16[16,2,40,512]{3,2,1,0:T(8,128)(2,1)S(1)}, u32[]{:S(2)}, u32[]{:S(2)}) async-start(bf16[16,2,40,512]{3,2,1,0:T(8,128)(2,1)} %shard_map.76), calls=%async_computation.2 | async-start | bytes 2621440 | tf_op jit(solution)/shard_map/all_to_all | solution.py:154
  97.2 1.3 shard_map.78
  98.5 1.9 %collective-permute-start.2 = (bf16[2,320,640]{2,1,0:T(8,128)(2,1)S(1)}, bf16[2,320,640]{2,1,0:T(8,128)(2,1)S(1)}, u32[]{:S(2)}, u32[]{:S(2)}) collective-permute-start(bf16[2,320,640]{2,1,0:T(8,128)(2,1)S(1)} %get-tuple-element.21), channel_id=1, source_target_pairs={{0,1},{1,0},{2,3},{3,2},{4,5},{5,4},{6,7},{7,6},{8,9},{9,8},{10,11... | collective-permute-start | bytes 2457608 | tf_op jit(solution)/shard_map/ppermute | solution.py:166
  100.4 2.3 %collective-permute-done.2 = bf16[2,320,640]{2,1,0:T(8,128)(2,1)S(1)} collective-permute-done((bf16[2,320,640]{2,1,0:T(8,128)(2,1)S(1)}, bf16[2,320,640]{2,1,0:T(8,128)(2,1)S(1)}, u32[]{:S(2)}, u32[]{:S(2)}) %collective-permute-start.2) | collective-permute-done | bytes 819232 | tf_op jit(solution)/shard_map/ppermute | solution.py:166
  102.9 2.1 %collective-permute-start.5 = (bf16[320,640]{1,0:T(8,128)(2,1)S(1)}, bf16[320,640]{1,0:T(8,128)(2,1)S(1)}, u32[]{:S(2)}, u32[]{:S(2)}) collective-permute-start(bf16[320,640]{1,0:T(8,128)(2,1)S(1)} %get-tuple-element.26), channel_id=1, source_target_pairs={{2,4},{4,2},{6,0},{0,6},{3,5},{5,3},{7,1},{1,7},{10,12},{12,10},{1... | collective-permute-start | bytes 1228808 | tf_op jit(solution)/shard_map/ppermute | solution.py:45
  105.1 2.9 %collective-permute-start.3 = (bf16[320,640]{1,0:T(8,128)(2,1)S(1)}, bf16[320,640]{1,0:T(8,128)(2,1)S(1)}, u32[]{:S(2)}, u32[]{:S(2)}) collective-permute-start(bf16[320,640]{1,0:T(8,128)(2,1)S(1)} %get-tuple-element.27), channel_id=1, source_target_pairs={{0,2},{2,0},{4,6},{6,4},{1,3},{3,1},{5,7},{7,5},{8,10},{10,8},{12,... | collective-permute-start | bytes 1228808 | tf_op jit(solution)/shard_map/ppermute | solution.py:45
  108.0 9.6 %collective-permute-done.5 = bf16[320,640]{1,0:T(8,128)(2,1)S(1)} collective-permute-done((bf16[320,640]{1,0:T(8,128)(2,1)S(1)}, bf16[320,640]{1,0:T(8,128)(2,1)S(1)}, u32[]{:S(2)}, u32[]{:S(2)}) %collective-permute-start.5) | collective-permute-done | bytes 409632 | tf_op jit(solution)/shard_map/ppermute | solution.py:45
  117.6 1.9 %collective-permute-start.6 = (bf16[320,640]{1,0:T(8,128)(2,1)S(1)}, bf16[320,640]{1,0:T(8,128)(2,1)S(1)}, u32[]{:S(2)}, u32[]{:S(2)}) collective-permute-start(bf16[320,640]{1,0:T(8,128)(2,1)S(1)} %add_convert_fusion.1), channel_id=1, source_target_pairs={{0,2},{2,0},{4,6},{6,4},{1,3},{3,1},{5,7},{7,5},{8,10},{10,8},{12,... | collective-permute-start | bytes 1228808 | tf_op jit(solution)/shard_map/ppermute | solution.py:47
  119.7 3.5 %collective-permute-start.4 = (bf16[320,640]{1,0:T(8,128)(2,1)S(1)}, bf16[320,640]{1,0:T(8,128)(2,1)S(1)}, u32[]{:S(2)}, u32[]{:S(2)}) collective-permute-start(bf16[320,640]{1,0:T(8,128)(2,1)S(1)} %add_convert_fusion.4), channel_id=1, source_target_pairs={{2,4},{4,2},{6,0},{0,6},{3,5},{5,3},{7,1},{1,7},{10,12},{12,10},{1... | collective-permute-start | bytes 1228808 | tf_op jit(solution)/shard_map/ppermute | solution.py:47
  123.2 7.0 %collective-permute-done.6 = bf16[320,640]{1,0:T(8,128)(2,1)S(1)} collective-permute-done((bf16[320,640]{1,0:T(8,128)(2,1)S(1)}, bf16[320,640]{1,0:T(8,128)(2,1)S(1)}, u32[]{:S(2)}, u32[]{:S(2)}) %collective-permute-start.6) | collective-permute-done | bytes 409632 | tf_op jit(solution)/shard_map/ppermute | solution.py:47
  130.3 1.9 %collective-permute-start.8 = (bf16[320,640]{1,0:T(8,128)(2,1)S(1)}, bf16[320,640]{1,0:T(8,128)(2,1)S(1)}, u32[]{:S(2)}, u32[]{:S(2)}) collective-permute-start(bf16[320,640]{1,0:T(8,128)(2,1)S(1)} %add_convert_fusion.out_mine_ref), channel_id=1, source_target_pairs={{0,1},{1,0},{2,3},{3,2},{4,5},{5,4},{6,7},{7,6},{8,9},{9,8},{10,11... | collective-permute-start | bytes 1228808 | tf_op jit(solution)/shard_map/ppermute | solution.py:169
  133.6 1.9 %collective-permute-start.7 = (bf16[320,640]{1,0:T(8,128)(2,1)S(1)}, bf16[320,640]{1,0:T(8,128)(2,1)S(1)}, u32[]{:S(2)}, u32[]{:S(2)}) collective-permute-start(bf16[320,640]{1,0:T(8,128)(2,1)S(1)} %add_convert_fusion.3.in_mine_ref), channel_id=1, source_target_pairs={{0,1},{1,0},{2,3},{3,2},{4,5},{5,4},{6,7},{7,6},{8,9},{9,8},{10,11... | collective-permute-start | bytes 1228808 | tf_op jit(solution)/shard_map/ppermute | solution.py:168
  135.5 1.7 %collective-permute-done.7.in_other_ref = bf16[320,640]{1,0:T(8,128)(2,1)S(1)} collective-permute-done((bf16[320,640]{1,0:T(8,128)(2,1)S(1)}, bf16[320,640]{1,0:T(8,128)(2,1)S(1)}, u32[]{:S(2)}, u32[]{:S(2)}) %collective-permute-start.7) | collective-permute-done | bytes 409632 | tf_op jit(solution)/shard_map/ppermute | solution.py:168
  138.5 10.9 %all-to-all-done.2.got_ref = bf16[16,2,40,512]{3,2,1,0:T(8,128)(2,1)S(1)} async-done(((bf16[16,2,40,512]{3,2,1,0:T(8,128)(2,1)}), bf16[16,2,40,512]{3,2,1,0:T(8,128)(2,1)S(1)}, u32[]{:S(2)}, u32[]{:S(2)}) %all-to-all-start.2) | async-done | bytes 1310752 | tf_op jit(solution)/shard_map/all_to_all | solution.py:154
  (27 shorter events, 7.3 us)
Async XLA Ops:
  39.3 12.7 %copy-start = (bf16[640,640]{1,0:T(8,128)(2,1)S(1)}, bf16[640,640]{1,0:T(8,128)(2,1)}, u32[]{:S(2)}) copy-start(bf16[640,640]{1,0:T(8,128)(2,1)} %in_w_ref.3) | copy-start | bytes 2457604
  40.1 10.4 %collective-permute-start.1 = (bf16[8,40,512]{2,1,0:T(8,128)(2,1)}, bf16[8,40,512]{2,1,0:T(8,128)(2,1)S(1)}, u32[]{:S(2)}, u32[]{:S(2)}) collective-permute-start(bf16[8,40,512]{2,1,0:T(8,128)(2,1)} %get-tuple-element.28), channel_id=1, source_target_pairs={{0,8},{8,16},{16,24},{24,32},{32,40},{40,48},{48,56},{56,64},{64,7... | collective-permute-start | bytes 983048 | tf_op jit(solution)/shard_map/ppermute | solution.py:32
  43.0 9.0 %collective-permute-start = (bf16[8,40,512]{2,1,0:T(8,128)(2,1)S(1)}, bf16[8,40,512]{2,1,0:T(8,128)(2,1)S(1)}, u32[]{:S(2)}, u32[]{:S(2)}) collective-permute-start(bf16[8,40,512]{2,1,0:T(8,128)(2,1)S(1)} %get-tuple-element.29), channel_id=1, source_target_pairs={{0,120},{8,0},{16,8},{24,16},{32,24},{40,32},{48,40},{56,48},{64,5... | collective-permute-start | bytes 983048 | tf_op jit(solution)/shard_map/ppermute | solution.py:32
  53.5 16.4 %copy-start.1 = (bf16[16,40,512]{2,1,0:T(8,128)(2,1)}, bf16[16,40,512]{2,1,0:T(8,128)(2,1)S(1)}, u32[]{:S(2)}) copy-start(bf16[16,40,512]{2,1,0:T(8,128)(2,1)S(1)} %get-tuple-element.18) | copy-start | bytes 1966084
  53.5 16.4 %copy-start.3 = (bf16[16,40,512]{2,1,0:T(8,128)(2,1)}, bf16[16,40,512]{2,1,0:T(8,128)(2,1)S(1)}, u32[]{:S(2)}) copy-start(bf16[16,40,512]{2,1,0:T(8,128)(2,1)S(1)} %get-tuple-element.19) | copy-start | bytes 1966084
  87.6 8.4 %copy-start.2 = (bf16[16,40,512]{2,1,0:T(8,128)(2,1)S(1)}, bf16[16,40,512]{2,1,0:T(8,128)(2,1)}, u32[]{:S(2)}) copy-start(bf16[16,40,512]{2,1,0:T(8,128)(2,1)} %copy-done.1) | copy-start | bytes 1966084
  87.6 61.7 %all-to-all-start.2 = ((bf16[16,2,40,512]{3,2,1,0:T(8,128)(2,1)}), bf16[16,2,40,512]{3,2,1,0:T(8,128)(2,1)S(1)}, u32[]{:S(2)}, u32[]{:S(2)}) async-start(bf16[16,2,40,512]{3,2,1,0:T(8,128)(2,1)} %shard_map.76), calls=%async_computation.2 | async-start | bytes 2621440 | tf_op jit(solution)/shard_map/all_to_all | solution.py:154
  96.1 1.1 copy-start.4
  98.5 4.2 %collective-permute-start.2 = (bf16[2,320,640]{2,1,0:T(8,128)(2,1)S(1)}, bf16[2,320,640]{2,1,0:T(8,128)(2,1)S(1)}, u32[]{:S(2)}, u32[]{:S(2)}) collective-permute-start(bf16[2,320,640]{2,1,0:T(8,128)(2,1)S(1)} %get-tuple-element.21), channel_id=1, source_target_pairs={{0,1},{1,0},{2,3},{3,2},{4,5},{5,4},{6,7},{7,6},{8,9},{9,8},{10,11... | collective-permute-start | bytes 2457608 | tf_op jit(solution)/shard_map/ppermute | solution.py:166
  102.9 14.6 %collective-permute-start.5 = (bf16[320,640]{1,0:T(8,128)(2,1)S(1)}, bf16[320,640]{1,0:T(8,128)(2,1)S(1)}, u32[]{:S(2)}, u32[]{:S(2)}) collective-permute-start(bf16[320,640]{1,0:T(8,128)(2,1)S(1)} %get-tuple-element.26), channel_id=1, source_target_pairs={{2,4},{4,2},{6,0},{0,6},{3,5},{5,3},{7,1},{1,7},{10,12},{12,10},{1... | collective-permute-start | bytes 1228808 | tf_op jit(solution)/shard_map/ppermute | solution.py:45
  105.1 14.5 %collective-permute-start.3 = (bf16[320,640]{1,0:T(8,128)(2,1)S(1)}, bf16[320,640]{1,0:T(8,128)(2,1)S(1)}, u32[]{:S(2)}, u32[]{:S(2)}) collective-permute-start(bf16[320,640]{1,0:T(8,128)(2,1)S(1)} %get-tuple-element.27), channel_id=1, source_target_pairs={{0,2},{2,0},{4,6},{6,4},{1,3},{3,1},{5,7},{7,5},{8,10},{10,8},{12,... | collective-permute-start | bytes 1228808 | tf_op jit(solution)/shard_map/ppermute | solution.py:45
  117.6 12.6 %collective-permute-start.6 = (bf16[320,640]{1,0:T(8,128)(2,1)S(1)}, bf16[320,640]{1,0:T(8,128)(2,1)S(1)}, u32[]{:S(2)}, u32[]{:S(2)}) collective-permute-start(bf16[320,640]{1,0:T(8,128)(2,1)S(1)} %add_convert_fusion.1), channel_id=1, source_target_pairs={{0,2},{2,0},{4,6},{6,4},{1,3},{3,1},{5,7},{7,5},{8,10},{10,8},{12,... | collective-permute-start | bytes 1228808 | tf_op jit(solution)/shard_map/ppermute | solution.py:47
  119.7 13.8 %collective-permute-start.4 = (bf16[320,640]{1,0:T(8,128)(2,1)S(1)}, bf16[320,640]{1,0:T(8,128)(2,1)S(1)}, u32[]{:S(2)}, u32[]{:S(2)}) collective-permute-start(bf16[320,640]{1,0:T(8,128)(2,1)S(1)} %add_convert_fusion.4), channel_id=1, source_target_pairs={{2,4},{4,2},{6,0},{0,6},{3,5},{5,3},{7,1},{1,7},{10,12},{12,10},{1... | collective-permute-start | bytes 1228808 | tf_op jit(solution)/shard_map/ppermute | solution.py:47
  130.3 5.2 %collective-permute-start.8 = (bf16[320,640]{1,0:T(8,128)(2,1)S(1)}, bf16[320,640]{1,0:T(8,128)(2,1)S(1)}, u32[]{:S(2)}, u32[]{:S(2)}) collective-permute-start(bf16[320,640]{1,0:T(8,128)(2,1)S(1)} %add_convert_fusion.out_mine_ref), channel_id=1, source_target_pairs={{0,1},{1,0},{2,3},{3,2},{4,5},{5,4},{6,7},{7,6},{8,9},{9,8},{10,11... | collective-permute-start | bytes 1228808 | tf_op jit(solution)/shard_map/ppermute | solution.py:169
  133.6 3.6 %collective-permute-start.7 = (bf16[320,640]{1,0:T(8,128)(2,1)S(1)}, bf16[320,640]{1,0:T(8,128)(2,1)S(1)}, u32[]{:S(2)}, u32[]{:S(2)}) collective-permute-start(bf16[320,640]{1,0:T(8,128)(2,1)S(1)} %add_convert_fusion.3.in_mine_ref), channel_id=1, source_target_pairs={{0,1},{1,0},{2,3},{3,2},{4,5},{5,4},{6,7},{7,6},{8,9},{9,8},{10,11... | collective-permute-start | bytes 1228808 | tf_op jit(solution)/shard_map/ppermute | solution.py:168

commit v7 on v6

--- a/solution.py
+++ b/solution.py
@@ -32,11 +32,6 @@
     return lax.ppermute(block, axis, [(i, (i + step) % count) for i in range(count)])
 
 
-def spread(block, axis, count):
-    copies = jnp.broadcast_to(block[None], (count,) + block.shape)
-    return lax.all_to_all(copies, axis, 0, 0, tiled=True)
-
-
 def add(a, b):
     return (a.astype(f32) + b.astype(f32)).astype(bf16)
 
@@ -52,17 +47,18 @@
 smem = pl.BlockSpec(memory_space=pltpu.SMEM)
 
 
-def kernel_call(body, outs, flops, *args, scratch=()):
+def kernel_call(body, outs, flops, *args, scratch=(), copies=0, limit=32):
     shapes = tuple(jax.ShapeDtypeStruct(shape, bf16) for shape in outs)
     moved = sum(2 * math.prod(a.shape) for a in args) + sum(2 * math.prod(s) for s in outs)
     return pl.pallas_call(
         body,
         out_shape=shapes,
         in_specs=[smem if a.dtype == jnp.int32 else vmem for a in args],
-        out_specs=(vmem,) * len(shapes),
-        scratch_shapes=[pltpu.VMEM(shape, bf16) for shape in scratch],
+        out_specs=(pl.BlockSpec(memory_space=pl.ANY) if copies else vmem,) * len(shapes),
+        scratch_shapes=[pltpu.VMEM(shape, bf16) for shape in scratch]
+        + [pltpu.SemaphoreType.DMA] * copies,
         cost_estimate=pl.CostEstimate(flops=flops, bytes_accessed=moved, transcendentals=0),
-        compiler_params=pltpu.CompilerParams(vmem_limit_bytes=32 * 1024 * 1024),
+        compiler_params=pltpu.CompilerParams(vmem_limit_bytes=limit * 1024 * 1024),
     )(*args)
 
 
@@ -84,11 +80,30 @@
         terms_ref[:, stream] = terms.astype(bf16).reshape(4, 128, 640)
 
 
-def out_kernel(out_w_ref, in_w_ref, rows_ref, terms_ref):
-    for stream, weight_ref in ((0, out_w_ref), (1, in_w_ref)):
-        rows = rows_ref[:, stream].reshape(512, 640)
-        terms = contract(weight_ref[...], rows, 1, 1)
-        terms_ref[:, stream] = terms.astype(bf16).reshape(16, 40, 512)
+def gelu_kernel(got_ref, rows_ref):
+    hidden, act_grad = got_ref[0, 0].astype(f32), got_ref[0, 1].astype(f32)
+    for source in range(1, 4):
+        hidden = hidden + got_ref[source, 0].astype(f32)
+        act_grad = act_grad + got_ref[source, 1].astype(f32)
+    value, slope = gelu_pair(hidden)
+    act, hidden_grad = value.astype(bf16), (act_grad * slope).astype(bf16)
+    for target in range(4):
+        rows_ref[target, 0] = act
+        rows_ref[target, 1] = hidden_grad
+
+
+def out_kernel(out_w_ref, in_w_ref, rows_ref, terms_ref, *parts):
+    copies = []
+    for number, (part_ref, sem) in enumerate(zip(parts[:4], parts[4:])):
+        stream, half = divmod(number, 2)
+        weight = (out_w_ref, in_w_ref)[stream][half * 320 : (half + 1) * 320]
+        terms = contract(weight, rows_ref[:, stream].reshape(512, 640), 1, 1)
+        part_ref[...] = terms.astype(bf16).reshape(8, 40, 512)
+        place = terms_ref.at[half * 8 : (half + 1) * 8, stream]
+        copies.append(pltpu.make_async_copy(part_ref, place, sem))
+        copies[-1].start()
+    for copy in copies:
+        copy.wait()
 
 
 def weight_kernel(core_ref, x_ref, cot_ref, rows_ref, mine_ref, other_ref, whole_ref):
@@ -138,11 +153,9 @@
         out_w,
     )
     x_t, cot_t = x_t.reshape(640, 512), cot_t.reshape(640, 512)
-    got = lax.all_to_all(terms, "row", 0, 0, tiled=True).astype(f32)
-    hidden, act_grad = jnp.sum(got[:, 0], axis=0), jnp.sum(got[:, 1], axis=0)
-    value, slope = gelu_pair(hidden)
-    pair = jnp.stack([value.astype(bf16), (act_grad * slope).astype(bf16)])
-    rows = spread(pair, "row", 4)
+    got = lax.all_to_all(terms, "row", 0, 0, tiled=True)
+    (copies,) = kernel_call(gelu_kernel, [(4, 2, 128, 640)], 30 * 128 * 640, got, limit=8)
+    rows = lax.all_to_all(copies, "row", 0, 0, tiled=True)
     (out_terms,) = kernel_call(
         out_kernel,
         [(16, 2, 40, 512)],
@@ -150,6 +163,8 @@
         out_w,
         w_in,
         rows,
+        scratch=[(8, 40, 512)] * 4,
+        copies=4,
     )
     out_got = lax.all_to_all(out_terms, COL, 0, 0, tiled=True)
     y_t, x_grad_t = kernel_call(sum_kernel, [(40, 512)] * 2, 2 * 16 * 40 * 512, out_got)

time: 151 us -> 151 us (level)
    pallas_call x5 -> x6, Pallas kernels: 7.12 us -> 7.27 us  [kernel_call(): pl.pallas_call(body, out_shape=shapes, in_specs=[smem if a.dtype == jnp.i...]
where the time goes in v7:
time: 151 us; the launch traced here: 150 us
  blocking collectives  69.2 us (46%)
  waiting for transfers between devices  35.8 us (24%)
  starting transfers between devices  31.7 us (21%)
  Pallas kernels  7.27 us (5%)
  local copies, waits for them, and re-layouts  3.71 us (2%)
    all_gather x1, blocking collectives, per_device(): far = lax.all_gather(both, 'high', axis=0)  37.9 us
    all_to_all x1, blocking collectives, per_device(): got = lax.all_to_all(terms, 'row', 0, 0, tiled=True)  16.6 us
    all_to_all x1, blocking collectives, per_device(): rows = lax.all_to_all(copies, 'row', 0, 0, tiled=True)  14.7 us
    all_to_all x1, waiting for transfers between devices, per_device(): out_got = lax.all_to_all(out_terms, COL, 0, 0, tiled=True)  10.9 us
    ppermute x1, waiting for transfers between devices, chip_sum(): lax.ppermute(out_half, 'chip', ODD)  9.59 us
    all_to_all x1, starting transfers between devices, per_device(): out_got = lax.all_to_all(out_terms, COL, 0, 0, tiled=True)  8.49 us
    pallas_call x6, Pallas kernels, kernel_call(): pl.pallas_call(body, out_shape=shapes, in_specs=[smem if a.dtype == jnp.i...  7.27 us
    ppermute x2, starting transfers between devices, permute(): lax.ppermute(block, axis, [(i, (i + step) % count) for i in range(count)])  7.04 us
  transfers between devices with their start and end apart: 10, of which 8 were waited for; matrix products, arithmetic and copies ran while one was open for 2% of the time, Pallas kernels for 2%

profile of v7, /device:TPU:24, one launch (start us, length us, event | category | flops | bytes accessed | tf_op | source)
XLA Modules:
  0.0 150.0 jit_solution(9888625136517612600)
XLA Ops:
  1.4 37.9 %all-gather = bf16[640,512]{1,0:T(8,128)(2,1)S(1)} all-gather(bf16[80,512]{1,0:T(8,128)(2,1)S(1)} %pad_maximum_fusion), channel_id=2, replica_groups=mesh['row'=4,'high'=8,'low'=2,'chip'=4,'core'=2] {'high'}, dimensions={0}, use_global_device_ids=true | all-gather | bytes 737280 | tf_op jit(solution)/shard_map/all_gather | solution.py:140
  40.1 2.9 %collective-permute-start.1 = (bf16[8,40,512]{2,1,0:T(8,128)(2,1)}, bf16[8,40,512]{2,1,0:T(8,128)(2,1)S(1)}, u32[]{:S(2)}, u32[]{:S(2)}) collective-permute-start(bf16[8,40,512]{2,1,0:T(8,128)(2,1)} %get-tuple-element.26), channel_id=1, source_target_pairs={{0,8},{8,16},{16,24},{24,32},{32,40},{40,48},{48,56},{56,64},{64,7... | collective-permute-start | bytes 983048 | tf_op jit(solution)/shard_map/ppermute | solution.py:32
  43.0 4.1 %collective-permute-start = (bf16[8,40,512]{2,1,0:T(8,128)(2,1)S(1)}, bf16[8,40,512]{2,1,0:T(8,128)(2,1)S(1)}, u32[]{:S(2)}, u32[]{:S(2)}) collective-permute-start(bf16[8,40,512]{2,1,0:T(8,128)(2,1)S(1)} %get-tuple-element.27), channel_id=1, source_target_pairs={{0,120},{8,0},{16,8},{24,16},{32,24},{40,32},{48,40},{56,48},{64,5... | collective-permute-start | bytes 983048 | tf_op jit(solution)/shard_map/ppermute | solution.py:32
  47.2 1.8 %copy.8 = bf16[640,640]{0,1:T(8,128)(2,1)S(1)} copy(bf16[640,640]{1,0:T(8,128)(2,1)} %param.6) | data formatting | bytes 1638400 | tf_op args[2]
  49.0 1.5 collective-permute-done.1.x_other_ref
  50.5 1.5 %collective-permute-done.cot_other_ref = bf16[8,40,512]{2,1,0:T(8,128)(2,1)S(1)} collective-permute-done((bf16[8,40,512]{2,1,0:T(8,128)(2,1)S(1)}, bf16[8,40,512]{2,1,0:T(8,128)(2,1)S(1)}, u32[]{:S(2)}, u32[]{:S(2)}) %collective-permute-start) | collective-permute-done | bytes 327712 | tf_op jit(solution)/shard_map/ppermute | solution.py:32
  52.0 1.4 shard_map.75
  53.4 16.6 %all_to_all.15.got_ref = bf16[4,2,128,640]{3,2,1,0:T(8,128)(2,1)S(1)} all-to-all(bf16[4,2,128,640]{3,2,1,0:T(8,128)(2,1)S(1)} %get-tuple-element.15), channel_id=1, replica_groups=mesh['row'=4,'high'=8,'low'=2,'chip'=4,'core'=2] {'row'}, dimensions={0} | all-to-all | bytes 2621440 | tf_op jit(solution)/shard_map/all_to_all | solution.py:156
  70.5 14.7 %all_to_all.16.rows_ref = bf16[4,2,128,640]{3,2,1,0:T(8,128)(2,1)S(1)} all-to-all(bf16[4,2,128,640]{3,2,1,0:T(8,128)(2,1)S(1)} %shard_map.76), channel_id=1, replica_groups=mesh['row'=4,'high'=8,'low'=2,'chip'=4,'core'=2] {'row'}, dimensions={0} | all-to-all | bytes 2621440 | tf_op jit(solution)/shard_map/all_to_all | solution.py:158
  85.2 2.1 %shard_map.77 = bf16[16,2,40,512]{3,2,1,0:T(8,128)(2,1)} custom-call(bf16[640,640]{1,0:T(8,128)(2,1)S(1)} %bitcast.15, bf16[640,640]{1,0:T(8,128)(2,1)S(1)} %copy-done, bf16[4,2,128,640]{3,2,1,0:T(8,128)(2,1)S(1)} %all_to_all.16.rows_ref), custom_call_target="tpu_custom_call" | custom-call | flops 838860800 | bytes 4259840 | tf_op jit(solution)/shard_map/pallas_call | solution.py:53
  87.3 8.5 %all-to-all-start.2 = ((bf16[16,2,40,512]{3,2,1,0:T(8,128)(2,1)}), bf16[16,2,40,512]{3,2,1,0:T(8,128)(2,1)S(1)}, u32[]{:S(2)}, u32[]{:S(2)}) async-start(bf16[16,2,40,512]{3,2,1,0:T(8,128)(2,1)} %shard_map.77), calls=%async_computation.2 | async-start | bytes 2621440 | tf_op jit(solution)/shard_map/all_to_all | solution.py:169
  96.9 1.3 shard_map.79
  98.2 1.9 %collective-permute-start.2 = (bf16[2,320,640]{2,1,0:T(8,128)(2,1)S(1)}, bf16[2,320,640]{2,1,0:T(8,128)(2,1)S(1)}, u32[]{:S(2)}, u32[]{:S(2)}) collective-permute-start(bf16[2,320,640]{2,1,0:T(8,128)(2,1)S(1)} %get-tuple-element.21), channel_id=1, source_target_pairs={{0,1},{1,0},{2,3},{3,2},{4,5},{5,4},{6,7},{7,6},{8,9},{9,8},{10,11... | collective-permute-start | bytes 2457608 | tf_op jit(solution)/shard_map/ppermute | solution.py:181
  100.2 2.3 %collective-permute-done.2 = bf16[2,320,640]{2,1,0:T(8,128)(2,1)S(1)} collective-permute-done((bf16[2,320,640]{2,1,0:T(8,128)(2,1)S(1)}, bf16[2,320,640]{2,1,0:T(8,128)(2,1)S(1)}, u32[]{:S(2)}, u32[]{:S(2)}) %collective-permute-start.2) | collective-permute-done | bytes 819232 | tf_op jit(solution)/shard_map/ppermute | solution.py:181
  102.7 2.1 %collective-permute-start.5 = (bf16[320,640]{1,0:T(8,128)(2,1)S(1)}, bf16[320,640]{1,0:T(8,128)(2,1)S(1)}, u32[]{:S(2)}, u32[]{:S(2)}) collective-permute-start(bf16[320,640]{1,0:T(8,128)(2,1)S(1)} %get-tuple-element.24), channel_id=1, source_target_pairs={{2,4},{4,2},{6,0},{0,6},{3,5},{5,3},{7,1},{1,7},{10,12},{12,10},{1... | collective-permute-start | bytes 1228808 | tf_op jit(solution)/shard_map/ppermute | solution.py:40
  104.8 2.9 %collective-permute-start.3 = (bf16[320,640]{1,0:T(8,128)(2,1)S(1)}, bf16[320,640]{1,0:T(8,128)(2,1)S(1)}, u32[]{:S(2)}, u32[]{:S(2)}) collective-permute-start(bf16[320,640]{1,0:T(8,128)(2,1)S(1)} %get-tuple-element.25), channel_id=1, source_target_pairs={{0,2},{2,0},{4,6},{6,4},{1,3},{3,1},{5,7},{7,5},{8,10},{10,8},{12,... | collective-permute-start | bytes 1228808 | tf_op jit(solution)/shard_map/ppermute | solution.py:40
  107.7 9.6 %collective-permute-done.5 = bf16[320,640]{1,0:T(8,128)(2,1)S(1)} collective-permute-done((bf16[320,640]{1,0:T(8,128)(2,1)S(1)}, bf16[320,640]{1,0:T(8,128)(2,1)S(1)}, u32[]{:S(2)}, u32[]{:S(2)}) %collective-permute-start.5) | collective-permute-done | bytes 409632 | tf_op jit(solution)/shard_map/ppermute | solution.py:40
  117.4 1.9 %collective-permute-start.6 = (bf16[320,640]{1,0:T(8,128)(2,1)S(1)}, bf16[320,640]{1,0:T(8,128)(2,1)S(1)}, u32[]{:S(2)}, u32[]{:S(2)}) collective-permute-start(bf16[320,640]{1,0:T(8,128)(2,1)S(1)} %add_convert_fusion.1), channel_id=1, source_target_pairs={{0,2},{2,0},{4,6},{6,4},{1,3},{3,1},{5,7},{7,5},{8,10},{10,8},{12,... | collective-permute-start | bytes 1228808 | tf_op jit(solution)/shard_map/ppermute | solution.py:42
  119.4 3.5 %collective-permute-start.4 = (bf16[320,640]{1,0:T(8,128)(2,1)S(1)}, bf16[320,640]{1,0:T(8,128)(2,1)S(1)}, u32[]{:S(2)}, u32[]{:S(2)}) collective-permute-start(bf16[320,640]{1,0:T(8,128)(2,1)S(1)} %add_convert_fusion.4), channel_id=1, source_target_pairs={{2,4},{4,2},{6,0},{0,6},{3,5},{5,3},{7,1},{1,7},{10,12},{12,10},{1... | collective-permute-start | bytes 1228808 | tf_op jit(solution)/shard_map/ppermute | solution.py:42
  122.9 7.0 %collective-permute-done.6 = bf16[320,640]{1,0:T(8,128)(2,1)S(1)} collective-permute-done((bf16[320,640]{1,0:T(8,128)(2,1)S(1)}, bf16[320,640]{1,0:T(8,128)(2,1)S(1)}, u32[]{:S(2)}, u32[]{:S(2)}) %collective-permute-start.6) | collective-permute-done | bytes 409632 | tf_op jit(solution)/shard_map/ppermute | solution.py:42
  130.0 1.9 %collective-permute-start.8 = (bf16[320,640]{1,0:T(8,128)(2,1)S(1)}, bf16[320,640]{1,0:T(8,128)(2,1)S(1)}, u32[]{:S(2)}, u32[]{:S(2)}) collective-permute-start(bf16[320,640]{1,0:T(8,128)(2,1)S(1)} %add_convert_fusion.out_mine_ref), channel_id=1, source_target_pairs={{0,1},{1,0},{2,3},{3,2},{4,5},{5,4},{6,7},{7,6},{8,9},{9,8},{10,11... | collective-permute-start | bytes 1228808 | tf_op jit(solution)/shard_map/ppermute | solution.py:184
  133.3 1.9 %collective-permute-start.7 = (bf16[320,640]{1,0:T(8,128)(2,1)S(1)}, bf16[320,640]{1,0:T(8,128)(2,1)S(1)}, u32[]{:S(2)}, u32[]{:S(2)}) collective-permute-start(bf16[320,640]{1,0:T(8,128)(2,1)S(1)} %add_convert_fusion.3.in_mine_ref), channel_id=1, source_target_pairs={{0,1},{1,0},{2,3},{3,2},{4,5},{5,4},{6,7},{7,6},{8,9},{9,8},{10,11... | collective-permute-start | bytes 1228808 | tf_op jit(solution)/shard_map/ppermute | solution.py:183
  135.2 1.7 %collective-permute-done.7.in_other_ref = bf16[320,640]{1,0:T(8,128)(2,1)S(1)} collective-permute-done((bf16[320,640]{1,0:T(8,128)(2,1)S(1)}, bf16[320,640]{1,0:T(8,128)(2,1)S(1)}, u32[]{:S(2)}, u32[]{:S(2)}) %collective-permute-start.7) | collective-permute-done | bytes 409632 | tf_op jit(solution)/shard_map/ppermute | solution.py:183
  138.2 10.9 %all-to-all-done.2.got_ref = bf16[16,2,40,512]{3,2,1,0:T(8,128)(2,1)S(1)} async-done(((bf16[16,2,40,512]{3,2,1,0:T(8,128)(2,1)}), bf16[16,2,40,512]{3,2,1,0:T(8,128)(2,1)S(1)}, u32[]{:S(2)}, u32[]{:S(2)}) %all-to-all-start.2) | async-done | bytes 1310752 | tf_op jit(solution)/shard_map/all_to_all | solution.py:169
  (23 shorter events, 7.0 us)
Async XLA Ops:
  39.3 12.7 %copy-start = (bf16[640,640]{1,0:T(8,128)(2,1)S(1)}, bf16[640,640]{1,0:T(8,128)(2,1)}, u32[]{:S(2)}) copy-start(bf16[640,640]{1,0:T(8,128)(2,1)} %in_w_ref.3) | copy-start | bytes 2457604
  40.1 10.4 %collective-permute-start.1 = (bf16[8,40,512]{2,1,0:T(8,128)(2,1)}, bf16[8,40,512]{2,1,0:T(8,128)(2,1)S(1)}, u32[]{:S(2)}, u32[]{:S(2)}) collective-permute-start(bf16[8,40,512]{2,1,0:T(8,128)(2,1)} %get-tuple-element.26), channel_id=1, source_target_pairs={{0,8},{8,16},{16,24},{24,32},{32,40},{40,48},{48,56},{56,64},{64,7... | collective-permute-start | bytes 983048 | tf_op jit(solution)/shard_map/ppermute | solution.py:32
  43.0 9.0 %collective-permute-start = (bf16[8,40,512]{2,1,0:T(8,128)(2,1)S(1)}, bf16[8,40,512]{2,1,0:T(8,128)(2,1)S(1)}, u32[]{:S(2)}, u32[]{:S(2)}) collective-permute-start(bf16[8,40,512]{2,1,0:T(8,128)(2,1)S(1)} %get-tuple-element.27), channel_id=1, source_target_pairs={{0,120},{8,0},{16,8},{24,16},{32,24},{40,32},{48,40},{56,48},{64,5... | collective-permute-start | bytes 983048 | tf_op jit(solution)/shard_map/ppermute | solution.py:32
  53.4 16.7 %copy-start.1 = (bf16[16,40,512]{2,1,0:T(8,128)(2,1)}, bf16[16,40,512]{2,1,0:T(8,128)(2,1)S(1)}, u32[]{:S(2)}) copy-start(bf16[16,40,512]{2,1,0:T(8,128)(2,1)S(1)} %get-tuple-element.18) | copy-start | bytes 1966084
  53.4 16.6 %copy-start.3 = (bf16[16,40,512]{2,1,0:T(8,128)(2,1)}, bf16[16,40,512]{2,1,0:T(8,128)(2,1)S(1)}, u32[]{:S(2)}) copy-start(bf16[16,40,512]{2,1,0:T(8,128)(2,1)S(1)} %get-tuple-element.19) | copy-start | bytes 1966084
  87.3 8.5 %copy-start.2 = (bf16[16,40,512]{2,1,0:T(8,128)(2,1)S(1)}, bf16[16,40,512]{2,1,0:T(8,128)(2,1)}, u32[]{:S(2)}) copy-start(bf16[16,40,512]{2,1,0:T(8,128)(2,1)} %copy-done.1) | copy-start | bytes 1966084
  87.3 61.9 %all-to-all-start.2 = ((bf16[16,2,40,512]{3,2,1,0:T(8,128)(2,1)}), bf16[16,2,40,512]{3,2,1,0:T(8,128)(2,1)S(1)}, u32[]{:S(2)}, u32[]{:S(2)}) async-start(bf16[16,2,40,512]{3,2,1,0:T(8,128)(2,1)} %shard_map.77), calls=%async_computation.2 | async-start | bytes 2621440 | tf_op jit(solution)/shard_map/all_to_all | solution.py:169
  95.8 1.1 copy-start.4
  98.2 4.2 %collective-permute-start.2 = (bf16[2,320,640]{2,1,0:T(8,128)(2,1)S(1)}, bf16[2,320,640]{2,1,0:T(8,128)(2,1)S(1)}, u32[]{:S(2)}, u32[]{:S(2)}) collective-permute-start(bf16[2,320,640]{2,1,0:T(8,128)(2,1)S(1)} %get-tuple-element.21), channel_id=1, source_target_pairs={{0,1},{1,0},{2,3},{3,2},{4,5},{5,4},{6,7},{7,6},{8,9},{9,8},{10,11... | collective-permute-start | bytes 2457608 | tf_op jit(solution)/shard_map/ppermute | solution.py:181
  102.7 14.6 %collective-permute-start.5 = (bf16[320,640]{1,0:T(8,128)(2,1)S(1)}, bf16[320,640]{1,0:T(8,128)(2,1)S(1)}, u32[]{:S(2)}, u32[]{:S(2)}) collective-permute-start(bf16[320,640]{1,0:T(8,128)(2,1)S(1)} %get-tuple-element.24), channel_id=1, source_target_pairs={{2,4},{4,2},{6,0},{0,6},{3,5},{5,3},{7,1},{1,7},{10,12},{12,10},{1... | collective-permute-start | bytes 1228808 | tf_op jit(solution)/shard_map/ppermute | solution.py:40
  104.8 14.5 %collective-permute-start.3 = (bf16[320,640]{1,0:T(8,128)(2,1)S(1)}, bf16[320,640]{1,0:T(8,128)(2,1)S(1)}, u32[]{:S(2)}, u32[]{:S(2)}) collective-permute-start(bf16[320,640]{1,0:T(8,128)(2,1)S(1)} %get-tuple-element.25), channel_id=1, source_target_pairs={{0,2},{2,0},{4,6},{6,4},{1,3},{3,1},{5,7},{7,5},{8,10},{10,8},{12,... | collective-permute-start | bytes 1228808 | tf_op jit(solution)/shard_map/ppermute | solution.py:40
  117.4 12.6 %collective-permute-start.6 = (bf16[320,640]{1,0:T(8,128)(2,1)S(1)}, bf16[320,640]{1,0:T(8,128)(2,1)S(1)}, u32[]{:S(2)}, u32[]{:S(2)}) collective-permute-start(bf16[320,640]{1,0:T(8,128)(2,1)S(1)} %add_convert_fusion.1), channel_id=1, source_target_pairs={{0,2},{2,0},{4,6},{6,4},{1,3},{3,1},{5,7},{7,5},{8,10},{10,8},{12,... | collective-permute-start | bytes 1228808 | tf_op jit(solution)/shard_map/ppermute | solution.py:42
  119.4 13.8 %collective-permute-start.4 = (bf16[320,640]{1,0:T(8,128)(2,1)S(1)}, bf16[320,640]{1,0:T(8,128)(2,1)S(1)}, u32[]{:S(2)}, u32[]{:S(2)}) collective-permute-start(bf16[320,640]{1,0:T(8,128)(2,1)S(1)} %add_convert_fusion.4), channel_id=1, source_target_pairs={{2,4},{4,2},{6,0},{0,6},{3,5},{5,3},{7,1},{1,7},{10,12},{12,10},{1... | collective-permute-start | bytes 1228808 | tf_op jit(solution)/shard_map/ppermute | solution.py:42
  130.0 5.2 %collective-permute-start.8 = (bf16[320,640]{1,0:T(8,128)(2,1)S(1)}, bf16[320,640]{1,0:T(8,128)(2,1)S(1)}, u32[]{:S(2)}, u32[]{:S(2)}) collective-permute-start(bf16[320,640]{1,0:T(8,128)(2,1)S(1)} %add_convert_fusion.out_mine_ref), channel_id=1, source_target_pairs={{0,1},{1,0},{2,3},{3,2},{4,5},{5,4},{6,7},{7,6},{8,9},{9,8},{10,11... | collective-permute-start | bytes 1228808 | tf_op jit(solution)/shard_map/ppermute | solution.py:184
  133.3 3.6 %collective-permute-start.7 = (bf16[320,640]{1,0:T(8,128)(2,1)S(1)}, bf16[320,640]{1,0:T(8,128)(2,1)S(1)}, u32[]{:S(2)}, u32[]{:S(2)}) collective-permute-start(bf16[320,640]{1,0:T(8,128)(2,1)S(1)} %add_convert_fusion.3.in_mine_ref), channel_id=1, source_target_pairs={{0,1},{1,0},{2,3},{3,2},{4,5},{5,4},{6,7},{7,6},{8,9},{9,8},{10,11... | collective-permute-start | bytes 1228808 | tf_op jit(solution)/shard_map/ppermute | solution.py:183

commit v8 on v7

--- a/solution.py
+++ b/solution.py
@@ -94,12 +94,12 @@
 
 def out_kernel(out_w_ref, in_w_ref, rows_ref, terms_ref, *parts):
     copies = []
-    for number, (part_ref, sem) in enumerate(zip(parts[:4], parts[4:])):
-        stream, half = divmod(number, 2)
-        weight = (out_w_ref, in_w_ref)[stream][half * 320 : (half + 1) * 320]
+    for number, (part_ref, sem) in enumerate(zip(parts[:8], parts[8:])):
+        stream, part = divmod(number, 4)
+        weight = (out_w_ref, in_w_ref)[stream][part * 160 : (part + 1) * 160]
         terms = contract(weight, rows_ref[:, stream].reshape(512, 640), 1, 1)
-        part_ref[...] = terms.astype(bf16).reshape(8, 40, 512)
-        place = terms_ref.at[half * 8 : (half + 1) * 8, stream]
+        part_ref[...] = terms.astype(bf16).reshape(4, 40, 512)
+        place = terms_ref.at[part * 4 : (part + 1) * 4, stream]
         copies.append(pltpu.make_async_copy(part_ref, place, sem))
         copies[-1].start()
     for copy in copies:
@@ -163,8 +163,8 @@
         out_w,
         w_in,
         rows,
-        scratch=[(8, 40, 512)] * 4,
-        copies=4,
+        scratch=[(4, 40, 512)] * 8,
+        copies=8,
     )
     out_got = lax.all_to_all(out_terms, COL, 0, 0, tiled=True)
     y_t, x_grad_t = kernel_call(sum_kernel, [(40, 512)] * 2, 2 * 16 * 40 * 512, out_got)

time: 151 us -> 151 us (level)
  no operation moved by 1% of the time
where the time goes in v8:
time: 151 us
  blocking collectives  69.2 us (46%)
  waiting for transfers between devices  35.8 us (24%)
  starting transfers between devices  31.7 us (21%)
  Pallas kernels  7.95 us (5%)
  local copies, waits for them, and re-layouts  3.71 us (2%)
    all_gather x1, blocking collectives, per_device(): far = lax.all_gather(both, 'high', axis=0)  37.9 us
    all_to_all x1, blocking collectives, per_device(): got = lax.all_to_all(terms, 'row', 0, 0, tiled=True)  16.6 us
    all_to_all x1, blocking collectives, per_device(): rows = lax.all_to_all(copies, 'row', 0, 0, tiled=True)  14.7 us
    all_to_all x1, waiting for transfers between devices, per_device(): out_got = lax.all_to_all(out_terms, COL, 0, 0, tiled=True)  10.9 us
    ppermute x1, waiting for transfers between devices, chip_sum(): lax.ppermute(out_half, 'chip', ODD)  9.59 us
    all_to_all x1, starting transfers between devices, per_device(): out_got = lax.all_to_all(out_terms, COL, 0, 0, tiled=True)  8.49 us
    pallas_call x6, Pallas kernels, kernel_call(): pl.pallas_call(body, out_shape=shapes, in_specs=[smem if a.dtype == jnp.i...  7.95 us
    ppermute x2, starting transfers between devices, permute(): lax.ppermute(block, axis, [(i, (i + step) % count) for i in range(count)])  7.04 us
  transfers between devices with their start and end apart: 10, of which 8 were waited for; matrix products, arithmetic and copies ran while one was open for 2% of the time, Pallas kernels for 2%

profile of v8, /device:TPU:24, one launch (start us, length us, event | category | flops | bytes accessed | tf_op | source)
XLA Modules:
  0.0 150.6 jit_solution(9210069541732452686)
XLA Ops:
  1.4 37.9 %all-gather = bf16[640,512]{1,0:T(8,128)(2,1)S(1)} all-gather(bf16[80,512]{1,0:T(8,128)(2,1)S(1)} %pad_maximum_fusion), channel_id=2, replica_groups=mesh['row'=4,'high'=8,'low'=2,'chip'=4,'core'=2] {'high'}, dimensions={0}, use_global_device_ids=true | all-gather | bytes 737280 | tf_op jit(solution)/shard_map/all_gather | solution.py:140
  40.1 2.9 %collective-permute-start.1 = (bf16[8,40,512]{2,1,0:T(8,128)(2,1)}, bf16[8,40,512]{2,1,0:T(8,128)(2,1)S(1)}, u32[]{:S(2)}, u32[]{:S(2)}) collective-permute-start(bf16[8,40,512]{2,1,0:T(8,128)(2,1)} %get-tuple-element.26), channel_id=1, source_target_pairs={{0,8},{8,16},{16,24},{24,32},{32,40},{40,48},{48,56},{56,64},{64,7... | collective-permute-start | bytes 983048 | tf_op jit(solution)/shard_map/ppermute | solution.py:32
  43.0 4.1 %collective-permute-start = (bf16[8,40,512]{2,1,0:T(8,128)(2,1)S(1)}, bf16[8,40,512]{2,1,0:T(8,128)(2,1)S(1)}, u32[]{:S(2)}, u32[]{:S(2)}) collective-permute-start(bf16[8,40,512]{2,1,0:T(8,128)(2,1)S(1)} %get-tuple-element.27), channel_id=1, source_target_pairs={{0,120},{8,0},{16,8},{24,16},{32,24},{40,32},{48,40},{56,48},{64,5... | collective-permute-start | bytes 983048 | tf_op jit(solution)/shard_map/ppermute | solution.py:32
  47.2 1.8 %copy.8 = bf16[640,640]{0,1:T(8,128)(2,1)S(1)} copy(bf16[640,640]{1,0:T(8,128)(2,1)} %param.6) | data formatting | bytes 1638400 | tf_op args[2]
  49.0 1.5 collective-permute-done.1.x_other_ref
  50.5 1.5 %collective-permute-done.cot_other_ref = bf16[8,40,512]{2,1,0:T(8,128)(2,1)S(1)} collective-permute-done((bf16[8,40,512]{2,1,0:T(8,128)(2,1)S(1)}, bf16[8,40,512]{2,1,0:T(8,128)(2,1)S(1)}, u32[]{:S(2)}, u32[]{:S(2)}) %collective-permute-start) | collective-permute-done | bytes 327712 | tf_op jit(solution)/shard_map/ppermute | solution.py:32
  52.0 1.4 shard_map.75
  53.4 16.6 %all_to_all.15.got_ref = bf16[4,2,128,640]{3,2,1,0:T(8,128)(2,1)S(1)} all-to-all(bf16[4,2,128,640]{3,2,1,0:T(8,128)(2,1)S(1)} %get-tuple-element.15), channel_id=1, replica_groups=mesh['row'=4,'high'=8,'low'=2,'chip'=4,'core'=2] {'row'}, dimensions={0} | all-to-all | bytes 2621440 | tf_op jit(solution)/shard_map/all_to_all | solution.py:156
  70.5 14.7 %all_to_all.16.rows_ref = bf16[4,2,128,640]{3,2,1,0:T(8,128)(2,1)S(1)} all-to-all(bf16[4,2,128,640]{3,2,1,0:T(8,128)(2,1)S(1)} %shard_map.76), channel_id=1, replica_groups=mesh['row'=4,'high'=8,'low'=2,'chip'=4,'core'=2] {'row'}, dimensions={0} | all-to-all | bytes 2621440 | tf_op jit(solution)/shard_map/all_to_all | solution.py:158
  85.2 2.8 %shard_map.77 = bf16[16,2,40,512]{3,2,1,0:T(8,128)(2,1)} custom-call(bf16[640,640]{1,0:T(8,128)(2,1)S(1)} %bitcast.15, bf16[640,640]{1,0:T(8,128)(2,1)S(1)} %copy-done, bf16[4,2,128,640]{3,2,1,0:T(8,128)(2,1)S(1)} %all_to_all.16.rows_ref), custom_call_target="tpu_custom_call" | custom-call | flops 838860800 | bytes 4259840 | tf_op jit(solution)/shard_map/pallas_call | solution.py:53
  88.0 8.5 %all-to-all-start.2 = ((bf16[16,2,40,512]{3,2,1,0:T(8,128)(2,1)}), bf16[16,2,40,512]{3,2,1,0:T(8,128)(2,1)S(1)}, u32[]{:S(2)}, u32[]{:S(2)}) async-start(bf16[16,2,40,512]{3,2,1,0:T(8,128)(2,1)} %shard_map.77), calls=%async_computation.2 | async-start | bytes 2621440 | tf_op jit(solution)/shard_map/all_to_all | solution.py:169
  97.6 1.3 shard_map.79
  98.9 1.9 %collective-permute-start.2 = (bf16[2,320,640]{2,1,0:T(8,128)(2,1)S(1)}, bf16[2,320,640]{2,1,0:T(8,128)(2,1)S(1)}, u32[]{:S(2)}, u32[]{:S(2)}) collective-permute-start(bf16[2,320,640]{2,1,0:T(8,128)(2,1)S(1)} %get-tuple-element.21), channel_id=1, source_target_pairs={{0,1},{1,0},{2,3},{3,2},{4,5},{5,4},{6,7},{7,6},{8,9},{9,8},{10,11... | collective-permute-start | bytes 2457608 | tf_op jit(solution)/shard_map/ppermute | solution.py:181
  100.8 2.3 %collective-permute-done.2 = bf16[2,320,640]{2,1,0:T(8,128)(2,1)S(1)} collective-permute-done((bf16[2,320,640]{2,1,0:T(8,128)(2,1)S(1)}, bf16[2,320,640]{2,1,0:T(8,128)(2,1)S(1)}, u32[]{:S(2)}, u32[]{:S(2)}) %collective-permute-start.2) | collective-permute-done | bytes 819232 | tf_op jit(solution)/shard_map/ppermute | solution.py:181
  103.3 2.1 %collective-permute-start.5 = (bf16[320,640]{1,0:T(8,128)(2,1)S(1)}, bf16[320,640]{1,0:T(8,128)(2,1)S(1)}, u32[]{:S(2)}, u32[]{:S(2)}) collective-permute-start(bf16[320,640]{1,0:T(8,128)(2,1)S(1)} %get-tuple-element.24), channel_id=1, source_target_pairs={{2,4},{4,2},{6,0},{0,6},{3,5},{5,3},{7,1},{1,7},{10,12},{12,10},{1... | collective-permute-start | bytes 1228808 | tf_op jit(solution)/shard_map/ppermute | solution.py:40
  105.5 2.9 %collective-permute-start.3 = (bf16[320,640]{1,0:T(8,128)(2,1)S(1)}, bf16[320,640]{1,0:T(8,128)(2,1)S(1)}, u32[]{:S(2)}, u32[]{:S(2)}) collective-permute-start(bf16[320,640]{1,0:T(8,128)(2,1)S(1)} %get-tuple-element.25), channel_id=1, source_target_pairs={{0,2},{2,0},{4,6},{6,4},{1,3},{3,1},{5,7},{7,5},{8,10},{10,8},{12,... | collective-permute-start | bytes 1228808 | tf_op jit(solution)/shard_map/ppermute | solution.py:40
  108.4 9.6 %collective-permute-done.5 = bf16[320,640]{1,0:T(8,128)(2,1)S(1)} collective-permute-done((bf16[320,640]{1,0:T(8,128)(2,1)S(1)}, bf16[320,640]{1,0:T(8,128)(2,1)S(1)}, u32[]{:S(2)}, u32[]{:S(2)}) %collective-permute-start.5) | collective-permute-done | bytes 409632 | tf_op jit(solution)/shard_map/ppermute | solution.py:40
  118.1 1.9 %collective-permute-start.6 = (bf16[320,640]{1,0:T(8,128)(2,1)S(1)}, bf16[320,640]{1,0:T(8,128)(2,1)S(1)}, u32[]{:S(2)}, u32[]{:S(2)}) collective-permute-start(bf16[320,640]{1,0:T(8,128)(2,1)S(1)} %add_convert_fusion.1), channel_id=1, source_target_pairs={{0,2},{2,0},{4,6},{6,4},{1,3},{3,1},{5,7},{7,5},{8,10},{10,8},{12,... | collective-permute-start | bytes 1228808 | tf_op jit(solution)/shard_map/ppermute | solution.py:42
  120.1 3.5 %collective-permute-start.4 = (bf16[320,640]{1,0:T(8,128)(2,1)S(1)}, bf16[320,640]{1,0:T(8,128)(2,1)S(1)}, u32[]{:S(2)}, u32[]{:S(2)}) collective-permute-start(bf16[320,640]{1,0:T(8,128)(2,1)S(1)} %add_convert_fusion.4), channel_id=1, source_target_pairs={{2,4},{4,2},{6,0},{0,6},{3,5},{5,3},{7,1},{1,7},{10,12},{12,10},{1... | collective-permute-start | bytes 1228808 | tf_op jit(solution)/shard_map/ppermute | solution.py:42
  123.6 7.0 %collective-permute-done.6 = bf16[320,640]{1,0:T(8,128)(2,1)S(1)} collective-permute-done((bf16[320,640]{1,0:T(8,128)(2,1)S(1)}, bf16[320,640]{1,0:T(8,128)(2,1)S(1)}, u32[]{:S(2)}, u32[]{:S(2)}) %collective-permute-start.6) | collective-permute-done | bytes 409632 | tf_op jit(solution)/shard_map/ppermute | solution.py:42
  130.7 1.9 %collective-permute-start.8 = (bf16[320,640]{1,0:T(8,128)(2,1)S(1)}, bf16[320,640]{1,0:T(8,128)(2,1)S(1)}, u32[]{:S(2)}, u32[]{:S(2)}) collective-permute-start(bf16[320,640]{1,0:T(8,128)(2,1)S(1)} %add_convert_fusion.out_mine_ref), channel_id=1, source_target_pairs={{0,1},{1,0},{2,3},{3,2},{4,5},{5,4},{6,7},{7,6},{8,9},{9,8},{10,11... | collective-permute-start | bytes 1228808 | tf_op jit(solution)/shard_map/ppermute | solution.py:184
  134.0 1.9 %collective-permute-start.7 = (bf16[320,640]{1,0:T(8,128)(2,1)S(1)}, bf16[320,640]{1,0:T(8,128)(2,1)S(1)}, u32[]{:S(2)}, u32[]{:S(2)}) collective-permute-start(bf16[320,640]{1,0:T(8,128)(2,1)S(1)} %add_convert_fusion.3.in_mine_ref), channel_id=1, source_target_pairs={{0,1},{1,0},{2,3},{3,2},{4,5},{5,4},{6,7},{7,6},{8,9},{9,8},{10,11... | collective-permute-start | bytes 1228808 | tf_op jit(solution)/shard_map/ppermute | solution.py:183
  135.9 1.7 %collective-permute-done.7.in_other_ref = bf16[320,640]{1,0:T(8,128)(2,1)S(1)} collective-permute-done((bf16[320,640]{1,0:T(8,128)(2,1)S(1)}, bf16[320,640]{1,0:T(8,128)(2,1)S(1)}, u32[]{:S(2)}, u32[]{:S(2)}) %collective-permute-start.7) | collective-permute-done | bytes 409632 | tf_op jit(solution)/shard_map/ppermute | solution.py:183
  138.9 10.9 %all-to-all-done.2.got_ref = bf16[16,2,40,512]{3,2,1,0:T(8,128)(2,1)S(1)} async-done(((bf16[16,2,40,512]{3,2,1,0:T(8,128)(2,1)}), bf16[16,2,40,512]{3,2,1,0:T(8,128)(2,1)S(1)}, u32[]{:S(2)}, u32[]{:S(2)}) %all-to-all-start.2) | async-done | bytes 1310752 | tf_op jit(solution)/shard_map/all_to_all | solution.py:169
  (23 shorter events, 7.0 us)
Async XLA Ops:
  39.3 12.7 %copy-start = (bf16[640,640]{1,0:T(8,128)(2,1)S(1)}, bf16[640,640]{1,0:T(8,128)(2,1)}, u32[]{:S(2)}) copy-start(bf16[640,640]{1,0:T(8,128)(2,1)} %in_w_ref.3) | copy-start | bytes 2457604
  40.1 10.4 %collective-permute-start.1 = (bf16[8,40,512]{2,1,0:T(8,128)(2,1)}, bf16[8,40,512]{2,1,0:T(8,128)(2,1)S(1)}, u32[]{:S(2)}, u32[]{:S(2)}) collective-permute-start(bf16[8,40,512]{2,1,0:T(8,128)(2,1)} %get-tuple-element.26), channel_id=1, source_target_pairs={{0,8},{8,16},{16,24},{24,32},{32,40},{40,48},{48,56},{56,64},{64,7... | collective-permute-start | bytes 983048 | tf_op jit(solution)/shard_map/ppermute | solution.py:32
  43.0 9.0 %collective-permute-start = (bf16[8,40,512]{2,1,0:T(8,128)(2,1)S(1)}, bf16[8,40,512]{2,1,0:T(8,128)(2,1)S(1)}, u32[]{:S(2)}, u32[]{:S(2)}) collective-permute-start(bf16[8,40,512]{2,1,0:T(8,128)(2,1)S(1)} %get-tuple-element.27), channel_id=1, source_target_pairs={{0,120},{8,0},{16,8},{24,16},{32,24},{40,32},{48,40},{56,48},{64,5... | collective-permute-start | bytes 983048 | tf_op jit(solution)/shard_map/ppermute | solution.py:32
  53.4 16.7 %copy-start.1 = (bf16[16,40,512]{2,1,0:T(8,128)(2,1)}, bf16[16,40,512]{2,1,0:T(8,128)(2,1)S(1)}, u32[]{:S(2)}) copy-start(bf16[16,40,512]{2,1,0:T(8,128)(2,1)S(1)} %get-tuple-element.18) | copy-start | bytes 1966084
  53.4 16.6 %copy-start.3 = (bf16[16,40,512]{2,1,0:T(8,128)(2,1)}, bf16[16,40,512]{2,1,0:T(8,128)(2,1)S(1)}, u32[]{:S(2)}) copy-start(bf16[16,40,512]{2,1,0:T(8,128)(2,1)S(1)} %get-tuple-element.19) | copy-start | bytes 1966084
  88.0 8.5 %copy-start.2 = (bf16[16,40,512]{2,1,0:T(8,128)(2,1)S(1)}, bf16[16,40,512]{2,1,0:T(8,128)(2,1)}, u32[]{:S(2)}) copy-start(bf16[16,40,512]{2,1,0:T(8,128)(2,1)} %copy-done.1) | copy-start | bytes 1966084
  88.0 61.9 %all-to-all-start.2 = ((bf16[16,2,40,512]{3,2,1,0:T(8,128)(2,1)}), bf16[16,2,40,512]{3,2,1,0:T(8,128)(2,1)S(1)}, u32[]{:S(2)}, u32[]{:S(2)}) async-start(bf16[16,2,40,512]{3,2,1,0:T(8,128)(2,1)} %shard_map.77), calls=%async_computation.2 | async-start | bytes 2621440 | tf_op jit(solution)/shard_map/all_to_all | solution.py:169
  96.5 1.1 copy-start.4
  98.9 4.2 %collective-permute-start.2 = (bf16[2,320,640]{2,1,0:T(8,128)(2,1)S(1)}, bf16[2,320,640]{2,1,0:T(8,128)(2,1)S(1)}, u32[]{:S(2)}, u32[]{:S(2)}) collective-permute-start(bf16[2,320,640]{2,1,0:T(8,128)(2,1)S(1)} %get-tuple-element.21), channel_id=1, source_target_pairs={{0,1},{1,0},{2,3},{3,2},{4,5},{5,4},{6,7},{7,6},{8,9},{9,8},{10,11... | collective-permute-start | bytes 2457608 | tf_op jit(solution)/shard_map/ppermute | solution.py:181
  103.3 14.6 %collective-permute-start.5 = (bf16[320,640]{1,0:T(8,128)(2,1)S(1)}, bf16[320,640]{1,0:T(8,128)(2,1)S(1)}, u32[]{:S(2)}, u32[]{:S(2)}) collective-permute-start(bf16[320,640]{1,0:T(8,128)(2,1)S(1)} %get-tuple-element.24), channel_id=1, source_target_pairs={{2,4},{4,2},{6,0},{0,6},{3,5},{5,3},{7,1},{1,7},{10,12},{12,10},{1... | collective-permute-start | bytes 1228808 | tf_op jit(solution)/shard_map/ppermute | solution.py:40
  105.5 14.5 %collective-permute-start.3 = (bf16[320,640]{1,0:T(8,128)(2,1)S(1)}, bf16[320,640]{1,0:T(8,128)(2,1)S(1)}, u32[]{:S(2)}, u32[]{:S(2)}) collective-permute-start(bf16[320,640]{1,0:T(8,128)(2,1)S(1)} %get-tuple-element.25), channel_id=1, source_target_pairs={{0,2},{2,0},{4,6},{6,4},{1,3},{3,1},{5,7},{7,5},{8,10},{10,8},{12,... | collective-permute-start | bytes 1228808 | tf_op jit(solution)/shard_map/ppermute | solution.py:40
  118.1 12.6 %collective-permute-start.6 = (bf16[320,640]{1,0:T(8,128)(2,1)S(1)}, bf16[320,640]{1,0:T(8,128)(2,1)S(1)}, u32[]{:S(2)}, u32[]{:S(2)}) collective-permute-start(bf16[320,640]{1,0:T(8,128)(2,1)S(1)} %add_convert_fusion.1), channel_id=1, source_target_pairs={{0,2},{2,0},{4,6},{6,4},{1,3},{3,1},{5,7},{7,5},{8,10},{10,8},{12,... | collective-permute-start | bytes 1228808 | tf_op jit(solution)/shard_map/ppermute | solution.py:42
  120.1 13.8 %collective-permute-start.4 = (bf16[320,640]{1,0:T(8,128)(2,1)S(1)}, bf16[320,640]{1,0:T(8,128)(2,1)S(1)}, u32[]{:S(2)}, u32[]{:S(2)}) collective-permute-start(bf16[320,640]{1,0:T(8,128)(2,1)S(1)} %add_convert_fusion.4), channel_id=1, source_target_pairs={{2,4},{4,2},{6,0},{0,6},{3,5},{5,3},{7,1},{1,7},{10,12},{12,10},{1... | collective-permute-start | bytes 1228808 | tf_op jit(solution)/shard_map/ppermute | solution.py:42
  130.7 5.2 %collective-permute-start.8 = (bf16[320,640]{1,0:T(8,128)(2,1)S(1)}, bf16[320,640]{1,0:T(8,128)(2,1)S(1)}, u32[]{:S(2)}, u32[]{:S(2)}) collective-permute-start(bf16[320,640]{1,0:T(8,128)(2,1)S(1)} %add_convert_fusion.out_mine_ref), channel_id=1, source_target_pairs={{0,1},{1,0},{2,3},{3,2},{4,5},{5,4},{6,7},{7,6},{8,9},{9,8},{10,11... | collective-permute-start | bytes 1228808 | tf_op jit(solution)/shard_map/ppermute | solution.py:184
  134.0 3.6 %collective-permute-start.7 = (bf16[320,640]{1,0:T(8,128)(2,1)S(1)}, bf16[320,640]{1,0:T(8,128)(2,1)S(1)}, u32[]{:S(2)}, u32[]{:S(2)}) collective-permute-start(bf16[320,640]{1,0:T(8,128)(2,1)S(1)} %add_convert_fusion.3.in_mine_ref), channel_id=1, source_target_pairs={{0,1},{1,0},{2,3},{3,2},{4,5},{5,4},{6,7},{7,6},{8,9},{9,8},{10,11... | collective-permute-start | bytes 1228808 | tf_op jit(solution)/shard_map/ppermute | solution.py:183
